TPU v7x, 256 devices: a whole 4x4x8 slice. The times are simulated.
256 devices in a mesh: dp: 16 (over z_hi, y, core), fsdp: 16 (over x, z_lo).
Axes of the slice: x: 4, y: 4, z: 8 (z_hi: 2, z_lo: 4; z = z_hi * 4 + z_lo), core: 2. Of those that a mesh axis runs over, the one named last changes fastest.
Arguments:
- gradient: bfloat16 [16, 16, 896, 4096], P('dp', None, 'fsdp'), may hold values from -6 to 6
- projector: bfloat16 [4096, 1024], P('fsdp'), may hold values from -0.09375 to 0.09375
- first_moment: float32 [16, 896, 1024], P('dp', 'fsdp'), may hold values from -4 to 4
- second_moment: float32 [16, 896, 1024], P('dp', 'fsdp'), may hold values from 0.002 to 0.05
Outputs:
- update: bfloat16 [16, 896, 4096], P('dp', None, 'fsdp')
- new_first: float32 [16, 896, 1024], P('dp', 'fsdp')
- new_second: float32 [16, 896, 1024], P('dp', 'fsdp')
All inputs are finite; a program needn't handle non-finite values.
Results may differ from a plain program's by a relative error of at most 0.0048.
Values may be sent and summed in bfloat16 or wider, within the bound.
No kernel may reach another device: no remote copies, remote signals or barrier semaphores. Data moves between devices by JAX's collectives and lax.ppermute only.
A program may use at most 64 MiB of HBM per device.

v0:
```python
import jax
import jax.numpy as jnp
from jax import lax
from jax.sharding import PartitionSpec as P

beta_one = 0.9
beta_two = 0.999
bias_one = 1.0 - 0.9**10
bias_two = 1.0 - 0.999**10
epsilon = 1e-08


def against_basis(left, basis_rows):
    return lax.dot_general(
        left, basis_rows, (((1,), (1,)), ((), ())), preferred_element_type=jnp.float32
    )


def per_device(gradient, projector, first_moment, second_moment):
    blocks = gradient.shape[1]
    owned = gradient.shape[2]
    width = gradient.shape[3]
    rank_cols = projector.shape[1]
    local_grad = gradient.reshape(blocks * owned, width)
    full_basis = lax.all_gather(projector, "fsdp", axis=0, tiled=True)
    partial_value = jnp.dot(local_grad, full_basis, preferred_element_type=jnp.float32)
    partial_value = partial_value.reshape(blocks, owned, rank_cols)
    projected = lax.psum_scatter(partial_value, "dp", scatter_dimension=0, tiled=True)
    new_first = beta_one * first_moment + (1.0 - beta_one) * projected
    new_second = beta_two * second_moment + (1.0 - beta_two) * projected * projected
    direction = new_first / bias_one / (jnp.sqrt(new_second / bias_two) + epsilon)
    direction = direction.astype(jnp.bfloat16).reshape(owned, rank_cols)
    owner_rows = against_basis(direction, full_basis).astype(jnp.bfloat16)
    update = lax.all_to_all(owner_rows, "fsdp", split_axis=1, concat_axis=0, tiled=True)
    update = update.reshape(1, update.shape[0], update.shape[1])
    return (update, new_first, new_second)


def solution(mesh):
    in_specs = (
        P("dp", None, "fsdp", None),
        P("fsdp", None),
        P("dp", "fsdp", None),
        P("dp", "fsdp", None),
    )
    out_specs = (P("dp", None, "fsdp"), P("dp", "fsdp", None), P("dp", "fsdp", None))
    return jax.shard_map(
        per_device, mesh=mesh, in_specs=in_specs, out_specs=out_specs, check_vma=False
    )
```

profile of v0, /device:TPU:1, one launch (start us, length us, event | category | flops | bytes accessed | tf_op | source)
XLA Modules:
  0.0 344.6 jit_solution(8871862614467268101)
XLA Ops:
  7.2 0.0 all-gather.2.cloned.1.call-start
  7.2 0.7 all-gather.2.cloned.1.call-update
  7.9 0.0 copy-start.2
  7.9 0.0 copy-start.3
  7.9 0.0 reduce-scatter.2.cloned.1.call-start
  8.0 193.2 %all-gather.2.cloned.1.call-done = bf16[4096,1024]{1,0:T(8,128)(2,1)} async-done(((bf16[256,1024]{1,0:T(8,128)(2,1)}), bf16[4096,1024]{1,0:T(8,128)(2,1)}) %all-gather.2.cloned.1.call-update) | async-done | bytes 8388624 | tf_op jit(solution)/shard_map/all_gather | solution.py:25
  201.2 13.7 %fusion = f32[16,56,1024]{2,1,0:T(8,128)} fusion(bf16[4096,1024]{1,0:T(8,128)(2,1)} %all-gather.2.cloned.1.call-done, bf16[1,16,56,4096]{3,2,1,0:T(8,128)(2,1)} %param.4), kind=kOutput, calls=%fused_computation | convolution fusion | flops 7516192768 | bytes 19398656 | tf_op jit(solution)/shard_map/dot_general | solution.py:26
  214.9 0.0 reduce-scatter.2.cloned.1.call-update
  214.9 96.4 %reduce-scatter.2.cloned.1.call-done = f32[1,56,1024]{2,1,0:T(8,128)} async-done(((f32[16,56,1024]{2,1,0:T(8,128)}), f32[1,56,1024]{2,1,0:T(8,128)}) %reduce-scatter.2.cloned.1.call-update) | async-done | bytes 229392 | tf_op jit(solution)/shard_map/reduce_scatter | solution.py:28
  311.3 0.0 copy-done.2
  311.3 0.0 copy-done.3
  311.3 1.0 multiply_add_fusion
  312.3 0.0 copy-start
  312.3 0.0 copy-start.1
  312.3 6.2 %convolution_convert_fusion = bf16[56,4096]{1,0:T(8,128)(2,1)S(1)} fusion(bf16[4096,1024]{1,0:T(8,128)(2,1)} %all-gather.2.cloned.1.call-done, f32[1,56,1024]{2,1,0:T(8,128)S(1)} %get-tuple-element.10, f32[1,56,1024]{2,1,0:T(8,128)S(1)} %get-tuple-element.9), kind=kOutput, calls=%fused_computation.3 | convolution fusion | flops 470278144 | bytes 9306112 | tf_op jit(solution)/shard_map/dot_general | solution.py:14
  318.6 18.3 %all_to_all.16 = bf16[56,16,256]{2,0,1:T(8,128)(2,1)S(1)} all-to-all(bf16[56,16,256]{2,0,1:T(8,128)(2,1)S(1)} %bitcast.17), channel_id=1, replica_groups=mesh['dp'=16,'fsdp'=16] {'fsdp'}, dimensions={1} | all-to-all | bytes 917504 | tf_op jit(solution)/shard_map/all_to_all | solution.py:34
  336.9 0.8 copy.13
  337.7 0.0 copy-done
  337.7 0.0 copy-done.1
  (1 shorter events, 0.0 us)
Async XLA Ops:
  7.2 194.0 %all-gather.2.cloned.1.call-start = ((), (), s32[]{:S(2)}) async-start(), calls=%async_computation.2 | async-start | bytes 8912896 | tf_op jit(solution)/shard_map/all_gather | solution.py:25
  7.9 303.4 %copy-start.2 = (f32[1,56,1024]{2,1,0:T(8,128)S(1)}, f32[1,56,1024]{2,1,0:T(8,128)}, u32[]{:S(2)}) copy-start(f32[1,56,1024]{2,1,0:T(8,128)} %param.6) | copy-start | bytes 688132
  7.9 303.4 %copy-start.3 = (f32[1,56,1024]{2,1,0:T(8,128)S(1)}, f32[1,56,1024]{2,1,0:T(8,128)}, u32[]{:S(2)}) copy-start(f32[1,56,1024]{2,1,0:T(8,128)} %param.7) | copy-start | bytes 688132
  7.9 303.4 %reduce-scatter.2.cloned.1.call-start = ((), (), s32[]{:S(2)}) async-start(), calls=%async_computation.3 | async-start | bytes 3899392 | tf_op jit(solution)/shard_map/reduce_scatter | solution.py:28
  312.3 25.4 %copy-start = (f32[1,56,1024]{2,1,0:T(8,128)}, f32[1,56,1024]{2,1,0:T(8,128)S(1)}, u32[]{:S(2)}) copy-start(f32[1,56,1024]{2,1,0:T(8,128)S(1)} %get-tuple-element.9) | copy-start | bytes 688132
  312.3 25.4 %copy-start.1 = (f32[1,56,1024]{2,1,0:T(8,128)}, f32[1,56,1024]{2,1,0:T(8,128)S(1)}, u32[]{:S(2)}) copy-start(f32[1,56,1024]{2,1,0:T(8,128)S(1)} %get-tuple-element.10) | copy-start | bytes 688132
Sparse Core Ops, SparseCore 0:
  9.8 191.3 all-gather.1
  215.0 96.2 reduce-scatter.1
where the time goes:
time: 345 us
  waiting for transfers between devices  290 us (84%)
  matrix products  20 us (6%)
  blocking collectives  18.3 us (5%)
  between operations  14.1 us (4%)
    all_gather x1, waiting for transfers between devices, per_device(): full_basis = lax.all_gather(projector, 'fsdp', axis=0, tiled=True)  193 us
    reduce_scatter x1, waiting for transfers between devices, per_device(): lax.psum_scatter(partial_value, 'dp', scatter_dimension=0, tiled=True)  96.4 us
    all_to_all x1, blocking collectives, per_device(): lax.all_to_all(owner_rows, 'fsdp', split_axis=1, concat_axis=0, tiled=True)  18.3 us
    dot_general x1, matrix products, per_device(): jnp.dot(local_grad, full_basis, preferred_element_type=jnp.float32)  13.7 us
  transfers between devices with their start and end apart: 2, of which 2 were waited for; matrix products, arithmetic and copies ran while one was open for 0% of the time, Pallas kernels for 0%

commit v1 on v0

v1 whole, which is shorter than its diff:
```python
import functools

import jax
import jax.numpy as jnp
from jax import lax
from jax.experimental import pallas as pl
from jax.experimental.pallas import tpu as pltpu
from jax.sharding import PartitionSpec as P

beta_one = 0.9
beta_two = 0.999
bias_one = 1.0 - 0.9**10
bias_two = 1.0 - 0.999**10
epsilon = 1e-08

ZH, Y, C, X, ZL = 2, 4, 2, 4, 4
AXES = ("dp", "fsdp")
OFFSETS = (0, 1, -1, 2)
GROUPS = 1


def linear(zh, y, c, x, zl):
    return (((zh * Y + y) * C + c) * X + x) * ZL + zl


def move(value, place):
    pairs = []
    for zh in range(ZH):
        for y in range(Y):
            for c in range(C):
                for x in range(X):
                    for zl in range(ZL):
                        target = place(zh, y, c, x, zl)
                        pairs.append((linear(zh, y, c, x, zl), linear(*target)))
    return lax.ppermute(value, AXES, pairs)


def along_x(step):
    return lambda zh, y, c, x, zl: (zh, y, c, (x + step) % X, zl)


def along_y(step):
    return lambda zh, y, c, x, zl: (zh, (y + step) % Y, c, x, zl)


def along_ring(step):
    def place(zh, y, c, x, zl):
        z = (zh * ZL + zl + step) % (ZH * ZL)
        return (z // ZL, y, c, x, z % ZL)

    return place


def along_line(step):
    return lambda zh, y, c, x, zl: (zh, y, c, x, (zl + step) % ZL)


def other_core(zh, y, c, x, zl):
    return (zh, y, 1 - c, x, zl)


def other_half(zh, y, c, x, zl):
    return (1 - zh, y, c, x, zl)


def by_core(first, second):
    def place(zh, y, c, x, zl):
        return (first if c == 0 else second)(zh, y, c, x, zl)

    return place


def project_kernel(pieces, last, has_acc, order, *refs):
    lefts = refs[: 2 * pieces]
    rights = refs[2 * pieces : 3 * pieces]
    rest = refs[3 * pieces :]
    if has_acc:
        acc_in, rest = rest[0], rest[1:]
    outs, total = rest[:-1], rest[-1]
    step = pl.program_id(0)
    steps = pl.num_programs(0)
    rows = total.shape[0]
    chunk = rows // 4
    for part in range(4):
        at = pl.ds(part * chunk, chunk)
        value = None
        for piece in range(pieces):
            basis = rights[piece][0]
            for side in range(2):
                term = jnp.dot(
                    lefts[2 * piece + side][at, :],
                    basis,
                    preferred_element_type=jnp.float32,
                )
                value = term if value is None else value + term

        @pl.when(step == 0)
        def _():
            if has_acc:
                total[at, :] = acc_in[at, :] + value
            else:
                total[at, :] = value

        @pl.when(step > 0)
        def _():
            total[at, :] += value

    @pl.when(step == steps - 1)
    def _():
        if not last:
            outs[0][...] = total[...]
        else:
            base = pieces * steps
            band = rows // (ZH * Y)
            for dy in range(Y):
                for half in range(ZH):
                    row = order[base + dy * ZH + half] * band
                    value = total[pl.ds(pl.multiple_of(row, 16), band), :]
                    outs[dy][half] = value.astype(outs[dy].dtype)


def project(order, grads, rights, acc, last):
    pieces = len(rights)
    steps, depth, width = rights[0].shape
    rows = grads[0].shape[0]
    in_specs = []
    operands = []
    for piece in range(pieces):
        for side in range(2):
            in_specs.append(
                pl.BlockSpec(
                    (rows, depth),
                    functools.partial(
                        lambda first, i, order: (0, order[first + i]), piece * steps
                    ),
                )
            )
            operands.append(grads[side])
    for right in rights:
        in_specs.append(pl.BlockSpec((1, depth, width), lambda i, order: (i, 0, 0)))
        operands.append(right)
    if acc is not None:
        in_specs.append(pl.BlockSpec((rows, width), lambda i, order: (0, 0)))
        operands.append(acc)
    if last:
        band = rows // (ZH * Y)
        shapes = [
            jax.ShapeDtypeStruct(
                (ZH, band, width), jnp.float32 if dy == 0 else jnp.bfloat16
            )
            for dy in range(Y)
        ]
        out_specs = [
            pl.BlockSpec((ZH, band, width), lambda i, order: (0, 0, 0))
            for _ in range(Y)
        ]
    else:
        shapes = [jax.ShapeDtypeStruct((rows, width), jnp.float32)]
        out_specs = [pl.BlockSpec((rows, width), lambda i, order: (0, 0))]
    return pl.pallas_call(
        functools.partial(project_kernel, pieces, last, acc is not None),
        out_shape=shapes,
        grid_spec=pltpu.PrefetchScalarGridSpec(
            num_scalar_prefetch=1,
            grid=(steps,),
            in_specs=in_specs,
            out_specs=out_specs,
            scratch_shapes=[pltpu.VMEM((rows, width), jnp.float32)],
        ),
        compiler_params=pltpu.CompilerParams(
            dimension_semantics=("arbitrary",), vmem_limit_bytes=28 * 1024 * 1024
        ),
        cost_estimate=pl.CostEstimate(
            flops=4 * pieces * steps * rows * depth * width,
            bytes_accessed=2 * pieces * steps * depth * (2 * rows + width)
            + 8 * rows * width,
            transcendentals=0,
        ),
    )(order, *operands)


def per_device(gradient, projector, first_moment, second_moment):
    blocks = gradient.shape[1]
    owned = gradient.shape[2]
    width = gradient.shape[3]
    depth, rank_cols = projector.shape
    half = rank_cols // 2
    part = half // GROUPS
    rows = blocks * owned
    dp = lax.axis_index("dp")
    fsdp = lax.axis_index("fsdp")
    zh, y, c = dp // (Y * C), (dp // C) % Y, dp % C
    x, zl = fsdp // ZL, fsdp % ZL

    own_grad = gradient.reshape(rows, width)
    grads = (own_grad, move(own_grad, other_core))
    own_half = lax.dynamic_slice(projector, (0, c * half), (depth, half))

    def column(inner, outer):
        dx = jnp.where(c == 0, inner, outer)
        dz = jnp.where(c == 0, outer, inner)
        return ((x + dx) % X) * ZL + (zl + dz) % ZL

    bands = [
        h * Y + (y + OFFSETS[dy]) % Y for dy in range(Y) for h in (zh, 1 - zh)
    ]
    order_a = jnp.stack([column(i, 0) for i in OFFSETS])
    order_b = jnp.stack([column(i, o) for o in (1, -1) for i in OFFSETS])
    order_c = jnp.stack([column(i, 2) for i in OFFSETS] + bands)

    reduced = []
    basis_own = []
    basis_send = []
    for group in range(GROUPS):
        piece = own_half[:, group * part : (group + 1) * part]
        held = [piece] + [
            move(piece, by_core(along_x(-o), along_ring(-o))) for o in OFFSETS[1:]
        ]
        held = jnp.stack(held)
        ahead = move(held, by_core(along_ring(-1), along_x(-1)))
        behind = move(held, by_core(along_ring(1), along_x(1)))
        far_a = move(ahead[:2], by_core(along_ring(-1), along_x(-1)))
        far_b = move(behind[2:], by_core(along_ring(1), along_x(1)))
        (acc,) = project(order_a, grads, [held], None, False)
        (acc,) = project(order_b, grads, [ahead, behind], acc, False)
        sums = project(order_c, grads, [far_a, far_b], acc, True)
        basis_own.append(held)
        basis_send.append(jnp.stack([held[0], ahead[0], behind[0], far_a[0]]))
        total = sums[0]
        for dy in range(1, Y):
            got = move(sums[dy], along_y(OFFSETS[dy]))
            total = total + got.astype(jnp.float32)
        got = move(total[1].astype(jnp.bfloat16), other_half)
        reduced.append(total[0] + got.astype(jnp.float32))
    reduced = jnp.concatenate(reduced, axis=1)
    mine = lax.dynamic_slice(reduced, (c * owned, 0), (owned, half))
    theirs = lax.dynamic_slice(reduced, ((1 - c) * owned, 0), (owned, half))
    other = move(theirs, other_core)
    projected = jnp.where(
        c == 0,
        jnp.concatenate([mine, other], axis=1),
        jnp.concatenate([other, mine], axis=1),
    ).reshape(1, owned, rank_cols)
    new_first = beta_one * first_moment + (1.0 - beta_one) * projected
    new_second = beta_two * second_moment + (1.0 - beta_two) * projected * projected
    direction = new_first / bias_one / (jnp.sqrt(new_second / bias_two) + epsilon)
    direction = direction.astype(jnp.bfloat16).reshape(owned, rank_cols)

    basis_own = jnp.concatenate(basis_own, axis=2)
    basis_other = move(jnp.concatenate(basis_send, axis=2), other_core)
    basis = jnp.where(
        c == 0,
        jnp.concatenate([basis_own, basis_other], axis=2),
        jnp.concatenate([basis_other, basis_own], axis=2),
    )
    gathered = jnp.stack(
        [direction]
        + [
            move(direction, by_core(along_line(-o), along_x(-o)))
            for o in OFFSETS[1:]
        ]
    ).reshape(4 * owned, rank_cols)
    pieces = []
    for i, offset in enumerate(OFFSETS):
        value = lax.dot_general(
            gathered,
            basis[i],
            (((1,), (1,)), ((), ())),
            preferred_element_type=jnp.float32,
        ).astype(jnp.bfloat16)
        if offset:
            value = move(value, by_core(along_x(offset), along_line(offset)))
        pieces.append(value.reshape(4, owned, depth))
    result = jnp.zeros((X * ZL, owned, depth), jnp.bfloat16)
    for i, outer in enumerate(OFFSETS):
        for j, inner in enumerate(OFFSETS):
            result = lax.dynamic_update_slice(
                result, pieces[i][j : j + 1], (column(-outer, inner), 0, 0)
            )
    update = result.reshape(1, X * ZL * owned, depth)
    return (update, new_first, new_second)


def solution(mesh):
    in_specs = (
        P("dp", None, "fsdp", None),
        P("fsdp", None),
        P("dp", "fsdp", None),
        P("dp", "fsdp", None),
    )
    out_specs = (P("dp", None, "fsdp"), P("dp", "fsdp", None), P("dp", "fsdp", None))
    return jax.shard_map(
        per_device, mesh=mesh, in_specs=in_specs, out_specs=out_specs, check_vma=False
    )
```

time: 345 us -> 112 us (0.32)
  waiting for transfers between devices: 290 us -> 36.8 us
  starting transfers between devices: 0.08 us -> 37.2 us
  Pallas kernels: 0 us -> 22.5 us
  matrix products: 20 us -> 1.35 us
  blocking collectives: 18.3 us -> 0 us
  between operations: 14.1 us -> 0.98 us
  local copies, waits for them, and re-layouts: 0.82 us -> 7.09 us
  other arithmetic: 1.01 us -> 4.88 us
    all_gather x1 -> x0, waiting for transfers between devices: 193 us -> none  [per_device(): full_basis = lax.all_gather(projector, 'fsdp', axis=0, tiled=True)]
    reduce_scatter x1 -> x0, waiting for transfers between devices: 96.4 us -> none  [per_device(): lax.psum_scatter(partial_value, 'dp', scatter_dimension=0, tiled=True)]
    ppermute x0 -> x20, starting transfers between devices: none -> 37.2 us  [move(): return lax.ppermute(value, AXES, pairs)]
    ppermute x0 -> x20, waiting for transfers between devices: none -> 36.8 us  [move(): return lax.ppermute(value, AXES, pairs)]
    pallas_call x0 -> x3, Pallas kernels: none -> 22.5 us  [project(): pl.pallas_call(functools.partial(project_kernel, pieces, last, acc is not...]
    dot_general x2 -> x4, matrix products: 20 us -> 1.35 us  [per_device(): lax.dot_general(gathered, basis[i], (((1,), (1,)), ((), ())), preferred_e...]
    all_to_all x1 -> x0, blocking collectives: 18.3 us -> none  [per_device(): lax.all_to_all(owner_rows, 'fsdp', split_axis=1, concat_axis=0, tiled=True)]
    unnamed x9 -> x10, local copies, waits for them, and re-layouts: 0.79 us -> 4.56 us
  transfers between devices with their start and end apart: 2 -> 20, of which waited for: 2 -> 12; matrix products, arithmetic and copies ran while one was open for 0% -> 7% of each run, Pallas kernels for 0% -> 15%
where the time goes in v1:
time: 112 us; the launch traced here: 111 us
  starting transfers between devices  37.2 us (33%)
  waiting for transfers between devices  36.8 us (33%)
  Pallas kernels  22.5 us (20%)
  local copies, waits for them, and re-layouts  7.09 us (6%)
  other arithmetic  4.88 us (4%)
  matrix products  1.35 us (1%)
    ppermute x20, starting transfers between devices, move(): return lax.ppermute(value, AXES, pairs)  37.2 us
    ppermute x20, waiting for transfers between devices, move(): return lax.ppermute(value, AXES, pairs)  36.8 us
    pallas_call x3, Pallas kernels, project(): pl.pallas_call(functools.partial(project_kernel, pieces, last, acc is not...  22.5 us
    unnamed x10, local copies, waits for them, and re-layouts  4.56 us
    select_n x1, other arithmetic, per_device(): jnp.where(c == 0, jnp.concatenate([basis_own, basis_other], axis=2), jnp....  2.38 us
  transfers between devices with their start and end apart: 20, of which 12 were waited for; matrix products, arithmetic and copies ran while one was open for 7% of the time, Pallas kernels for 15%

profile of v1, /device:TPU:1, one launch (start us, length us, event | category | flops | bytes accessed | tf_op | source)
XLA Modules:
  0.0 110.7 jit_solution(18359732547785217264)
XLA Ops:
  0.6 3.3 %collective-permute-start = (bf16[896,4096]{1,0:T(8,128)(2,1)}, bf16[896,4096]{1,0:T(8,128)(2,1)}, u32[]{:S(2)}, u32[]{:S(2)}) collective-permute-start(bf16[896,4096]{1,0:T(8,128)(2,1)} %bitcast.125), channel_id=1, source_target_pairs={{0,16},{1,17},{2,18},{3,19},{4,20},{5,21},{6,22},{7,23},{8,24},{9,... | collective-permute-start | bytes 22020104 | tf_op jit(solution)/shard_map/ppermute | solution.py:35
  4.0 4.6 %collective-permute-start.3 = (bf16[256,512]{1,0:T(8,128)(2,1)S(1)}, bf16[256,512]{1,0:T(8,128)(2,1)S(1)}, u32[]{:S(2)}, u32[]{:S(2)}) collective-permute-start(bf16[256,512]{1,0:T(8,128)(2,1)S(1)} %constant_dynamic-slice_fusion.1), channel_id=1, source_target_pairs={{0,8},{1,9},{2,10},{3,11},{4,12},{5,13},{6,14},{7,15},{8,0},{9,1},... | collective-permute-start | bytes 786440 | tf_op jit(solution)/shard_map/ppermute | solution.py:35
  8.6 0.7 collective-permute-start.2
  9.4 1.9 %collective-permute-start.1 = (bf16[256,512]{1,0:T(8,128)(2,1)S(1)}, bf16[256,512]{1,0:T(8,128)(2,1)S(1)}, u32[]{:S(2)}, u32[]{:S(2)}) collective-permute-start(bf16[256,512]{1,0:T(8,128)(2,1)S(1)} %constant_dynamic-slice_fusion.1), channel_id=1, source_target_pairs={{0,12},{1,13},{2,14},{3,15},{4,0},{5,1},{6,2},{7,3},{8,4},{9,5},{1... | collective-permute-start | bytes 786440 | tf_op jit(solution)/shard_map/ppermute | solution.py:35
  11.3 2.0 %collective-permute-done.3 = bf16[256,512]{1,0:T(8,128)(2,1)S(1)} collective-permute-done((bf16[256,512]{1,0:T(8,128)(2,1)S(1)}, bf16[256,512]{1,0:T(8,128)(2,1)S(1)}, u32[]{:S(2)}, u32[]{:S(2)}) %collective-permute-start.3) | collective-permute-done | bytes 262176 | tf_op jit(solution)/shard_map/ppermute | solution.py:35
  13.3 2.0 %collective-permute-done.2 = bf16[256,512]{1,0:T(8,128)(2,1)S(1)} collective-permute-done((bf16[256,512]{1,0:T(8,128)(2,1)S(1)}, bf16[256,512]{1,0:T(8,128)(2,1)S(1)}, u32[]{:S(2)}, u32[]{:S(2)}) %collective-permute-start.2) | collective-permute-done | bytes 262176 | tf_op jit(solution)/shard_map/ppermute | solution.py:35
  15.3 2.9 %collective-permute-done.1 = bf16[256,512]{1,0:T(8,128)(2,1)S(1)} collective-permute-done((bf16[256,512]{1,0:T(8,128)(2,1)S(1)}, bf16[256,512]{1,0:T(8,128)(2,1)S(1)}, u32[]{:S(2)}, u32[]{:S(2)}) %collective-permute-start.1) | collective-permute-done | bytes 262176 | tf_op jit(solution)/shard_map/ppermute | solution.py:35
  18.2 0.7 copy-done.3
  18.9 0.1 fusion.1.refs_2_
  19.0 2.0 %collective-permute-start.4 = (bf16[4,256,512]{2,1,0:T(8,128)(2,1)S(1)}, bf16[4,256,512]{2,1,0:T(8,128)(2,1)S(1)}, u32[]{:S(2)}, u32[]{:S(2)}) collective-permute-start(bf16[4,256,512]{2,1,0:T(8,128)(2,1)S(1)} %fusion.1.refs_2_), channel_id=1, source_target_pairs={{0,131},{1,0},{2,1},{3,2},{4,135},{5,4},{6,5},{7,6},{8,139},{9,8},... | collective-permute-start | bytes 3145736 | tf_op jit(solution)/shard_map/ppermute | solution.py:35
  21.0 0.1 stack.137.order
  21.0 0.1 stack.123.order
  21.2 11.9 %collective-permute-done.4.refs_4_ = bf16[4,256,512]{2,1,0:T(8,128)(2,1)S(1)} collective-permute-done((bf16[4,256,512]{2,1,0:T(8,128)(2,1)S(1)}, bf16[4,256,512]{2,1,0:T(8,128)(2,1)S(1)}, u32[]{:S(2)}, u32[]{:S(2)}) %collective-permute-start.4) | collective-permute-done | bytes 1048608 | tf_op jit(solution)/shard_map/ppermute | solution.py:35
  33.2 3.2 %collective-permute-start.5 = (bf16[2,256,512]{2,1,0:T(8,128)(2,1)S(1)}, bf16[2,256,512]{2,1,0:T(8,128)(2,1)S(1)}, u32[]{:S(2)}, u32[]{:S(2)}) collective-permute-start(bf16[2,256,512]{2,1,0:T(8,128)(2,1)S(1)} %slice.173), channel_id=1, source_target_pairs={{0,131},{1,0},{2,1},{3,2},{4,135},{5,4},{6,5},{7,6},{8,139},{9,8},... | collective-permute-start | bytes 1572872 | tf_op jit(solution)/shard_map/ppermute | solution.py:35
  36.3 1.1 slice.174
  37.4 0.1 collective-permute-start.7
  37.5 3.1 %copy-done.1 = bf16[1,16,56,4096]{3,2,1,0:T(8,128)(2,1)S(1)} copy-done((bf16[1,16,56,4096]{3,2,1,0:T(8,128)(2,1)S(1)}, bf16[1,16,56,4096]{3,2,1,0:T(8,128)(2,1)}, u32[]{:S(2)}) %copy-start.1) | copy-done | bytes 7340056
  40.6 7.3 %shard_map.67.refs_6_ = f32[896,512]{1,0:T(8,128)S(1)} custom-call(s32[4]{0:T(128)S(1)} %pad_add_fusion.order, bf16[896,4096]{1,0:T(8,128)(2,1)S(1)} %bitcast.126, bf16[896,4096]{1,0:T(8,128)(2,1)} %collective-permute-done.refs_1_.refs_3_, bf16[4,256,512]{2,1,0:T(8,128)(2,1)S(1)} %fusion.1.refs_2_), custom_call_target="tpu_custom_call" | custom-call | flops 1879048192 | bytes 8388608 | tf_op jit(solution)/shard_map/pallas_call | solution.py:160
  47.9 9.6 %shard_map.68.refs_6_ = f32[896,512]{1,0:T(8,128)S(1)} custom-call(s32[8]{0:T(128)S(1)} %stack.137.order, bf16[896,4096]{1,0:T(8,128)(2,1)S(1)} %bitcast.127, bf16[896,4096]{1,0:T(8,128)(2,1)} %collective-permute-done.refs_1_.refs_3_, bf16[896,4096]{1,0:T(8,128)(2,1)S(1)} %bitcast.128, bf16[896,4096]{1,0:T(8,128)(2,1)} %collective-permute-done.refs_1_.refs_3_, ...), custom_call_target="tpu_custom_call" | custom-call | flops 3758096384 | bytes 13107200 | tf_op jit(solution)/shard_map/pallas_call | solution.py:160
  57.6 5.5 %shard_map.69 = (f32[2,112,512]{2,1,0:T(8,128)S(1)}, bf16[2,112,512]{2,1,0:T(8,128)(2,1)S(1)}, bf16[2,112,512]{2,1,0:T(8,128)(2,1)S(1)}, bf16[2,112,512]{2,1,0:T(8,128)(2,1)S(1)}) custom-call(s32[12]{0:T(128)S(1)} %stack.123.order, bf16[896,4096]{1,0:T(8,128)(2,1)S(1)} %bitcast.129, bf16[896,4096]{1,0:T(8,128)(2,1)} %collective-permute-done.refs_1_.refs_3_, ...), custom_call_target="tpu_custom_call" | custom-call | flops 1879048192 | bytes 8388608 | tf_op jit(solution)/shard_map/pallas_call | solution.py:160
  63.1 3.0 %collective-permute-start.10 = (bf16[2,112,512]{2,1,0:T(8,128)(2,1)S(1)}, bf16[2,112,512]{2,1,0:T(8,128)(2,1)S(1)}, u32[]{:S(2)}, u32[]{:S(2)}) collective-permute-start(bf16[2,112,512]{2,1,0:T(8,128)(2,1)S(1)} %get-tuple-element.10), channel_id=1, source_target_pairs={{0,64},{1,65},{2,66},{3,67},{4,68},{5,69},{6,70},{7,71},{8,72},{9,... | collective-permute-start | bytes 688136 | tf_op jit(solution)/shard_map/ppermute | solution.py:35
  66.1 0.8 collective-permute-start.9
  66.9 0.7 collective-permute-start.8
  67.6 1.0 slice.178
  68.6 0.1 fusion.3
  68.8 1.5 %collective-permute-start.16 = (bf16[4,256,512]{2,1,0:T(8,128)(2,1)S(1)}, bf16[4,256,512]{2,1,0:T(8,128)(2,1)}, u32[]{:S(2)}, u32[]{:S(2)}) collective-permute-start(bf16[4,256,512]{2,1,0:T(8,128)(2,1)S(1)} %fusion.3), channel_id=1, source_target_pairs={{0,16},{1,17},{2,18},{3,19},{4,20},{5,21},{6,22},{7,23},{8,24},{9,... | collective-permute-start | bytes 3145736 | tf_op jit(solution)/shard_map/ppermute | solution.py:35
  70.3 1.0 collective-permute-done.10
  71.3 5.3 %collective-permute-done.9 = bf16[2,112,512]{2,1,0:T(8,128)(2,1)S(1)} collective-permute-done((bf16[2,112,512]{2,1,0:T(8,128)(2,1)S(1)}, bf16[2,112,512]{2,1,0:T(8,128)(2,1)S(1)}, u32[]{:S(2)}, u32[]{:S(2)}) %collective-permute-start.9) | collective-permute-done | bytes 229408 | tf_op jit(solution)/shard_map/ppermute | solution.py:35
  76.6 0.1 convert_add_fusion
  76.7 3.6 %collective-permute-start.11 = (bf16[112,512]{1,0:T(8,128)(2,1)S(1)}, bf16[112,512]{1,0:T(8,128)(2,1)S(1)}, u32[]{:S(2)}, u32[]{:S(2)}) collective-permute-start(bf16[112,512]{1,0:T(8,128)(2,1)S(1)} %fusion.6), channel_id=1, source_target_pairs={{0,128},{1,129},{2,130},{3,131},{4,132},{5,133},{6,134},{7,135},{8... | collective-permute-start | bytes 344072 | tf_op jit(solution)/shard_map/ppermute | solution.py:35
  80.3 4.4 %collective-permute-done.11 = bf16[112,512]{1,0:T(8,128)(2,1)S(1)} collective-permute-done((bf16[112,512]{1,0:T(8,128)(2,1)S(1)}, bf16[112,512]{1,0:T(8,128)(2,1)S(1)}, u32[]{:S(2)}, u32[]{:S(2)}) %collective-permute-start.11) | collective-permute-done | bytes 114720 | tf_op jit(solution)/shard_map/ppermute | solution.py:35
  84.8 4.6 %collective-permute-start.12 = (f32[56,512]{1,0:T(8,128)S(1)}, f32[56,512]{1,0:T(8,128)S(1)}, u32[]{:S(2)}, u32[]{:S(2)}) collective-permute-start(f32[56,512]{1,0:T(8,128)S(1)} %get-tuple-element.14), channel_id=1, source_target_pairs={{0,16},{1,17},{2,18},{3,19},{4,20},{5,21},{6,22},{7,23},{8,24},{9,... | collective-permute-start | bytes 344072 | tf_op jit(solution)/shard_map/ppermute | solution.py:35
  89.4 1.0 collective-permute-done.12
  90.3 2.0 %divide_convert_fusion = (bf16[1,56,1024]{2,1,0:T(8,128)(2,1)S(1)}, f32[1,56,1024]{2,1,0:T(8,128)}, f32[1,56,1024]{2,1,0:T(8,128)}) fusion(f32[1,56,512]{2,1,0:T(8,128)S(1)} %get-tuple-element.15, f32[1,56,512]{2,1,0:T(8,128)S(1)} %bitcast.145, pred[]{:T(512)S(6)} %eq.144, f32[1,56,1024]{2,1,0:T(8,128)} %param.6, f32[1,56,1024]{2,1,0:T(8,128)} %param.7), kind=kLoop, calls=%fused_computation.23 | loop fusion | flops 860160 | bytes 1261569 | tf_op jit(solution)/shard_map/convert_element_type | solution.py:247
  92.3 1.2 %collective-permute-start.15 = (bf16[56,1024]{1,0:T(8,128)(2,1)S(1)}, bf16[56,1024]{1,0:T(8,128)(2,1)S(1)}, u32[]{:S(2)}, u32[]{:S(2)}) collective-permute-start(bf16[56,1024]{1,0:T(8,128)(2,1)S(1)} %bitcast.137), channel_id=1, source_target_pairs={{0,2},{1,3},{2,0},{3,1},{4,6},{5,7},{6,4},{7,5},{8,10},{9,11},{10,... | collective-permute-start | bytes 344072 | tf_op jit(solution)/shard_map/ppermute | solution.py:35
  93.5 1.9 %collective-permute-start.14 = (bf16[56,1024]{1,0:T(8,128)(2,1)S(1)}, bf16[56,1024]{1,0:T(8,128)(2,1)S(1)}, u32[]{:S(2)}, u32[]{:S(2)}) collective-permute-start(bf16[56,1024]{1,0:T(8,128)(2,1)S(1)} %bitcast.138), channel_id=1, source_target_pairs={{0,1},{1,2},{2,3},{3,0},{4,5},{5,6},{6,7},{7,4},{8,9},{9,10},{10,1... | collective-permute-start | bytes 344072 | tf_op jit(solution)/shard_map/ppermute | solution.py:35
  95.4 0.7 collective-permute-start.13
  96.1 2.4 %maximum_select_fusion = bf16[4,256,1024]{2,1,0:T(8,128)(2,1)S(1)} fusion(bf16[4,256,512]{2,1,0:T(8,128)(2,1)} %collective-permute-done.16, bf16[1,256,512]{2,1,0:T(8,128)(2,1)S(1)} %bitcast.132, bf16[1,256,512]{2,1,0:T(8,128)(2,1)S(1)} %bitcast.134, bf16[1,256,512]{2,1,0:T(8,128)(2,1)} %bitcast.136, bf16[1,256,512]{2,1,0:T(8,128)(2,1)S(1)} %fusion.28, pred[]{:T(512)S(6)} %eq.144), kind=kLoop, calls=%fused_computation | loop fusion | flops 22020096 | bytes 4194305 | tf_op jit(solution)/shard_map/jit(_where)/select_n | solution.py:251
  98.5 0.3 collective-permute-done.14
  98.9 0.5 collective-permute-done.13
  99.4 0.3 convolution_convert_fusion.3
  99.7 0.3 convolution_convert_fusion.2
  100.1 0.3 convolution_convert_fusion.1
  100.4 0.3 convolution_convert_fusion
  100.9 3.3 %collective-permute-start.18 = (bf16[224,256]{1,0:T(8,128)(2,1)S(1)}, bf16[224,256]{1,0:T(8,128)(2,1)S(1)}, u32[]{:S(2)}, u32[]{:S(2)}) collective-permute-start(bf16[224,256]{1,0:T(8,128)(2,1)S(1)} %convolution_convert_fusion.1), channel_id=1, source_target_pairs={{0,12},{1,13},{2,14},{3,15},{4,0},{5,1},{6,2},{7,3},{8,4},{9,5},{1... | collective-permute-start | bytes 344072 | tf_op jit(solution)/shard_map/ppermute | solution.py:35
  104.2 2.1 %collective-permute-done.17 = bf16[224,256]{1,0:T(8,128)(2,1)S(1)} collective-permute-done((bf16[224,256]{1,0:T(8,128)(2,1)S(1)}, bf16[224,256]{1,0:T(8,128)(2,1)S(1)}, u32[]{:S(2)}, u32[]{:S(2)}) %collective-permute-start.17) | collective-permute-done | bytes 114720 | tf_op jit(solution)/shard_map/ppermute | solution.py:35
  106.4 3.5 %collective-permute-done.19 = bf16[224,256]{1,0:T(8,128)(2,1)S(1)} collective-permute-done((bf16[224,256]{1,0:T(8,128)(2,1)S(1)}, bf16[224,256]{1,0:T(8,128)(2,1)S(1)}, u32[]{:S(2)}, u32[]{:S(2)}) %collective-permute-start.19) | collective-permute-done | bytes 114720 | tf_op jit(solution)/shard_map/ppermute | solution.py:35
  110.0 0.8 copy-done.4
  (45 shorter events, 0.6 us)
Async XLA Ops:
  0.6 3.3 %copy-start = (bf16[256,1024]{1,0:T(8,128)(2,1)S(1)}, bf16[256,1024]{1,0:T(8,128)(2,1)}, u32[]{:S(2)}) copy-start(bf16[256,1024]{1,0:T(8,128)(2,1)} %param.5) | copy-start | bytes 1572868
  0.6 36.9 %collective-permute-start = (bf16[896,4096]{1,0:T(8,128)(2,1)}, bf16[896,4096]{1,0:T(8,128)(2,1)}, u32[]{:S(2)}, u32[]{:S(2)}) collective-permute-start(bf16[896,4096]{1,0:T(8,128)(2,1)} %bitcast.125), channel_id=1, source_target_pairs={{0,16},{1,17},{2,18},{3,19},{4,20},{5,21},{6,22},{7,23},{8,24},{9,... | collective-permute-start | bytes 22020104 | tf_op jit(solution)/shard_map/ppermute | solution.py:35
  4.0 9.3 %collective-permute-start.3 = (bf16[256,512]{1,0:T(8,128)(2,1)S(1)}, bf16[256,512]{1,0:T(8,128)(2,1)S(1)}, u32[]{:S(2)}, u32[]{:S(2)}) collective-permute-start(bf16[256,512]{1,0:T(8,128)(2,1)S(1)} %constant_dynamic-slice_fusion.1), channel_id=1, source_target_pairs={{0,8},{1,9},{2,10},{3,11},{4,12},{5,13},{6,14},{7,15},{8,0},{9,1},... | collective-permute-start | bytes 786440 | tf_op jit(solution)/shard_map/ppermute | solution.py:35
  8.6 6.7 %collective-permute-start.2 = (bf16[256,512]{1,0:T(8,128)(2,1)S(1)}, bf16[256,512]{1,0:T(8,128)(2,1)S(1)}, u32[]{:S(2)}, u32[]{:S(2)}) collective-permute-start(bf16[256,512]{1,0:T(8,128)(2,1)S(1)} %constant_dynamic-slice_fusion.1), channel_id=1, source_target_pairs={{0,4},{1,5},{2,6},{3,7},{4,8},{5,9},{6,10},{7,11},{8,12},{9,13},{1... | collective-permute-start | bytes 786440 | tf_op jit(solution)/shard_map/ppermute | solution.py:35
  9.4 8.8 %collective-permute-start.1 = (bf16[256,512]{1,0:T(8,128)(2,1)S(1)}, bf16[256,512]{1,0:T(8,128)(2,1)S(1)}, u32[]{:S(2)}, u32[]{:S(2)}) collective-permute-start(bf16[256,512]{1,0:T(8,128)(2,1)S(1)} %constant_dynamic-slice_fusion.1), channel_id=1, source_target_pairs={{0,12},{1,13},{2,14},{3,15},{4,0},{5,1},{6,2},{7,3},{8,4},{9,5},{1... | collective-permute-start | bytes 786440 | tf_op jit(solution)/shard_map/ppermute | solution.py:35
  18.2 0.7 copy-start.3
  19.0 14.1 %collective-permute-start.4 = (bf16[4,256,512]{2,1,0:T(8,128)(2,1)S(1)}, bf16[4,256,512]{2,1,0:T(8,128)(2,1)S(1)}, u32[]{:S(2)}, u32[]{:S(2)}) collective-permute-start(bf16[4,256,512]{2,1,0:T(8,128)(2,1)S(1)} %fusion.1.refs_2_), channel_id=1, source_target_pairs={{0,131},{1,0},{2,1},{3,2},{4,135},{5,4},{6,5},{7,6},{8,139},{9,8},... | collective-permute-start | bytes 3145736 | tf_op jit(solution)/shard_map/ppermute | solution.py:35
  21.0 15.4 %collective-permute-start.6 = (bf16[4,256,512]{2,1,0:T(8,128)(2,1)S(1)}, bf16[4,256,512]{2,1,0:T(8,128)(2,1)}, u32[]{:S(2)}, u32[]{:S(2)}) collective-permute-start(bf16[4,256,512]{2,1,0:T(8,128)(2,1)S(1)} %fusion.1.refs_2_), channel_id=1, source_target_pairs={{0,1},{1,2},{2,3},{3,128},{4,5},{5,6},{6,7},{7,132},{8,9},{9,10},{... | collective-permute-start | bytes 3145736 | tf_op jit(solution)/shard_map/ppermute | solution.py:35
  33.2 24.4 %collective-permute-start.5 = (bf16[2,256,512]{2,1,0:T(8,128)(2,1)S(1)}, bf16[2,256,512]{2,1,0:T(8,128)(2,1)S(1)}, u32[]{:S(2)}, u32[]{:S(2)}) collective-permute-start(bf16[2,256,512]{2,1,0:T(8,128)(2,1)S(1)} %slice.173), channel_id=1, source_target_pairs={{0,131},{1,0},{2,1},{3,2},{4,135},{5,4},{6,5},{7,6},{8,139},{9,8},... | collective-permute-start | bytes 1572872 | tf_op jit(solution)/shard_map/ppermute | solution.py:35
  37.4 20.1 %collective-permute-start.7 = (bf16[2,256,512]{2,1,0:T(8,128)(2,1)S(1)}, bf16[2,256,512]{2,1,0:T(8,128)(2,1)S(1)}, u32[]{:S(2)}, u32[]{:S(2)}) collective-permute-start(bf16[2,256,512]{2,1,0:T(8,128)(2,1)S(1)} %slice.174), channel_id=1, source_target_pairs={{0,1},{1,2},{2,3},{3,128},{4,5},{5,6},{6,7},{7,132},{8,9},{9,10},{... | collective-permute-start | bytes 1572872 | tf_op jit(solution)/shard_map/ppermute | solution.py:35
  37.5 3.1 %copy-start.1 = (bf16[1,16,56,4096]{3,2,1,0:T(8,128)(2,1)S(1)}, bf16[1,16,56,4096]{3,2,1,0:T(8,128)(2,1)}, u32[]{:S(2)}) copy-start(bf16[1,16,56,4096]{3,2,1,0:T(8,128)(2,1)} %param.4) | copy-start | bytes 22020100
  40.6 7.3 %copy-start.2 = (bf16[1,16,56,4096]{3,2,1,0:T(8,128)(2,1)S(1)}, bf16[1,16,56,4096]{3,2,1,0:T(8,128)(2,1)}, u32[]{:S(2)}) copy-start(bf16[1,16,56,4096]{3,2,1,0:T(8,128)(2,1)} %param.4) | copy-start | bytes 22020100
  63.1 8.1 %collective-permute-start.10 = (bf16[2,112,512]{2,1,0:T(8,128)(2,1)S(1)}, bf16[2,112,512]{2,1,0:T(8,128)(2,1)S(1)}, u32[]{:S(2)}, u32[]{:S(2)}) collective-permute-start(bf16[2,112,512]{2,1,0:T(8,128)(2,1)S(1)} %get-tuple-element.10), channel_id=1, source_target_pairs={{0,64},{1,65},{2,66},{3,67},{4,68},{5,69},{6,70},{7,71},{8,72},{9,... | collective-permute-start | bytes 688136 | tf_op jit(solution)/shard_map/ppermute | solution.py:35
  66.1 10.4 %collective-permute-start.9 = (bf16[2,112,512]{2,1,0:T(8,128)(2,1)S(1)}, bf16[2,112,512]{2,1,0:T(8,128)(2,1)S(1)}, u32[]{:S(2)}, u32[]{:S(2)}) collective-permute-start(bf16[2,112,512]{2,1,0:T(8,128)(2,1)S(1)} %get-tuple-element.9), channel_id=1, source_target_pairs={{0,96},{1,97},{2,98},{3,99},{4,100},{5,101},{6,102},{7,103},{8,104... | collective-permute-start | bytes 688136 | tf_op jit(solution)/shard_map/ppermute | solution.py:35
  66.9 9.7 %collective-permute-start.8 = (bf16[2,112,512]{2,1,0:T(8,128)(2,1)S(1)}, bf16[2,112,512]{2,1,0:T(8,128)(2,1)S(1)}, u32[]{:S(2)}, u32[]{:S(2)}) collective-permute-start(bf16[2,112,512]{2,1,0:T(8,128)(2,1)S(1)} %get-tuple-element.8), channel_id=1, source_target_pairs={{0,32},{1,33},{2,34},{3,35},{4,36},{5,37},{6,38},{7,39},{8,40},{9,... | collective-permute-start | bytes 688136 | tf_op jit(solution)/shard_map/ppermute | solution.py:35
  68.8 27.4 %collective-permute-start.16 = (bf16[4,256,512]{2,1,0:T(8,128)(2,1)S(1)}, bf16[4,256,512]{2,1,0:T(8,128)(2,1)}, u32[]{:S(2)}, u32[]{:S(2)}) collective-permute-start(bf16[4,256,512]{2,1,0:T(8,128)(2,1)S(1)} %fusion.3), channel_id=1, source_target_pairs={{0,16},{1,17},{2,18},{3,19},{4,20},{5,21},{6,22},{7,23},{8,24},{9,... | collective-permute-start | bytes 3145736 | tf_op jit(solution)/shard_map/ppermute | solution.py:35
  76.7 8.0 %collective-permute-start.11 = (bf16[112,512]{1,0:T(8,128)(2,1)S(1)}, bf16[112,512]{1,0:T(8,128)(2,1)S(1)}, u32[]{:S(2)}, u32[]{:S(2)}) collective-permute-start(bf16[112,512]{1,0:T(8,128)(2,1)S(1)} %fusion.6), channel_id=1, source_target_pairs={{0,128},{1,129},{2,130},{3,131},{4,132},{5,133},{6,134},{7,135},{8... | collective-permute-start | bytes 344072 | tf_op jit(solution)/shard_map/ppermute | solution.py:35
  84.8 5.5 %collective-permute-start.12 = (f32[56,512]{1,0:T(8,128)S(1)}, f32[56,512]{1,0:T(8,128)S(1)}, u32[]{:S(2)}, u32[]{:S(2)}) collective-permute-start(f32[56,512]{1,0:T(8,128)S(1)} %get-tuple-element.14), channel_id=1, source_target_pairs={{0,16},{1,17},{2,18},{3,19},{4,20},{5,21},{6,22},{7,23},{8,24},{9,... | collective-permute-start | bytes 344072 | tf_op jit(solution)/shard_map/ppermute | solution.py:35
  92.3 6.2 %collective-permute-start.15 = (bf16[56,1024]{1,0:T(8,128)(2,1)S(1)}, bf16[56,1024]{1,0:T(8,128)(2,1)S(1)}, u32[]{:S(2)}, u32[]{:S(2)}) collective-permute-start(bf16[56,1024]{1,0:T(8,128)(2,1)S(1)} %bitcast.137), channel_id=1, source_target_pairs={{0,2},{1,3},{2,0},{3,1},{4,6},{5,7},{6,4},{7,5},{8,10},{9,11},{10,... | collective-permute-start | bytes 344072 | tf_op jit(solution)/shard_map/ppermute | solution.py:35
  93.5 5.4 %collective-permute-start.14 = (bf16[56,1024]{1,0:T(8,128)(2,1)S(1)}, bf16[56,1024]{1,0:T(8,128)(2,1)S(1)}, u32[]{:S(2)}, u32[]{:S(2)}) collective-permute-start(bf16[56,1024]{1,0:T(8,128)(2,1)S(1)} %bitcast.138), channel_id=1, source_target_pairs={{0,1},{1,2},{2,3},{3,0},{4,5},{5,6},{6,7},{7,4},{8,9},{9,10},{10,1... | collective-permute-start | bytes 344072 | tf_op jit(solution)/shard_map/ppermute | solution.py:35
  95.4 3.9 %collective-permute-start.13 = (bf16[56,1024]{1,0:T(8,128)(2,1)S(1)}, bf16[56,1024]{1,0:T(8,128)(2,1)S(1)}, u32[]{:S(2)}, u32[]{:S(2)}) collective-permute-start(bf16[56,1024]{1,0:T(8,128)(2,1)S(1)} %bitcast.139), channel_id=1, source_target_pairs={{0,3},{1,0},{2,1},{3,2},{4,7},{5,4},{6,5},{7,6},{8,11},{9,8},{10,9... | collective-permute-start | bytes 344072 | tf_op jit(solution)/shard_map/ppermute | solution.py:35
  100.8 5.5 %collective-permute-start.17 = (bf16[224,256]{1,0:T(8,128)(2,1)S(1)}, bf16[224,256]{1,0:T(8,128)(2,1)S(1)}, u32[]{:S(2)}, u32[]{:S(2)}) collective-permute-start(bf16[224,256]{1,0:T(8,128)(2,1)S(1)} %convolution_convert_fusion.2), channel_id=1, source_target_pairs={{0,4},{1,5},{2,6},{3,7},{4,8},{5,9},{6,10},{7,11},{8,12},{9,13},{1... | collective-permute-start | bytes 344072 | tf_op jit(solution)/shard_map/ppermute | solution.py:35
  100.9 5.5 %collective-permute-start.18 = (bf16[224,256]{1,0:T(8,128)(2,1)S(1)}, bf16[224,256]{1,0:T(8,128)(2,1)S(1)}, u32[]{:S(2)}, u32[]{:S(2)}) collective-permute-start(bf16[224,256]{1,0:T(8,128)(2,1)S(1)} %convolution_convert_fusion.1), channel_id=1, source_target_pairs={{0,12},{1,13},{2,14},{3,15},{4,0},{5,1},{6,2},{7,3},{8,4},{9,5},{1... | collective-permute-start | bytes 344072 | tf_op jit(solution)/shard_map/ppermute | solution.py:35
  104.1 5.8 %collective-permute-start.19 = (bf16[224,256]{1,0:T(8,128)(2,1)S(1)}, bf16[224,256]{1,0:T(8,128)(2,1)S(1)}, u32[]{:S(2)}, u32[]{:S(2)}) collective-permute-start(bf16[224,256]{1,0:T(8,128)(2,1)S(1)} %convolution_convert_fusion), channel_id=1, source_target_pairs={{0,8},{1,9},{2,10},{3,11},{4,12},{5,13},{6,14},{7,15},{8,0},{9,1},... | collective-permute-start | bytes 344072 | tf_op jit(solution)/shard_map/ppermute | solution.py:35
  109.9 0.8 copy-start.4

commit v2 on v0

v2 whole, which is shorter than its diff:
```python
import functools

import jax
import jax.numpy as jnp
import numpy as np
from jax import lax
from jax.experimental import pallas as pl
from jax.experimental.pallas import tpu as pltpu
from jax.sharding import PartitionSpec as P

beta_one = 0.9
beta_two = 0.999
bias_one = 1.0 - 0.9**10
bias_two = 1.0 - 0.999**10
epsilon = 1e-08

ZH, Y, C, X, ZL = 2, 4, 2, 4, 4
AXES = ("dp", "fsdp")
OFFSETS = (0, 1, -1, 2)
GROUPS = 2


def linear(zh, y, c, x, zl):
    return (((zh * Y + y) * C + c) * X + x) * ZL + zl


def move(value, place):
    pairs = []
    for zh in range(ZH):
        for y in range(Y):
            for c in range(C):
                for x in range(X):
                    for zl in range(ZL):
                        target = place(zh, y, c, x, zl)
                        pairs.append((linear(zh, y, c, x, zl), linear(*target)))
    return lax.ppermute(value, AXES, pairs)


def along_x(step):
    return lambda zh, y, c, x, zl: (zh, y, c, (x + step) % X, zl)


def along_y(step):
    return lambda zh, y, c, x, zl: (zh, (y + step) % Y, c, x, zl)


def along_ring(step):
    def place(zh, y, c, x, zl):
        z = (zh * ZL + zl + step) % (ZH * ZL)
        return (z // ZL, y, c, x, z % ZL)

    return place


def along_line(step):
    return lambda zh, y, c, x, zl: (zh, y, c, x, (zl + step) % ZL)


def other_core(zh, y, c, x, zl):
    return (zh, y, 1 - c, x, zl)


def other_half(zh, y, c, x, zl):
    return (1 - zh, y, c, x, zl)


def by_core(first, second):
    def place(zh, y, c, x, zl):
        return (first if c == 0 else second)(zh, y, c, x, zl)

    return place


def block_at(c, x, zl, inner, outer):
    dx, dz = (inner, outer) if c == 0 else (outer, inner)
    return (x + dx) % X * ZL + (zl + dz) % ZL


def places_of(zh, y, c, x, zl):
    blocks = [block_at(c, x, zl, i, o) for o in OFFSETS for i in OFFSETS]
    rows = [block_at(c, x, zl, -i, o) for i in OFFSETS for o in OFFSETS]
    bands = [(y + o) % Y for o in OFFSETS]
    return blocks + bands + [zh, 1 - zh] + rows + [c]


BANDS = len(OFFSETS) ** 2
SLOTS = BANDS + Y
ROWS = SLOTS + ZH
CORE = ROWS + len(OFFSETS) ** 2


def all_places():
    return np.array(
        [
            places_of(zh, y, c, x, zl)
            for zh in range(ZH)
            for y in range(Y)
            for c in range(C)
            for x in range(X)
            for zl in range(ZL)
        ],
        np.int32,
    )


def project_kernel(outers, last, has_acc, places, *refs):
    grad, rest = refs[0], refs[1:]
    outs = rest[-(Y if last else 2) :]
    rest = rest[: -len(outs)]
    if has_acc:
        acc, rest = rest[-1], rest[:-1]
    pieces = [
        (OFFSETS.index(outer) * len(OFFSETS) + i, right, i)
        for outer, right in zip(outers, rest)
        for i in range(len(OFFSETS))
    ]
    depth, width = rest[0].shape[1:]
    band = grad.shape[1] // Y
    for dy in range(Y):
        row = places[BANDS + dy] if last else dy
        at = pl.ds(pl.multiple_of(row * band, 16), band)
        value = None
        for n, right, i in pieces:
            columns = pl.ds(pl.multiple_of(places[n] * depth, depth), depth)
            term = jnp.dot(
                grad[:, at, columns].reshape(ZH * band, depth),
                right[i],
                preferred_element_type=jnp.float32,
            )
            value = term if value is None else value + term
        value = value.reshape(ZH, band, width)
        if has_acc:
            value = value + acc[:, at, :]
        if last:
            for h in range(ZH):
                slot = places[SLOTS + h]
                outs[dy][slot] = value[h].astype(outs[dy].dtype)
        else:
            outs[0][:, at, :] = value
    if not last:
        outs[1][...] = value[0, : outs[1].shape[0], : outs[1].shape[1]]


def project(places, outers, grad, rights, acc, last):
    depth, width = rights[0].shape[1:]
    half_rows = grad.shape[1]
    count = sum(right.shape[0] for right in rights)
    whole = pl.BlockSpec(memory_space=pltpu.VMEM)
    operands = [grad, *rights] + ([] if acc is None else [acc])
    if last:
        shapes = [
            jax.ShapeDtypeStruct(
                (ZH, half_rows // Y, width), jnp.float32 if dy == 0 else jnp.bfloat16
            )
            for dy in range(Y)
        ]
    else:
        shapes = [
            jax.ShapeDtypeStruct((ZH, half_rows, width), jnp.float32),
            jax.ShapeDtypeStruct((8, 128), jnp.float32),
        ]
    return pl.pallas_call(
        functools.partial(project_kernel, outers, last, acc is not None),
        out_shape=shapes,
        in_specs=[pl.BlockSpec(memory_space=pltpu.SMEM)] + [whole] * len(operands),
        out_specs=[whole] * len(shapes),
        compiler_params=pltpu.CompilerParams(vmem_limit_bytes=14 * 1024 * 1024),
        cost_estimate=pl.CostEstimate(
            flops=2 * count * ZH * half_rows * depth * width,
            bytes_accessed=2 * count * depth * (2 * half_rows + width),
            transcendentals=0,
        ),
    )(places, *operands)


def stack_kernel(*refs):
    near, outs = refs[: len(OFFSETS)], refs[len(OFFSETS) + 2 :]
    for group, out in enumerate(outs):
        for i, piece in enumerate(near):
            out[i] = piece[group]


def stack_near(near, grad, places):
    groups, depth, width = near[0].shape
    whole = pl.BlockSpec(memory_space=pltpu.VMEM)
    return pl.pallas_call(
        stack_kernel,
        out_shape=[jax.ShapeDtypeStruct((len(near), depth, width), near[0].dtype)]
        * groups,
        in_specs=[whole] * len(near)
        + [pl.BlockSpec(memory_space=pltpu.HBM), pl.BlockSpec(memory_space=pltpu.SMEM)],
        out_specs=[whole] * groups,
        compiler_params=pltpu.CompilerParams(vmem_limit_bytes=5 * 1024 * 1024),
    )(*near, grad, places)


def add_kernel(first, second, out, slots, sems):
    band = slots.shape[2]
    per_half = out.shape[1] // band
    count = out.shape[0] * per_half

    def copies(n):
        at = (n // per_half, pl.ds((n % per_half) * band, band))
        return [
            pltpu.make_async_copy(
                ref.at[at], slots.at[side, n % 2], sems.at[side, n % 2]
            )
            for side, ref in enumerate((first, second))
        ]

    for copy in copies(0):
        copy.start()
    for n in range(count):
        if n + 1 < count:
            for copy in copies(n + 1):
                copy.start()
        for copy in copies(n):
            copy.wait()
        row = (n % per_half) * band

        def rows_on(i, carry):
            at = pl.ds(pl.multiple_of(i * 16, 16), 16)
            into = pl.ds(pl.multiple_of(row + i * 16, 16), 16)
            out[n // per_half, into, :] = slots[0, n % 2, at] + slots[1, n % 2, at]
            return carry

        lax.fori_loop(0, band // 16, rows_on, 0)


def add(first, second):
    halves, rows, width = first.shape
    band = rows // 4
    anywhere = pl.BlockSpec(memory_space=pltpu.HBM)
    return pl.pallas_call(
        add_kernel,
        out_shape=jax.ShapeDtypeStruct(first.shape, first.dtype),
        in_specs=[anywhere, anywhere],
        out_specs=pl.BlockSpec(memory_space=pltpu.VMEM),
        scratch_shapes=[
            pltpu.VMEM((2, 2, band, width), first.dtype),
            pltpu.SemaphoreType.DMA((2, 2)),
        ],
        compiler_params=pltpu.CompilerParams(vmem_limit_bytes=13 * 1024 * 1024),
        cost_estimate=pl.CostEstimate(
            flops=halves * rows * width,
            bytes_accessed=6 * halves * rows * width,
            transcendentals=0,
        ),
    )(first, second)


def pass_on(value, *after):
    main = pl.BlockSpec(memory_space=pltpu.HBM)
    return pl.pallas_call(
        lambda *refs: None,
        out_shape=jax.ShapeDtypeStruct(value.shape, value.dtype),
        in_specs=[main] + [pl.BlockSpec(memory_space=pl.ANY)] * len(after),
        out_specs=main,
        input_output_aliases={0: 0},
        compiler_params=pltpu.CompilerParams(vmem_limit_bytes=1024 * 1024),
    )(value, *after)


def collect_kernel(*refs):
    ins, out = refs[:-1], refs[-1]
    pieces, _, width = out.shape
    part = ins[0].shape[2]
    for n, ref in enumerate(ins):
        group, piece = n // pieces, n % pieces
        out[piece, :, group * part : (group + 1) * part] = ref[0]


def collect(groups):
    arrays = [array for group in groups for array in group]
    _, depth, part = arrays[0].shape
    pieces, width = len(groups[0]), part * len(groups)
    return pl.pallas_call(
        collect_kernel,
        grid=(1,),
        out_shape=jax.ShapeDtypeStruct((pieces, depth, width), arrays[0].dtype),
        in_specs=[pl.BlockSpec((1, depth, part), lambda i: (0, 0, 0))] * len(arrays),
        out_specs=pl.BlockSpec((pieces, depth, width), lambda i: (0, 0, 0)),
        compiler_params=pltpu.CompilerParams(vmem_limit_bytes=5 * 1024 * 1024),
    )(*arrays)


def split_kernel(groups, places, *refs):
    sums, mine, theirs = refs[:-2], refs[-2], refs[-1]
    owned = mine.shape[0]
    own = pl.ds(pl.multiple_of(places[CORE] * owned, 8), owned)
    other = pl.ds(pl.multiple_of((1 - places[CORE]) * owned, 8), owned)
    part = mine.shape[1] // groups
    for group in range(groups):
        kept, got = sums[2 * group : 2 * group + 2]
        at = slice(group * part, (group + 1) * part)
        mine[:, at] = kept[own, :] + got[own, :]
        theirs[:, at] = kept[other, :] + got[other, :]


def split(places, sums):
    groups = len(sums) // 2
    rows, part = sums[0].shape
    whole = pl.BlockSpec(memory_space=pltpu.VMEM)
    return pl.pallas_call(
        functools.partial(split_kernel, groups),
        out_shape=[jax.ShapeDtypeStruct((rows // C, part * groups), jnp.float32)] * 2,
        in_specs=[pl.BlockSpec(memory_space=pltpu.SMEM)] + [whole] * len(sums),
        out_specs=[whole] * 2,
        compiler_params=pltpu.CompilerParams(vmem_limit_bytes=5 * 1024 * 1024),
    )(places, *sums)


def adam_kernel(places, mine, other, first, second, new_first, new_second, direction):
    half = mine.shape[1]
    is_first = places[CORE] == 0
    own, far = mine[...], other[...]
    for n in range(C):
        at = slice(n * half, (n + 1) * half)
        value = jnp.where(is_first, far, own) if n else jnp.where(is_first, own, far)
        moment = beta_one * first[0, :, at] + (1.0 - beta_one) * value
        square = beta_two * second[0, :, at] + (1.0 - beta_two) * value * value
        new_first[0, :, at] = moment
        new_second[0, :, at] = square
    for n in range(C):
        step = []
        for m in (n, 1 - n):
            at = slice(m * half, (m + 1) * half)
            root = jnp.sqrt(new_second[0, :, at] / bias_two) + epsilon
            step.append(new_first[0, :, at] / bias_one / root)
        value = jnp.where(is_first, step[0], step[1])
        direction[:, n * half : (n + 1) * half] = value.astype(direction.dtype)


def adam(places, mine, other, first, second):
    whole = pl.BlockSpec(memory_space=pltpu.VMEM)
    return pl.pallas_call(
        adam_kernel,
        out_shape=[
            jax.ShapeDtypeStruct(first.shape, jnp.float32),
            jax.ShapeDtypeStruct(first.shape, jnp.float32),
            jax.ShapeDtypeStruct(first.shape[1:], jnp.bfloat16),
        ],
        in_specs=[pl.BlockSpec(memory_space=pltpu.SMEM)] + [whole] * 4,
        out_specs=[whole] * 3,
        compiler_params=pltpu.CompilerParams(vmem_limit_bytes=5 * 1024 * 1024),
    )(places, mine, other, first, second)


def place_kernel(places, *refs):
    pieces, out = refs[:-1], refs[-1]
    for i, piece in enumerate(pieces):
        for j in range(len(OFFSETS)):
            out[places[ROWS + i * len(OFFSETS) + j]] = piece[j]


def place_rows(places, pieces):
    count, owned, depth = pieces[0].shape
    whole = pl.BlockSpec(memory_space=pltpu.VMEM)
    return pl.pallas_call(
        place_kernel,
        out_shape=jax.ShapeDtypeStruct((count * len(pieces), owned, depth), jnp.bfloat16),
        in_specs=[pl.BlockSpec(memory_space=pltpu.SMEM)] + [whole] * len(pieces),
        out_specs=whole,
        compiler_params=pltpu.CompilerParams(vmem_limit_bytes=5 * 1024 * 1024),
    )(places, *pieces)


def per_device(gradient, projector, first_moment, second_moment):
    blocks = gradient.shape[1]
    owned = gradient.shape[2]
    width = gradient.shape[3]
    depth, rank_cols = projector.shape
    half = rank_cols // 2
    part = half // GROUPS
    rows = blocks * owned
    dp = lax.axis_index("dp")
    fsdp = lax.axis_index("fsdp")
    places = lax.dynamic_index_in_dim(
        jnp.asarray(all_places()), dp * (X * ZL) + fsdp, 0, keepdims=False
    )
    c = dp % C

    own_grad = gradient.reshape(ZH, rows // ZH, width)
    other_grad = move(own_grad, other_core)
    both = add(own_grad, other_grad)
    own_half = lax.dynamic_slice(projector, (0, c * half), (depth, half))
    own_half = jnp.stack(
        [own_half[:, g * part : (g + 1) * part] for g in range(GROUPS)]
    )
    near = [own_half] + [
        move(own_half, by_core(along_x(-o), along_ring(-o))) for o in OFFSETS[1:]
    ]

    reduced = []
    stacks = stack_near(near, other_grad, places)
    ahead = [move(held, by_core(along_ring(-1), along_x(-1))) for held in stacks]
    behind = [move(held, by_core(along_ring(1), along_x(1))) for held in stacks]
    accs, done = zip(
        *[project(places, (0,), both, [held], None, False) for held in stacks]
    )
    ahead[0] = pass_on(ahead[0], *done)
    behind[1] = pass_on(behind[1], *done)
    far = [
        move(ahead[0], by_core(along_ring(-1), along_x(-1))),
        move(behind[1], by_core(along_ring(1), along_x(1))),
    ]
    for group in range(GROUPS):
        acc, _ = project(
            places, (1, -1), both, [ahead[group], behind[group]], accs[group], False
        )
        sums = project(places, (2,), both, [far[group]], acc, True)
        total = sums[0]
        for dy in range(1, Y):
            got = move(sums[dy], along_y(OFFSETS[dy]))
            total = total + got.astype(jnp.float32)
        got = move(total[1].astype(jnp.bfloat16), other_half)
        reduced += [total[0], got.astype(jnp.float32)]
    mine, theirs = split(places, reduced)
    other = move(theirs, other_core)
    new_first, new_second, direction = adam(
        places, mine, other, first_moment, second_moment
    )
    basis_other = move(collect(list(zip(stacks, ahead, behind, far))), other_core)
    basis = jnp.concatenate([*stacks, basis_other], axis=2)
    gathered = jnp.stack(
        [direction]
        + [
            move(direction, by_core(along_line(-o), along_x(-o)))
            for o in OFFSETS[1:]
        ]
    ).reshape(4 * owned, rank_cols)
    pieces = []
    for i, offset in enumerate(OFFSETS):
        value = lax.dot_general(
            gathered,
            basis[i],
            (((1,), (1,)), ((), ())),
            preferred_element_type=jnp.float32,
        ).astype(jnp.bfloat16)
        if offset:
            value = move(value, by_core(along_x(offset), along_line(offset)))
        pieces.append(value.reshape(4, owned, depth))
    result = place_rows(places, pieces)
    update = result.reshape(1, X * ZL * owned, depth)
    return (update, new_first, new_second)


def solution(mesh):
    in_specs = (
        P("dp", None, "fsdp", None),
        P("fsdp", None),
        P("dp", "fsdp", None),
        P("dp", "fsdp", None),
    )
    out_specs = (P("dp", None, "fsdp"), P("dp", "fsdp", None), P("dp", "fsdp", None))
    return jax.shard_map(
        per_device, mesh=mesh, in_specs=in_specs, out_specs=out_specs, check_vma=False
    )
```

time: 345 us -> 92.3 us (0.27)
  waiting for transfers between devices: 290 us -> 22.9 us
  starting transfers between devices: 0.08 us -> 44.4 us
  Pallas kernels: 0 us -> 19.9 us
  matrix products: 20 us -> 1.36 us
  blocking collectives: 18.3 us -> 0 us
  between operations: 14.1 us -> 0.87 us
    all_gather x1 -> x0, waiting for transfers between devices: 193 us -> none  [per_device(): full_basis = lax.all_gather(projector, 'fsdp', axis=0, tiled=True)]
    reduce_scatter x1 -> x0, waiting for transfers between devices: 96.4 us -> none  [per_device(): lax.psum_scatter(partial_value, 'dp', scatter_dimension=0, tiled=True)]
    ppermute x0 -> x26, starting transfers between devices: none -> 44.4 us  [move(): return lax.ppermute(value, AXES, pairs)]
    ppermute x0 -> x26, waiting for transfers between devices: none -> 22.9 us  [move(): return lax.ppermute(value, AXES, pairs)]
    pallas_call x0 -> x14, Pallas kernels: none -> 19.9 us  [the longest x6 9.24 us: project(): pl.pallas_call(functools.partial(project_kernel, outers, last, acc is not...]
    dot_general x2 -> x4, matrix products: 20 us -> 1.36 us  [per_device(): lax.dot_general(gathered, basis[i], (((1,), (1,)), ((), ())), preferred_e...]
    all_to_all x1 -> x0, blocking collectives: 18.3 us -> none  [per_device(): lax.all_to_all(owner_rows, 'fsdp', split_axis=1, concat_axis=0, tiled=True)]
  transfers between devices with their start and end apart: 2 -> 26, of which waited for: 2 -> 13; matrix products, arithmetic and copies ran while one was open for 0% -> 3% of each run, Pallas kernels for 0% -> 19%
where the time goes in v2:
time: 92.3 us; the launch traced here: 92.1 us
  starting transfers between devices  44.4 us (48%)
  waiting for transfers between devices  22.9 us (25%)
  Pallas kernels  19.9 us (22%)
  local copies, waits for them, and re-layouts  2.38 us (3%)
  matrix products  1.36 us (1%)
    ppermute x26, starting transfers between devices, move(): return lax.ppermute(value, AXES, pairs)  44.4 us
    ppermute x26, waiting for transfers between devices, move(): return lax.ppermute(value, AXES, pairs)  22.9 us
    pallas_call x6, Pallas kernels, project(): pl.pallas_call(functools.partial(project_kernel, outers, last, acc is not...  9.24 us
    pallas_call x1, Pallas kernels, add(): pl.pallas_call(add_kernel, out_shape=jax.ShapeDtypeStruct(first.shape, fi...  6.64 us
  transfers between devices with their start and end apart: 26, of which 13 were waited for; matrix products, arithmetic and copies ran while one was open for 3% of the time, Pallas kernels for 19%

profile of v2, /device:TPU:1, one launch (start us, length us, event | category | flops | bytes accessed | tf_op | source)
XLA Modules:
  0.0 92.1 jit_solution(2624528417740937329)
XLA Ops:
  0.6 3.3 %collective-permute-start = (bf16[2,448,4096]{2,1,0:T(8,128)(2,1)}, bf16[2,448,4096]{2,1,0:T(8,128)(2,1)}, u32[]{:S(2)}, u32[]{:S(2)}) collective-permute-start(bf16[2,448,4096]{2,1,0:T(8,128)(2,1)} %bitcast.41), channel_id=1, source_target_pairs={{0,16},{1,17},{2,18},{3,19},{4,20},{5,21},{6,22},{7,23},{8,24},{9,... | collective-permute-start | bytes 22020104 | tf_op jit(solution)/shard_map/ppermute | solution.py:36
  4.0 1.0 %dynamic-slice_bitcast_fusion.1 = (bf16[1,256,256]{2,1,0:T(8,128)(2,1)S(1)}, bf16[1,256,256]{2,1,0:T(8,128)(2,1)S(1)}) fusion(bf16[256,1024]{1,0:T(8,128)(2,1)} %param.6, s32[]{:T(128)S(6)} %select_n.16, s32[]{:T(128)S(6)} %add.42), kind=kLoop, calls=%fused_computation.13 | loop fusion | bytes 524296 | tf_op jit(solution)/shard_map/stack | solution.py:387
  5.0 4.4 %collective-permute-start.3 = (bf16[2,256,256]{2,1,0:T(8,128)(2,1)S(1)}, bf16[2,256,256]{2,1,0:T(8,128)(2,1)S(1)}, u32[]{:S(2)}, u32[]{:S(2)}) collective-permute-start(bf16[2,256,256]{2,1,0:T(8,128)(2,1)S(1)} %pad_maximum_fusion.1.refs_0_), channel_id=1, source_target_pairs={{0,8},{1,9},{2,10},{3,11},{4,12},{5,13},{6,14},{7,15},{8,0},{9,1},... | collective-permute-start | bytes 786440 | tf_op jit(solution)/shard_map/ppermute | solution.py:36
  9.3 0.7 collective-permute-start.2
  10.1 1.9 %collective-permute-start.1 = (bf16[2,256,256]{2,1,0:T(8,128)(2,1)S(1)}, bf16[2,256,256]{2,1,0:T(8,128)(2,1)S(1)}, u32[]{:S(2)}, u32[]{:S(2)}) collective-permute-start(bf16[2,256,256]{2,1,0:T(8,128)(2,1)S(1)} %pad_maximum_fusion.1.refs_0_), channel_id=1, source_target_pairs={{0,12},{1,13},{2,14},{3,15},{4,0},{5,1},{6,2},{7,3},{8,4},{9,5},{1... | collective-permute-start | bytes 786440 | tf_op jit(solution)/shard_map/ppermute | solution.py:36
  12.0 0.7 fusion.2.refs_5_.places
  12.7 1.6 %collective-permute-done.3.refs_3_ = bf16[2,256,256]{2,1,0:T(8,128)(2,1)S(1)} collective-permute-done((bf16[2,256,256]{2,1,0:T(8,128)(2,1)S(1)}, bf16[2,256,256]{2,1,0:T(8,128)(2,1)S(1)}, u32[]{:S(2)}, u32[]{:S(2)}) %collective-permute-start.3) | collective-permute-done | bytes 262176 | tf_op jit(solution)/shard_map/ppermute | solution.py:36
  14.3 1.5 %collective-permute-done.2.refs_2_ = bf16[2,256,256]{2,1,0:T(8,128)(2,1)S(1)} collective-permute-done((bf16[2,256,256]{2,1,0:T(8,128)(2,1)S(1)}, bf16[2,256,256]{2,1,0:T(8,128)(2,1)S(1)}, u32[]{:S(2)}, u32[]{:S(2)}) %collective-permute-start.2) | collective-permute-done | bytes 262176 | tf_op jit(solution)/shard_map/ppermute | solution.py:36
  15.8 3.4 %collective-permute-done.1.refs_1_ = bf16[2,256,256]{2,1,0:T(8,128)(2,1)S(1)} collective-permute-done((bf16[2,256,256]{2,1,0:T(8,128)(2,1)S(1)}, bf16[2,256,256]{2,1,0:T(8,128)(2,1)S(1)}, u32[]{:S(2)}, u32[]{:S(2)}) %collective-permute-start.1) | collective-permute-done | bytes 262176 | tf_op jit(solution)/shard_map/ppermute | solution.py:36
  19.2 0.6 shard_map.77
  19.8 1.7 %collective-permute-start.4 = (bf16[4,256,256]{2,1,0:T(8,128)(2,1)S(1)}, bf16[4,256,256]{2,1,0:T(8,128)(2,1)S(1)}, u32[]{:S(2)}, u32[]{:S(2)}) collective-permute-start(bf16[4,256,256]{2,1,0:T(8,128)(2,1)S(1)} %get-tuple-element.24.refs_1_.refs_0_), channel_id=1, source_target_pairs={{0,131},{1,0},{2,1},{3,2},{4,135},{5,4},{6,5},{7,6},{8,139},{9,8},... | collective-permute-start | bytes 1572872 | tf_op jit(solution)/shard_map/ppermute | solution.py:36
  21.5 0.4 collective-permute-start.6
  21.8 0.4 copy-done
  22.2 6.6 %shard_map.76.refs_0_ = bf16[2,448,4096]{2,1,0:T(8,128)(2,1)S(1)} custom-call(bf16[2,448,4096]{2,1,0:T(8,128)(2,1)S(1)} %bitcast.42, bf16[2,448,4096]{2,1,0:T(8,128)(2,1)} %collective-permute-done.second.refs_4_), custom_call_target="tpu_custom_call" | custom-call | flops 3670016 | bytes 22020096 | tf_op jit(solution)/shard_map/pallas_call | solution.py:234
  28.9 1.2 %shard_map.78 = (f32[2,448,256]{2,1,0:T(8,128)S(1)}, f32[8,128]{1,0:T(8,128)S(1)}) custom-call(s32[39]{0:T(128)S(1)} %fusion.2.refs_5_.places, bf16[2,448,4096]{2,1,0:T(8,128)(2,1)S(1)} %shard_map.76.refs_0_, bf16[4,256,256]{2,1,0:T(8,128)(2,1)S(1)} %get-tuple-element.24.refs_1_.refs_0_), custom_call_target="tpu_custom_call" | custom-call | flops 469762048 | bytes 2359296 | tf_op jit(solution)/shard_map/pallas_call | solution.py:162
  30.1 1.2 %shard_map.79 = (f32[2,448,256]{2,1,0:T(8,128)S(1)}, f32[8,128]{1,0:T(8,128)S(1)}) custom-call(s32[39]{0:T(128)S(1)} %fusion.2.refs_5_.places, bf16[2,448,4096]{2,1,0:T(8,128)(2,1)S(1)} %shard_map.76.refs_0_, bf16[4,256,256]{2,1,0:T(8,128)(2,1)S(1)} %get-tuple-element.26.refs_1_.refs_4_), custom_call_target="tpu_custom_call" | custom-call | flops 469762048 | bytes 2359296 | tf_op jit(solution)/shard_map/pallas_call | solution.py:162
  31.3 2.0 %collective-permute-start.5 = (bf16[4,256,256]{2,1,0:T(8,128)(2,1)S(1)}, bf16[4,256,256]{2,1,0:T(8,128)(2,1)S(1)}, u32[]{:S(2)}, u32[]{:S(2)}) collective-permute-start(bf16[4,256,256]{2,1,0:T(8,128)(2,1)S(1)} %shard_map.80.refs_1_), channel_id=1, source_target_pairs={{0,131},{1,0},{2,1},{3,2},{4,135},{5,4},{6,5},{7,6},{8,139},{9,8},... | collective-permute-start | bytes 1572872 | tf_op jit(solution)/shard_map/ppermute | solution.py:36
  33.3 1.4 %collective-permute-start.13 = (bf16[4,256,256]{2,1,0:T(8,128)(2,1)S(1)}, bf16[4,256,256]{2,1,0:T(8,128)(2,1)S(1)}, u32[]{:S(2)}, u32[]{:S(2)}) collective-permute-start(bf16[4,256,256]{2,1,0:T(8,128)(2,1)S(1)} %get-tuple-element.26.refs_1_.refs_4_), channel_id=1, source_target_pairs={{0,131},{1,0},{2,1},{3,2},{4,135},{5,4},{6,5},{7,6},{8,139},{9,8},... | collective-permute-start | bytes 1572872 | tf_op jit(solution)/shard_map/ppermute | solution.py:36
  34.8 1.6 %collective-permute-done.6.refs_2_ = bf16[4,256,256]{2,1,0:T(8,128)(2,1)S(1)} collective-permute-done((bf16[4,256,256]{2,1,0:T(8,128)(2,1)S(1)}, bf16[4,256,256]{2,1,0:T(8,128)(2,1)S(1)}, u32[]{:S(2)}, u32[]{:S(2)}) %collective-permute-start.6) | collective-permute-done | bytes 524320 | tf_op jit(solution)/shard_map/ppermute | solution.py:36
  36.4 2.2 %shard_map.81 = (f32[2,448,256]{2,1,0:T(8,128)S(1)}, f32[8,128]{1,0:T(8,128)}) custom-call(s32[39]{0:T(128)S(1)} %fusion.2.refs_5_.places, bf16[2,448,4096]{2,1,0:T(8,128)(2,1)S(1)} %shard_map.76.refs_0_, bf16[4,256,256]{2,1,0:T(8,128)(2,1)S(1)} %shard_map.80.refs_1_, bf16[4,256,256]{2,1,0:T(8,128)(2,1)S(1)} %collective-permute-done.6.refs_2_, ...), custom_call_target="tpu_custom_call" | custom-call | flops 939524096 | bytes 4718592 | tf_op jit(solution)/shard_map/pallas_call | solution.py:162
  38.6 1.1 %collective-permute-done.5.refs_1_.refs_3_ = bf16[4,256,256]{2,1,0:T(8,128)(2,1)S(1)} collective-permute-done((bf16[4,256,256]{2,1,0:T(8,128)(2,1)S(1)}, bf16[4,256,256]{2,1,0:T(8,128)(2,1)S(1)}, u32[]{:S(2)}, u32[]{:S(2)}) %collective-permute-start.5) | collective-permute-done | bytes 524320 | tf_op jit(solution)/shard_map/ppermute | solution.py:36
  39.7 1.2 %shard_map.82 = (f32[2,112,256]{2,1,0:T(8,128)S(1)}, bf16[2,112,256]{2,1,0:T(8,128)(2,1)S(1)}, bf16[2,112,256]{2,1,0:T(8,128)(2,1)S(1)}, bf16[2,112,256]{2,1,0:T(8,128)(2,1)S(1)}) custom-call(s32[39]{0:T(128)S(1)} %fusion.2.refs_5_.places, bf16[2,448,4096]{2,1,0:T(8,128)(2,1)S(1)} %shard_map.76.refs_0_, ...), custom_call_target="tpu_custom_call" | custom-call | flops 469762048 | bytes 2359296 | tf_op jit(solution)/shard_map/pallas_call | solution.py:162
  40.9 1.1 %collective-permute-start.7 = (bf16[2,112,256]{2,1,0:T(8,128)(2,1)S(1)}, bf16[2,112,256]{2,1,0:T(8,128)(2,1)S(1)}, u32[]{:S(2)}, u32[]{:S(2)}) collective-permute-start(bf16[2,112,256]{2,1,0:T(8,128)(2,1)S(1)} %get-tuple-element.31), channel_id=1, source_target_pairs={{0,32},{1,33},{2,34},{3,35},{4,36},{5,37},{6,38},{7,39},{8,40},{9,... | collective-permute-start | bytes 344072 | tf_op jit(solution)/shard_map/ppermute | solution.py:36
  42.0 1.6 %collective-permute-start.8 = (bf16[2,112,256]{2,1,0:T(8,128)(2,1)S(1)}, bf16[2,112,256]{2,1,0:T(8,128)(2,1)S(1)}, u32[]{:S(2)}, u32[]{:S(2)}) collective-permute-start(bf16[2,112,256]{2,1,0:T(8,128)(2,1)S(1)} %get-tuple-element.32), channel_id=1, source_target_pairs={{0,96},{1,97},{2,98},{3,99},{4,100},{5,101},{6,102},{7,103},{8,104... | collective-permute-start | bytes 344072 | tf_op jit(solution)/shard_map/ppermute | solution.py:36
  43.7 1.4 %collective-permute-start.9 = (bf16[2,112,256]{2,1,0:T(8,128)(2,1)S(1)}, bf16[2,112,256]{2,1,0:T(8,128)(2,1)S(1)}, u32[]{:S(2)}, u32[]{:S(2)}) collective-permute-start(bf16[2,112,256]{2,1,0:T(8,128)(2,1)S(1)} %get-tuple-element.33), channel_id=1, source_target_pairs={{0,64},{1,65},{2,66},{3,67},{4,68},{5,69},{6,70},{7,71},{8,72},{9,... | collective-permute-start | bytes 344072 | tf_op jit(solution)/shard_map/ppermute | solution.py:36
  45.2 2.2 %shard_map.84 = (f32[2,448,256]{2,1,0:T(8,128)S(1)}, f32[8,128]{1,0:T(8,128)}) custom-call(s32[39]{0:T(128)S(1)} %fusion.2.refs_5_.places, bf16[2,448,4096]{2,1,0:T(8,128)(2,1)S(1)} %shard_map.76.refs_0_, bf16[4,256,256]{2,1,0:T(8,128)(2,1)S(1)} %collective-permute-done.13.refs_1_.refs_5_, bf16[4,256,256]{2,1,0:T(8,128)(2,1)S(1)} %shard_map.83.refs_2_.refs_6_, ...), custom_call_target="tpu_custom_call" | custom-call | flops 939524096 | bytes 4718592 | tf_op jit(solution)/shard_map/pallas_call | solution.py:162
  47.4 1.2 %shard_map.85 = (f32[2,112,256]{2,1,0:T(8,128)S(1)}, bf16[2,112,256]{2,1,0:T(8,128)(2,1)S(1)}, bf16[2,112,256]{2,1,0:T(8,128)(2,1)S(1)}, bf16[2,112,256]{2,1,0:T(8,128)(2,1)S(1)}) custom-call(s32[39]{0:T(128)S(1)} %fusion.2.refs_5_.places, bf16[2,448,4096]{2,1,0:T(8,128)(2,1)S(1)} %shard_map.76.refs_0_, ...), custom_call_target="tpu_custom_call" | custom-call | flops 469762048 | bytes 2359296 | tf_op jit(solution)/shard_map/pallas_call | solution.py:162
  48.6 1.2 %collective-permute-start.14 = (bf16[2,112,256]{2,1,0:T(8,128)(2,1)S(1)}, bf16[2,112,256]{2,1,0:T(8,128)(2,1)S(1)}, u32[]{:S(2)}, u32[]{:S(2)}) collective-permute-start(bf16[2,112,256]{2,1,0:T(8,128)(2,1)S(1)} %get-tuple-element.37), channel_id=1, source_target_pairs={{0,32},{1,33},{2,34},{3,35},{4,36},{5,37},{6,38},{7,39},{8,40},{9,... | collective-permute-start | bytes 344072 | tf_op jit(solution)/shard_map/ppermute | solution.py:36
  49.9 1.5 %collective-permute-start.15 = (bf16[2,112,256]{2,1,0:T(8,128)(2,1)S(1)}, bf16[2,112,256]{2,1,0:T(8,128)(2,1)S(1)}, u32[]{:S(2)}, u32[]{:S(2)}) collective-permute-start(bf16[2,112,256]{2,1,0:T(8,128)(2,1)S(1)} %get-tuple-element.38), channel_id=1, source_target_pairs={{0,96},{1,97},{2,98},{3,99},{4,100},{5,101},{6,102},{7,103},{8,104... | collective-permute-start | bytes 344072 | tf_op jit(solution)/shard_map/ppermute | solution.py:36
  51.5 1.6 %collective-permute-start.16 = (bf16[2,112,256]{2,1,0:T(8,128)(2,1)S(1)}, bf16[2,112,256]{2,1,0:T(8,128)(2,1)S(1)}, u32[]{:S(2)}, u32[]{:S(2)}) collective-permute-start(bf16[2,112,256]{2,1,0:T(8,128)(2,1)S(1)} %get-tuple-element.39), channel_id=1, source_target_pairs={{0,64},{1,65},{2,66},{3,67},{4,68},{5,69},{6,70},{7,71},{8,72},{9,... | collective-permute-start | bytes 344072 | tf_op jit(solution)/shard_map/ppermute | solution.py:36
  53.2 1.3 %collective-permute-start.22 = (bf16[4,256,512]{2,1,0:T(8,128)(2,1)S(1)}, bf16[4,256,512]{2,1,0:T(8,128)(2,1)S(1)}, u32[]{:S(2)}, u32[]{:S(2)}) collective-permute-start(bf16[4,256,512]{2,1,0:T(8,128)(2,1)S(1)} %shard_map.88), channel_id=1, source_target_pairs={{0,16},{1,17},{2,18},{3,19},{4,20},{5,21},{6,22},{7,23},{8,24},{9,... | collective-permute-start | bytes 3145736 | tf_op jit(solution)/shard_map/ppermute | solution.py:36
  54.6 3.4 %collective-permute-start.10 = (bf16[112,256]{1,0:T(8,128)(2,1)S(1)}, bf16[112,256]{1,0:T(8,128)(2,1)S(1)}, u32[]{:S(2)}, u32[]{:S(2)}) collective-permute-start(bf16[112,256]{1,0:T(8,128)(2,1)S(1)} %fusion), channel_id=1, source_target_pairs={{0,128},{1,129},{2,130},{3,131},{4,132},{5,133},{6,134},{7,135},{8... | collective-permute-start | bytes 172040 | tf_op jit(solution)/shard_map/ppermute | solution.py:36
  58.0 2.3 %collective-permute-start.17 = (bf16[112,256]{1,0:T(8,128)(2,1)S(1)}, bf16[112,256]{1,0:T(8,128)(2,1)S(1)}, u32[]{:S(2)}, u32[]{:S(2)}) collective-permute-start(bf16[112,256]{1,0:T(8,128)(2,1)S(1)} %fusion.1), channel_id=1, source_target_pairs={{0,128},{1,129},{2,130},{3,131},{4,132},{5,133},{6,134},{7,135},{8... | collective-permute-start | bytes 172040 | tf_op jit(solution)/shard_map/ppermute | solution.py:36
  60.3 1.8 %collective-permute-done.10 = bf16[112,256]{1,0:T(8,128)(2,1)S(1)} collective-permute-done((bf16[112,256]{1,0:T(8,128)(2,1)S(1)}, bf16[112,256]{1,0:T(8,128)(2,1)S(1)}, u32[]{:S(2)}, u32[]{:S(2)}) %collective-permute-start.10) | collective-permute-done | bytes 57376 | tf_op jit(solution)/shard_map/ppermute | solution.py:36
  62.1 3.0 %collective-permute-done.17 = bf16[112,256]{1,0:T(8,128)(2,1)S(1)} collective-permute-done((bf16[112,256]{1,0:T(8,128)(2,1)S(1)}, bf16[112,256]{1,0:T(8,128)(2,1)S(1)}, u32[]{:S(2)}, u32[]{:S(2)}) %collective-permute-start.17) | collective-permute-done | bytes 57376 | tf_op jit(solution)/shard_map/ppermute | solution.py:36
  65.1 0.6 shard_map.86
  65.7 3.5 %collective-permute-start.18 = (f32[56,512]{1,0:T(8,128)S(1)}, f32[56,512]{1,0:T(8,128)S(1)}, u32[]{:S(2)}, u32[]{:S(2)}) collective-permute-start(f32[56,512]{1,0:T(8,128)S(1)} %get-tuple-element.41), channel_id=1, source_target_pairs={{0,16},{1,17},{2,18},{3,19},{4,20},{5,21},{6,22},{7,23},{8,24},{9,... | collective-permute-start | bytes 344072 | tf_op jit(solution)/shard_map/ppermute | solution.py:36
  69.3 0.9 collective-permute-done.18.other
  70.2 1.4 %shard_map.87 = (f32[1,56,1024]{2,1,0:T(8,128)}, f32[1,56,1024]{2,1,0:T(8,128)}, bf16[56,1024]{1,0:T(8,128)(2,1)S(1)}) custom-call(s32[39]{0:T(128)S(1)} %fusion.2.refs_5_.places, f32[56,512]{1,0:T(8,128)S(1)} %get-tuple-element.40.mine, f32[56,512]{1,0:T(8,128)S(1)} %collective-permute-done.18.other, f32[1,56,1024]{2,1,0:T(8,128)S(1)} %copy-done.1, ...), custom_call_target="tpu_custom_call" | custom-call | tf_op jit(solution)/shard_map/pallas_call | solution.py:336
  71.6 2.2 %collective-permute-start.21 = (bf16[56,1024]{1,0:T(8,128)(2,1)S(1)}, bf16[56,1024]{1,0:T(8,128)(2,1)S(1)}, u32[]{:S(2)}, u32[]{:S(2)}) collective-permute-start(bf16[56,1024]{1,0:T(8,128)(2,1)S(1)} %get-tuple-element.42), channel_id=1, source_target_pairs={{0,2},{1,3},{2,0},{3,1},{4,6},{5,7},{6,4},{7,5},{8,10},{9,11},{10,... | collective-permute-start | bytes 344072 | tf_op jit(solution)/shard_map/ppermute | solution.py:36
  73.8 1.1 %collective-permute-start.20 = (bf16[56,1024]{1,0:T(8,128)(2,1)S(1)}, bf16[56,1024]{1,0:T(8,128)(2,1)S(1)}, u32[]{:S(2)}, u32[]{:S(2)}) collective-permute-start(bf16[56,1024]{1,0:T(8,128)(2,1)S(1)} %get-tuple-element.42), channel_id=1, source_target_pairs={{0,1},{1,2},{2,3},{3,0},{4,5},{5,6},{6,7},{7,4},{8,9},{9,10},{10,1... | collective-permute-start | bytes 344072 | tf_op jit(solution)/shard_map/ppermute | solution.py:36
  74.9 1.6 %collective-permute-start.19 = (bf16[56,1024]{1,0:T(8,128)(2,1)S(1)}, bf16[56,1024]{1,0:T(8,128)(2,1)S(1)}, u32[]{:S(2)}, u32[]{:S(2)}) collective-permute-start(bf16[56,1024]{1,0:T(8,128)(2,1)S(1)} %get-tuple-element.42), channel_id=1, source_target_pairs={{0,3},{1,0},{2,1},{3,2},{4,7},{5,4},{6,5},{7,6},{8,11},{9,8},{10,9... | collective-permute-start | bytes 344072 | tf_op jit(solution)/shard_map/ppermute | solution.py:36
  76.8 2.2 %collective-permute-done.20 = bf16[56,1024]{1,0:T(8,128)(2,1)S(1)} collective-permute-done((bf16[56,1024]{1,0:T(8,128)(2,1)S(1)}, bf16[56,1024]{1,0:T(8,128)(2,1)S(1)}, u32[]{:S(2)}, u32[]{:S(2)}) %collective-permute-start.20) | collective-permute-done | bytes 114720 | tf_op jit(solution)/shard_map/ppermute | solution.py:36
  80.2 1.2 %collective-permute-start.23 = (bf16[224,256]{1,0:T(8,128)(2,1)S(1)}, bf16[224,256]{1,0:T(8,128)(2,1)S(1)}, u32[]{:S(2)}, u32[]{:S(2)}) collective-permute-start(bf16[224,256]{1,0:T(8,128)(2,1)S(1)} %convolution_convert_fusion.2), channel_id=1, source_target_pairs={{0,4},{1,5},{2,6},{3,7},{4,8},{5,9},{6,10},{7,11},{8,12},{9,13},{1... | collective-permute-start | bytes 344072 | tf_op jit(solution)/shard_map/ppermute | solution.py:36
  81.4 3.3 %collective-permute-start.24 = (bf16[224,256]{1,0:T(8,128)(2,1)S(1)}, bf16[224,256]{1,0:T(8,128)(2,1)S(1)}, u32[]{:S(2)}, u32[]{:S(2)}) collective-permute-start(bf16[224,256]{1,0:T(8,128)(2,1)S(1)} %convolution_convert_fusion.1), channel_id=1, source_target_pairs={{0,12},{1,13},{2,14},{3,15},{4,0},{5,1},{6,2},{7,3},{8,4},{9,5},{1... | collective-permute-start | bytes 344072 | tf_op jit(solution)/shard_map/ppermute | solution.py:36
  85.2 1.6 %collective-permute-done.23 = bf16[224,256]{1,0:T(8,128)(2,1)S(1)} collective-permute-done((bf16[224,256]{1,0:T(8,128)(2,1)S(1)}, bf16[224,256]{1,0:T(8,128)(2,1)S(1)}, u32[]{:S(2)}, u32[]{:S(2)}) %collective-permute-start.23) | collective-permute-done | bytes 114720 | tf_op jit(solution)/shard_map/ppermute | solution.py:36
  86.8 3.9 %collective-permute-done.25 = bf16[224,256]{1,0:T(8,128)(2,1)S(1)} collective-permute-done((bf16[224,256]{1,0:T(8,128)(2,1)S(1)}, bf16[224,256]{1,0:T(8,128)(2,1)S(1)}, u32[]{:S(2)}, u32[]{:S(2)}) %collective-permute-start.25) | collective-permute-done | bytes 114720 | tf_op jit(solution)/shard_map/ppermute | solution.py:36
  90.7 1.3 %shard_map.89 = bf16[16,56,256]{2,1,0:T(8,128)(2,1)} custom-call(s32[39]{0:T(128)S(1)} %fusion.2.refs_5_.places, bf16[4,56,256]{2,1,0:T(8,128)(2,1)S(1)} %bitcast.47, bf16[4,56,256]{2,1,0:T(8,128)(2,1)S(1)} %bitcast.44, bf16[4,56,256]{2,1,0:T(8,128)(2,1)S(1)} %bitcast.45, bf16[4,56,256]{2,1,0:T(8,128)(2,1)S(1)} %bitcast.46), custom_call_target="tpu_custom_call" | custom-call | tf_op jit(solution)/shard_map/pallas_call | solution.py:359
  (43 shorter events, 2.5 us)
Async XLA Ops:
  0.6 18.5 %collective-permute-start = (bf16[2,448,4096]{2,1,0:T(8,128)(2,1)}, bf16[2,448,4096]{2,1,0:T(8,128)(2,1)}, u32[]{:S(2)}, u32[]{:S(2)}) collective-permute-start(bf16[2,448,4096]{2,1,0:T(8,128)(2,1)} %bitcast.41), channel_id=1, source_target_pairs={{0,16},{1,17},{2,18},{3,19},{4,20},{5,21},{6,22},{7,23},{8,24},{9,... | collective-permute-start | bytes 22020104 | tf_op jit(solution)/shard_map/ppermute | solution.py:36
  5.0 9.3 %collective-permute-start.3 = (bf16[2,256,256]{2,1,0:T(8,128)(2,1)S(1)}, bf16[2,256,256]{2,1,0:T(8,128)(2,1)S(1)}, u32[]{:S(2)}, u32[]{:S(2)}) collective-permute-start(bf16[2,256,256]{2,1,0:T(8,128)(2,1)S(1)} %pad_maximum_fusion.1.refs_0_), channel_id=1, source_target_pairs={{0,8},{1,9},{2,10},{3,11},{4,12},{5,13},{6,14},{7,15},{8,0},{9,1},... | collective-permute-start | bytes 786440 | tf_op jit(solution)/shard_map/ppermute | solution.py:36
  9.3 6.4 %collective-permute-start.2 = (bf16[2,256,256]{2,1,0:T(8,128)(2,1)S(1)}, bf16[2,256,256]{2,1,0:T(8,128)(2,1)S(1)}, u32[]{:S(2)}, u32[]{:S(2)}) collective-permute-start(bf16[2,256,256]{2,1,0:T(8,128)(2,1)S(1)} %pad_maximum_fusion.1.refs_0_), channel_id=1, source_target_pairs={{0,4},{1,5},{2,6},{3,7},{4,8},{5,9},{6,10},{7,11},{8,12},{9,13},{1... | collective-permute-start | bytes 786440 | tf_op jit(solution)/shard_map/ppermute | solution.py:36
  10.1 9.1 %collective-permute-start.1 = (bf16[2,256,256]{2,1,0:T(8,128)(2,1)S(1)}, bf16[2,256,256]{2,1,0:T(8,128)(2,1)S(1)}, u32[]{:S(2)}, u32[]{:S(2)}) collective-permute-start(bf16[2,256,256]{2,1,0:T(8,128)(2,1)S(1)} %pad_maximum_fusion.1.refs_0_), channel_id=1, source_target_pairs={{0,12},{1,13},{2,14},{3,15},{4,0},{5,1},{6,2},{7,3},{8,4},{9,5},{1... | collective-permute-start | bytes 786440 | tf_op jit(solution)/shard_map/ppermute | solution.py:36
  19.2 3.1 %copy-start = (bf16[1,16,56,4096]{3,2,1,0:T(8,128)(2,1)S(1)}, bf16[1,16,56,4096]{3,2,1,0:T(8,128)(2,1)}, u32[]{:S(2)}) copy-start(bf16[1,16,56,4096]{3,2,1,0:T(8,128)(2,1)} %param.5) | copy-start | bytes 22020100
  19.8 11.5 %collective-permute-start.4 = (bf16[4,256,256]{2,1,0:T(8,128)(2,1)S(1)}, bf16[4,256,256]{2,1,0:T(8,128)(2,1)S(1)}, u32[]{:S(2)}, u32[]{:S(2)}) collective-permute-start(bf16[4,256,256]{2,1,0:T(8,128)(2,1)S(1)} %get-tuple-element.24.refs_1_.refs_0_), channel_id=1, source_target_pairs={{0,131},{1,0},{2,1},{3,2},{4,135},{5,4},{6,5},{7,6},{8,139},{9,8},... | collective-permute-start | bytes 1572872 | tf_op jit(solution)/shard_map/ppermute | solution.py:36
  21.5 13.3 %collective-permute-start.11 = (bf16[4,256,256]{2,1,0:T(8,128)(2,1)S(1)}, bf16[4,256,256]{2,1,0:T(8,128)(2,1)S(1)}, u32[]{:S(2)}, u32[]{:S(2)}) collective-permute-start(bf16[4,256,256]{2,1,0:T(8,128)(2,1)S(1)} %get-tuple-element.26.refs_1_.refs_4_), channel_id=1, source_target_pairs={{0,1},{1,2},{2,3},{3,128},{4,5},{5,6},{6,7},{7,132},{8,9},{9,10},{... | collective-permute-start | bytes 1572872 | tf_op jit(solution)/shard_map/ppermute | solution.py:36
  21.5 14.9 %collective-permute-start.6 = (bf16[4,256,256]{2,1,0:T(8,128)(2,1)S(1)}, bf16[4,256,256]{2,1,0:T(8,128)(2,1)S(1)}, u32[]{:S(2)}, u32[]{:S(2)}) collective-permute-start(bf16[4,256,256]{2,1,0:T(8,128)(2,1)S(1)} %get-tuple-element.24.refs_1_.refs_0_), channel_id=1, source_target_pairs={{0,1},{1,2},{2,3},{3,128},{4,5},{5,6},{6,7},{7,132},{8,9},{9,10},{... | collective-permute-start | bytes 1572872 | tf_op jit(solution)/shard_map/ppermute | solution.py:36
  31.3 8.4 %collective-permute-start.5 = (bf16[4,256,256]{2,1,0:T(8,128)(2,1)S(1)}, bf16[4,256,256]{2,1,0:T(8,128)(2,1)S(1)}, u32[]{:S(2)}, u32[]{:S(2)}) collective-permute-start(bf16[4,256,256]{2,1,0:T(8,128)(2,1)S(1)} %shard_map.80.refs_1_), channel_id=1, source_target_pairs={{0,131},{1,0},{2,1},{3,2},{4,135},{5,4},{6,5},{7,6},{8,139},{9,8},... | collective-permute-start | bytes 1572872 | tf_op jit(solution)/shard_map/ppermute | solution.py:36
  33.3 11.9 %collective-permute-start.13 = (bf16[4,256,256]{2,1,0:T(8,128)(2,1)S(1)}, bf16[4,256,256]{2,1,0:T(8,128)(2,1)S(1)}, u32[]{:S(2)}, u32[]{:S(2)}) collective-permute-start(bf16[4,256,256]{2,1,0:T(8,128)(2,1)S(1)} %get-tuple-element.26.refs_1_.refs_4_), channel_id=1, source_target_pairs={{0,131},{1,0},{2,1},{3,2},{4,135},{5,4},{6,5},{7,6},{8,139},{9,8},... | collective-permute-start | bytes 1572872 | tf_op jit(solution)/shard_map/ppermute | solution.py:36
  34.7 12.7 %collective-permute-start.12 = (bf16[4,256,256]{2,1,0:T(8,128)(2,1)S(1)}, bf16[4,256,256]{2,1,0:T(8,128)(2,1)S(1)}, u32[]{:S(2)}, u32[]{:S(2)}) collective-permute-start(bf16[4,256,256]{2,1,0:T(8,128)(2,1)S(1)} %shard_map.83.refs_2_.refs_6_), channel_id=1, source_target_pairs={{0,1},{1,2},{2,3},{3,128},{4,5},{5,6},{6,7},{7,132},{8,9},{9,10},{... | collective-permute-start | bytes 1572872 | tf_op jit(solution)/shard_map/ppermute | solution.py:36
  40.9 10.6 %collective-permute-start.7 = (bf16[2,112,256]{2,1,0:T(8,128)(2,1)S(1)}, bf16[2,112,256]{2,1,0:T(8,128)(2,1)S(1)}, u32[]{:S(2)}, u32[]{:S(2)}) collective-permute-start(bf16[2,112,256]{2,1,0:T(8,128)(2,1)S(1)} %get-tuple-element.31), channel_id=1, source_target_pairs={{0,32},{1,33},{2,34},{3,35},{4,36},{5,37},{6,38},{7,39},{8,40},{9,... | collective-permute-start | bytes 344072 | tf_op jit(solution)/shard_map/ppermute | solution.py:36
  42.0 11.2 %collective-permute-start.8 = (bf16[2,112,256]{2,1,0:T(8,128)(2,1)S(1)}, bf16[2,112,256]{2,1,0:T(8,128)(2,1)S(1)}, u32[]{:S(2)}, u32[]{:S(2)}) collective-permute-start(bf16[2,112,256]{2,1,0:T(8,128)(2,1)S(1)} %get-tuple-element.32), channel_id=1, source_target_pairs={{0,96},{1,97},{2,98},{3,99},{4,100},{5,101},{6,102},{7,103},{8,104... | collective-permute-start | bytes 344072 | tf_op jit(solution)/shard_map/ppermute | solution.py:36
  43.7 10.8 %collective-permute-start.9 = (bf16[2,112,256]{2,1,0:T(8,128)(2,1)S(1)}, bf16[2,112,256]{2,1,0:T(8,128)(2,1)S(1)}, u32[]{:S(2)}, u32[]{:S(2)}) collective-permute-start(bf16[2,112,256]{2,1,0:T(8,128)(2,1)S(1)} %get-tuple-element.33), channel_id=1, source_target_pairs={{0,64},{1,65},{2,66},{3,67},{4,68},{5,69},{6,70},{7,71},{8,72},{9,... | collective-permute-start | bytes 344072 | tf_op jit(solution)/shard_map/ppermute | solution.py:36
  48.6 9.3 %collective-permute-start.14 = (bf16[2,112,256]{2,1,0:T(8,128)(2,1)S(1)}, bf16[2,112,256]{2,1,0:T(8,128)(2,1)S(1)}, u32[]{:S(2)}, u32[]{:S(2)}) collective-permute-start(bf16[2,112,256]{2,1,0:T(8,128)(2,1)S(1)} %get-tuple-element.37), channel_id=1, source_target_pairs={{0,32},{1,33},{2,34},{3,35},{4,36},{5,37},{6,38},{7,39},{8,40},{9,... | collective-permute-start | bytes 344072 | tf_op jit(solution)/shard_map/ppermute | solution.py:36
  49.9 8.1 %collective-permute-start.15 = (bf16[2,112,256]{2,1,0:T(8,128)(2,1)S(1)}, bf16[2,112,256]{2,1,0:T(8,128)(2,1)S(1)}, u32[]{:S(2)}, u32[]{:S(2)}) collective-permute-start(bf16[2,112,256]{2,1,0:T(8,128)(2,1)S(1)} %get-tuple-element.38), channel_id=1, source_target_pairs={{0,96},{1,97},{2,98},{3,99},{4,100},{5,101},{6,102},{7,103},{8,104... | collective-permute-start | bytes 344072 | tf_op jit(solution)/shard_map/ppermute | solution.py:36
  51.5 18.7 %copy-start.1 = (f32[1,56,1024]{2,1,0:T(8,128)S(1)}, f32[1,56,1024]{2,1,0:T(8,128)}, u32[]{:S(2)}) copy-start(f32[1,56,1024]{2,1,0:T(8,128)} %first.1) | copy-start | bytes 688132
  51.5 18.7 %copy-start.2 = (f32[1,56,1024]{2,1,0:T(8,128)S(1)}, f32[1,56,1024]{2,1,0:T(8,128)}, u32[]{:S(2)}) copy-start(f32[1,56,1024]{2,1,0:T(8,128)} %second.1) | copy-start | bytes 688132
  51.5 6.4 %collective-permute-start.16 = (bf16[2,112,256]{2,1,0:T(8,128)(2,1)S(1)}, bf16[2,112,256]{2,1,0:T(8,128)(2,1)S(1)}, u32[]{:S(2)}, u32[]{:S(2)}) collective-permute-start(bf16[2,112,256]{2,1,0:T(8,128)(2,1)S(1)} %get-tuple-element.39), channel_id=1, source_target_pairs={{0,64},{1,65},{2,66},{3,67},{4,68},{5,69},{6,70},{7,71},{8,72},{9,... | collective-permute-start | bytes 344072 | tf_op jit(solution)/shard_map/ppermute | solution.py:36
  53.2 25.9 %collective-permute-start.22 = (bf16[4,256,512]{2,1,0:T(8,128)(2,1)S(1)}, bf16[4,256,512]{2,1,0:T(8,128)(2,1)S(1)}, u32[]{:S(2)}, u32[]{:S(2)}) collective-permute-start(bf16[4,256,512]{2,1,0:T(8,128)(2,1)S(1)} %shard_map.88), channel_id=1, source_target_pairs={{0,16},{1,17},{2,18},{3,19},{4,20},{5,21},{6,22},{7,23},{8,24},{9,... | collective-permute-start | bytes 3145736 | tf_op jit(solution)/shard_map/ppermute | solution.py:36
  54.6 7.5 %collective-permute-start.10 = (bf16[112,256]{1,0:T(8,128)(2,1)S(1)}, bf16[112,256]{1,0:T(8,128)(2,1)S(1)}, u32[]{:S(2)}, u32[]{:S(2)}) collective-permute-start(bf16[112,256]{1,0:T(8,128)(2,1)S(1)} %fusion), channel_id=1, source_target_pairs={{0,128},{1,129},{2,130},{3,131},{4,132},{5,133},{6,134},{7,135},{8... | collective-permute-start | bytes 172040 | tf_op jit(solution)/shard_map/ppermute | solution.py:36
  58.0 7.1 %collective-permute-start.17 = (bf16[112,256]{1,0:T(8,128)(2,1)S(1)}, bf16[112,256]{1,0:T(8,128)(2,1)S(1)}, u32[]{:S(2)}, u32[]{:S(2)}) collective-permute-start(bf16[112,256]{1,0:T(8,128)(2,1)S(1)} %fusion.1), channel_id=1, source_target_pairs={{0,128},{1,129},{2,130},{3,131},{4,132},{5,133},{6,134},{7,135},{8... | collective-permute-start | bytes 172040 | tf_op jit(solution)/shard_map/ppermute | solution.py:36
  65.7 4.5 %collective-permute-start.18 = (f32[56,512]{1,0:T(8,128)S(1)}, f32[56,512]{1,0:T(8,128)S(1)}, u32[]{:S(2)}, u32[]{:S(2)}) collective-permute-start(f32[56,512]{1,0:T(8,128)S(1)} %get-tuple-element.41), channel_id=1, source_target_pairs={{0,16},{1,17},{2,18},{3,19},{4,20},{5,21},{6,22},{7,23},{8,24},{9,... | collective-permute-start | bytes 344072 | tf_op jit(solution)/shard_map/ppermute | solution.py:36
  71.6 5.1 %collective-permute-start.21 = (bf16[56,1024]{1,0:T(8,128)(2,1)S(1)}, bf16[56,1024]{1,0:T(8,128)(2,1)S(1)}, u32[]{:S(2)}, u32[]{:S(2)}) collective-permute-start(bf16[56,1024]{1,0:T(8,128)(2,1)S(1)} %get-tuple-element.42), channel_id=1, source_target_pairs={{0,2},{1,3},{2,0},{3,1},{4,6},{5,7},{6,4},{7,5},{8,10},{9,11},{10,... | collective-permute-start | bytes 344072 | tf_op jit(solution)/shard_map/ppermute | solution.py:36
  73.8 5.1 %collective-permute-start.20 = (bf16[56,1024]{1,0:T(8,128)(2,1)S(1)}, bf16[56,1024]{1,0:T(8,128)(2,1)S(1)}, u32[]{:S(2)}, u32[]{:S(2)}) collective-permute-start(bf16[56,1024]{1,0:T(8,128)(2,1)S(1)} %get-tuple-element.42), channel_id=1, source_target_pairs={{0,1},{1,2},{2,3},{3,0},{4,5},{5,6},{6,7},{7,4},{8,9},{9,10},{10,1... | collective-permute-start | bytes 344072 | tf_op jit(solution)/shard_map/ppermute | solution.py:36
  74.9 4.1 %collective-permute-start.19 = (bf16[56,1024]{1,0:T(8,128)(2,1)S(1)}, bf16[56,1024]{1,0:T(8,128)(2,1)S(1)}, u32[]{:S(2)}, u32[]{:S(2)}) collective-permute-start(bf16[56,1024]{1,0:T(8,128)(2,1)S(1)} %get-tuple-element.42), channel_id=1, source_target_pairs={{0,3},{1,0},{2,1},{3,2},{4,7},{5,4},{6,5},{7,6},{8,11},{9,8},{10,9... | collective-permute-start | bytes 344072 | tf_op jit(solution)/shard_map/ppermute | solution.py:36
  80.2 6.6 %collective-permute-start.23 = (bf16[224,256]{1,0:T(8,128)(2,1)S(1)}, bf16[224,256]{1,0:T(8,128)(2,1)S(1)}, u32[]{:S(2)}, u32[]{:S(2)}) collective-permute-start(bf16[224,256]{1,0:T(8,128)(2,1)S(1)} %convolution_convert_fusion.2), channel_id=1, source_target_pairs={{0,4},{1,5},{2,6},{3,7},{4,8},{5,9},{6,10},{7,11},{8,12},{9,13},{1... | collective-permute-start | bytes 344072 | tf_op jit(solution)/shard_map/ppermute | solution.py:36
  81.4 5.5 %collective-permute-start.24 = (bf16[224,256]{1,0:T(8,128)(2,1)S(1)}, bf16[224,256]{1,0:T(8,128)(2,1)S(1)}, u32[]{:S(2)}, u32[]{:S(2)}) collective-permute-start(bf16[224,256]{1,0:T(8,128)(2,1)S(1)} %convolution_convert_fusion.1), channel_id=1, source_target_pairs={{0,12},{1,13},{2,14},{3,15},{4,0},{5,1},{6,2},{7,3},{8,4},{9,5},{1... | collective-permute-start | bytes 344072 | tf_op jit(solution)/shard_map/ppermute | solution.py:36
  84.6 6.1 %collective-permute-start.25 = (bf16[224,256]{1,0:T(8,128)(2,1)S(1)}, bf16[224,256]{1,0:T(8,128)(2,1)S(1)}, u32[]{:S(2)}, u32[]{:S(2)}) collective-permute-start(bf16[224,256]{1,0:T(8,128)(2,1)S(1)} %convolution_convert_fusion), channel_id=1, source_target_pairs={{0,8},{1,9},{2,10},{3,11},{4,12},{5,13},{6,14},{7,15},{8,0},{9,1},... | collective-permute-start | bytes 344072 | tf_op jit(solution)/shard_map/ppermute | solution.py:36

commit v3 on v2

--- a/solution.py
+++ b/solution.py
@@ -50,6 +50,10 @@
         return (z // ZL, y, c, x, z % ZL)
 
     return place
+
+
+def two_along_ring(zh, y, c, x, zl):
+    return along_ring(2 if zl % 2 else -2)(zh, y, c, x, zl)
 
 
 def along_line(step):
@@ -103,10 +107,10 @@
     )
 
 
-def project_kernel(outers, last, has_acc, places, *refs):
+def project_kernel(outers, last, has_acc, after, places, *refs):
     grad, rest = refs[0], refs[1:]
     outs = rest[-(Y if last else 2) :]
-    rest = rest[: -len(outs)]
+    rest = rest[: len(rest) - len(outs) - after]
     if has_acc:
         acc, rest = rest[-1], rest[:-1]
     pieces = [
@@ -141,12 +145,12 @@
         outs[1][...] = value[0, : outs[1].shape[0], : outs[1].shape[1]]
 
 
-def project(places, outers, grad, rights, acc, last):
+def project(places, outers, grad, rights, acc, last, after=()):
     depth, width = rights[0].shape[1:]
     half_rows = grad.shape[1]
     count = sum(right.shape[0] for right in rights)
     whole = pl.BlockSpec(memory_space=pltpu.VMEM)
-    operands = [grad, *rights] + ([] if acc is None else [acc])
+    operands = [grad, *rights] + ([] if acc is None else [acc]) + list(after)
     if last:
         shapes = [
             jax.ShapeDtypeStruct(
@@ -160,7 +164,9 @@
             jax.ShapeDtypeStruct((8, 128), jnp.float32),
         ]
     return pl.pallas_call(
-        functools.partial(project_kernel, outers, last, acc is not None),
+        functools.partial(
+            project_kernel, outers, last, acc is not None, len(after)
+        ),
         out_shape=shapes,
         in_specs=[pl.BlockSpec(memory_space=pltpu.SMEM)] + [whole] * len(operands),
         out_specs=[whole] * len(shapes),
@@ -195,33 +201,29 @@
 
 
 def add_kernel(first, second, out, slots, sems):
-    band = slots.shape[2]
+    band = slots.shape[1]
     per_half = out.shape[1] // band
     count = out.shape[0] * per_half
-
-    def copies(n):
+    depth = slots.shape[0]
+
+    def copy(n):
         at = (n // per_half, pl.ds((n % per_half) * band, band))
-        return [
-            pltpu.make_async_copy(
-                ref.at[at], slots.at[side, n % 2], sems.at[side, n % 2]
-            )
-            for side, ref in enumerate((first, second))
-        ]
-
-    for copy in copies(0):
-        copy.start()
+        return pltpu.make_async_copy(
+            second.at[at], slots.at[n % depth], sems.at[n % depth]
+        )
+
+    for n in range(depth - 1):
+        copy(n).start()
     for n in range(count):
-        if n + 1 < count:
-            for copy in copies(n + 1):
-                copy.start()
-        for copy in copies(n):
-            copy.wait()
-        row = (n % per_half) * band
+        if n + depth - 1 < count:
+            copy(n + depth - 1).start()
+        copy(n).wait()
+        half, row = n // per_half, (n % per_half) * band
 
         def rows_on(i, carry):
             at = pl.ds(pl.multiple_of(i * 16, 16), 16)
             into = pl.ds(pl.multiple_of(row + i * 16, 16), 16)
-            out[n // per_half, into, :] = slots[0, n % 2, at] + slots[1, n % 2, at]
+            out[half, into, :] = first[half, into, :] + slots[n % depth, at]
             return carry
 
         lax.fori_loop(0, band // 16, rows_on, 0)
@@ -230,17 +232,17 @@
 def add(first, second):
     halves, rows, width = first.shape
     band = rows // 4
-    anywhere = pl.BlockSpec(memory_space=pltpu.HBM)
+    whole = pl.BlockSpec(memory_space=pltpu.VMEM)
     return pl.pallas_call(
         add_kernel,
         out_shape=jax.ShapeDtypeStruct(first.shape, first.dtype),
-        in_specs=[anywhere, anywhere],
-        out_specs=pl.BlockSpec(memory_space=pltpu.VMEM),
+        in_specs=[whole, pl.BlockSpec(memory_space=pltpu.HBM)],
+        out_specs=whole,
         scratch_shapes=[
-            pltpu.VMEM((2, 2, band, width), first.dtype),
-            pltpu.SemaphoreType.DMA((2, 2)),
+            pltpu.VMEM((3, band, width), first.dtype),
+            pltpu.SemaphoreType.DMA((3,)),
         ],
-        compiler_params=pltpu.CompilerParams(vmem_limit_bytes=13 * 1024 * 1024),
+        compiler_params=pltpu.CompilerParams(vmem_limit_bytes=19 * 1024 * 1024),
         cost_estimate=pl.CostEstimate(
             flops=halves * rows * width,
             bytes_accessed=6 * halves * rows * width,
@@ -261,27 +263,28 @@
     )(value, *after)
 
 
-def collect_kernel(*refs):
-    ins, out = refs[:-1], refs[-1]
-    pieces, _, width = out.shape
+def collect_kernel(pieces, groups, *refs):
+    ins, out = refs[: pieces * groups], refs[-1]
     part = ins[0].shape[2]
     for n, ref in enumerate(ins):
         group, piece = n // pieces, n % pieces
         out[piece, :, group * part : (group + 1) * part] = ref[0]
 
 
-def collect(groups):
+def collect(groups, *after):
     arrays = [array for group in groups for array in group]
     _, depth, part = arrays[0].shape
     pieces, width = len(groups[0]), part * len(groups)
-    return pl.pallas_call(
-        collect_kernel,
+    first = pl.BlockSpec((1, depth, part), lambda i: (0, 0, 0))
+    one = [pl.BlockSpec((8, 128), lambda i: (0, 0))] * len(after)
+    return pl.pallas_call(
+        functools.partial(collect_kernel, pieces, len(groups)),
         grid=(1,),
         out_shape=jax.ShapeDtypeStruct((pieces, depth, width), arrays[0].dtype),
-        in_specs=[pl.BlockSpec((1, depth, part), lambda i: (0, 0, 0))] * len(arrays),
+        in_specs=[first] * len(arrays) + one,
         out_specs=pl.BlockSpec((pieces, depth, width), lambda i: (0, 0, 0)),
         compiler_params=pltpu.CompilerParams(vmem_limit_bytes=5 * 1024 * 1024),
-    )(*arrays)
+    )(*arrays, *after)
 
 
 def split_kernel(groups, places, *refs):
@@ -387,8 +390,11 @@
     own_half = jnp.stack(
         [own_half[:, g * part : (g + 1) * part] for g in range(GROUPS)]
     )
-    near = [own_half] + [
-        move(own_half, by_core(along_x(-o), along_ring(-o))) for o in OFFSETS[1:]
+    near = [
+        own_half,
+        move(own_half, by_core(along_x(-1), along_ring(-1))),
+        move(own_half, by_core(along_x(1), along_ring(1))),
+        move(own_half, by_core(along_x(2), two_along_ring)),
     ]
 
     reduced = []
@@ -404,11 +410,14 @@
         move(ahead[0], by_core(along_ring(-1), along_x(-1))),
         move(behind[1], by_core(along_ring(1), along_x(1))),
     ]
-    for group in range(GROUPS):
-        acc, _ = project(
-            places, (1, -1), both, [ahead[group], behind[group]], accs[group], False
-        )
-        sums = project(places, (2,), both, [far[group]], acc, True)
+    near_two = [ahead[0], behind[0]]
+    acc0, _ = project(places, (1, -1), both, near_two, accs[0], False)
+    acc1, token = project(places, (-1,), both, [behind[1]], accs[1], False)
+    sums0 = project(places, (2,), both, [far[0]], acc0, True, (token,))
+    sums1 = project(
+        places, (1, 2), both, [ahead[1], far[1]], acc1, True, (sums0[1],)
+    )
+    for sums in (sums0, sums1):
         total = sums[0]
         for dy in range(1, Y):
             got = move(sums[dy], along_y(OFFSETS[dy]))
@@ -420,7 +429,9 @@
     new_first, new_second, direction = adam(
         places, mine, other, first_moment, second_moment
     )
-    basis_other = move(collect(list(zip(stacks, ahead, behind, far))), other_core)
+    basis_other = move(
+        collect(list(zip(stacks, ahead, behind, far))), other_core
+    )
     basis = jnp.concatenate([*stacks, basis_other], axis=2)
     gathered = jnp.stack(
         [direction]

time: 92.3 us -> 87.7 us (0.950)
  waiting for transfers between devices: 22.9 us -> 17.4 us
  starting transfers between devices: 44.4 us -> 48.5 us
  Pallas kernels: 19.9 us -> 17.1 us
    ppermute x26, waiting for transfers between devices: 22.9 us -> 17.4 us  [move(): return lax.ppermute(value, AXES, pairs)]
    ppermute x26, starting transfers between devices: 44.4 us -> 48.5 us  [move(): return lax.ppermute(value, AXES, pairs)]
    pallas_call x1, Pallas kernels: 6.64 us -> 4.37 us  [add(): pl.pallas_call(add_kernel, out_shape=jax.ShapeDtypeStruct(first.shape, fi...]
  transfers between devices with their start and end apart: 26 -> 26, of which waited for: 13 -> 7; matrix products, arithmetic and copies ran while one was open for 3% -> 3% of each run, Pallas kernels for 19% -> 17%
where the time goes in v3:
time: 87.7 us; the launch traced here: 87.4 us
  starting transfers between devices  48.5 us (55%)
  waiting for transfers between devices  17.4 us (20%)
  Pallas kernels  17.1 us (19%)
  local copies, waits for them, and re-layouts  1.99 us (2%)
  matrix products  1.36 us (2%)
  between operations  0.91 us (1%)
    ppermute x26, starting transfers between devices, move(): return lax.ppermute(value, AXES, pairs)  48.5 us
    ppermute x26, waiting for transfers between devices, move(): return lax.ppermute(value, AXES, pairs)  17.4 us
    pallas_call x6, Pallas kernels, project(): pl.pallas_call(functools.partial(project_kernel, outers, last, acc is not...  8.69 us
    pallas_call x1, Pallas kernels, add(): pl.pallas_call(add_kernel, out_shape=jax.ShapeDtypeStruct(first.shape, fi...  4.37 us
  transfers between devices with their start and end apart: 26, of which 7 were waited for; matrix products, arithmetic and copies ran while one was open for 3% of the time, Pallas kernels for 17%

profile of v3, /device:TPU:1, one launch (start us, length us, event | category | flops | bytes accessed | tf_op | source)
XLA Modules:
  0.0 87.4 jit_solution(3300903780098144006)
XLA Ops:
  0.6 3.3 %collective-permute-start = (bf16[2,448,4096]{2,1,0:T(8,128)(2,1)}, bf16[2,448,4096]{2,1,0:T(8,128)(2,1)}, u32[]{:S(2)}, u32[]{:S(2)}) collective-permute-start(bf16[2,448,4096]{2,1,0:T(8,128)(2,1)} %bitcast.41), channel_id=1, source_target_pairs={{0,16},{1,17},{2,18},{3,19},{4,20},{5,21},{6,22},{7,23},{8,24},{9,... | collective-permute-start | bytes 22020104 | tf_op jit(solution)/shard_map/ppermute | solution.py:36
  4.0 1.0 %dynamic-slice_bitcast_fusion.1 = (bf16[1,256,256]{2,1,0:T(8,128)(2,1)S(1)}, bf16[1,256,256]{2,1,0:T(8,128)(2,1)S(1)}) fusion(bf16[256,1024]{1,0:T(8,128)(2,1)} %param.6, s32[]{:T(128)S(6)} %select_n.16, s32[]{:T(128)S(6)} %add.42), kind=kLoop, calls=%fused_computation.13 | loop fusion | bytes 524296 | tf_op jit(solution)/shard_map/stack | solution.py:390
  5.0 4.4 %collective-permute-start.3 = (bf16[2,256,256]{2,1,0:T(8,128)(2,1)S(1)}, bf16[2,256,256]{2,1,0:T(8,128)(2,1)S(1)}, u32[]{:S(2)}, u32[]{:S(2)}) collective-permute-start(bf16[2,256,256]{2,1,0:T(8,128)(2,1)S(1)} %pad_maximum_fusion.1.refs_0_), channel_id=1, source_target_pairs={{0,8},{1,9},{2,10},{3,11},{4,12},{5,13},{6,14},{7,15},{8,0},{9,1},... | collective-permute-start | bytes 786440 | tf_op jit(solution)/shard_map/ppermute | solution.py:36
  9.3 2.7 %collective-permute-start.1 = (bf16[2,256,256]{2,1,0:T(8,128)(2,1)S(1)}, bf16[2,256,256]{2,1,0:T(8,128)(2,1)S(1)}, u32[]{:S(2)}, u32[]{:S(2)}) collective-permute-start(bf16[2,256,256]{2,1,0:T(8,128)(2,1)S(1)} %pad_maximum_fusion.1.refs_0_), channel_id=1, source_target_pairs={{0,12},{1,13},{2,14},{3,15},{4,0},{5,1},{6,2},{7,3},{8,4},{9,5},{1... | collective-permute-start | bytes 786440 | tf_op jit(solution)/shard_map/ppermute | solution.py:36
  12.0 0.7 fusion.2.refs_5_.places
  12.7 3.1 %collective-permute-done.2.refs_2_ = bf16[2,256,256]{2,1,0:T(8,128)(2,1)S(1)} collective-permute-done((bf16[2,256,256]{2,1,0:T(8,128)(2,1)S(1)}, bf16[2,256,256]{2,1,0:T(8,128)(2,1)S(1)}, u32[]{:S(2)}, u32[]{:S(2)}) %collective-permute-start.2) | collective-permute-done | bytes 262176 | tf_op jit(solution)/shard_map/ppermute | solution.py:36
  15.8 0.6 shard_map.77
  16.4 2.6 %collective-permute-start.4 = (bf16[4,256,256]{2,1,0:T(8,128)(2,1)S(1)}, bf16[4,256,256]{2,1,0:T(8,128)(2,1)S(1)}, u32[]{:S(2)}, u32[]{:S(2)}) collective-permute-start(bf16[4,256,256]{2,1,0:T(8,128)(2,1)S(1)} %get-tuple-element.25.refs_1_.refs_0_), channel_id=1, source_target_pairs={{0,131},{1,0},{2,1},{3,2},{4,135},{5,4},{6,5},{7,6},{8,139},{9,8},... | collective-permute-start | bytes 1572872 | tf_op jit(solution)/shard_map/ppermute | solution.py:36
  19.0 0.2 collective-permute-start.6
  19.2 4.4 %shard_map.76.refs_0_ = bf16[2,448,4096]{2,1,0:T(8,128)(2,1)S(1)} custom-call(bf16[2,448,4096]{2,1,0:T(8,128)(2,1)S(1)} %bitcast.42, bf16[2,448,4096]{2,1,0:T(8,128)(2,1)} %collective-permute-done.second.refs_4_), custom_call_target="tpu_custom_call" | custom-call | flops 3670016 | bytes 22020096 | tf_op jit(solution)/shard_map/pallas_call | solution.py:236
  23.5 1.2 %shard_map.78 = (f32[2,448,256]{2,1,0:T(8,128)S(1)}, f32[8,128]{1,0:T(8,128)S(1)}) custom-call(s32[39]{0:T(128)S(1)} %fusion.2.refs_5_.places, bf16[2,448,4096]{2,1,0:T(8,128)(2,1)S(1)} %shard_map.76.refs_0_, bf16[4,256,256]{2,1,0:T(8,128)(2,1)S(1)} %get-tuple-element.25.refs_1_.refs_0_), custom_call_target="tpu_custom_call" | custom-call | flops 469762048 | bytes 2359296 | tf_op jit(solution)/shard_map/pallas_call | solution.py:166
  24.7 1.2 %shard_map.79 = (f32[2,448,256]{2,1,0:T(8,128)S(1)}, f32[8,128]{1,0:T(8,128)S(1)}) custom-call(s32[39]{0:T(128)S(1)} %fusion.2.refs_5_.places, bf16[2,448,4096]{2,1,0:T(8,128)(2,1)S(1)} %shard_map.76.refs_0_, bf16[4,256,256]{2,1,0:T(8,128)(2,1)S(1)} %get-tuple-element.27.refs_1_.refs_4_), custom_call_target="tpu_custom_call" | custom-call | flops 469762048 | bytes 2359296 | tf_op jit(solution)/shard_map/pallas_call | solution.py:166
  25.9 2.6 %collective-permute-start.5 = (bf16[4,256,256]{2,1,0:T(8,128)(2,1)S(1)}, bf16[4,256,256]{2,1,0:T(8,128)(2,1)S(1)}, u32[]{:S(2)}, u32[]{:S(2)}) collective-permute-start(bf16[4,256,256]{2,1,0:T(8,128)(2,1)S(1)} %shard_map.80.refs_1_), channel_id=1, source_target_pairs={{0,131},{1,0},{2,1},{3,2},{4,135},{5,4},{6,5},{7,6},{8,139},{9,8},... | collective-permute-start | bytes 1572872 | tf_op jit(solution)/shard_map/ppermute | solution.py:36
  28.5 1.4 %collective-permute-start.12 = (bf16[4,256,256]{2,1,0:T(8,128)(2,1)S(1)}, bf16[4,256,256]{2,1,0:T(8,128)(2,1)S(1)}, u32[]{:S(2)}, u32[]{:S(2)}) collective-permute-start(bf16[4,256,256]{2,1,0:T(8,128)(2,1)S(1)} %get-tuple-element.27.refs_1_.refs_4_), channel_id=1, source_target_pairs={{0,131},{1,0},{2,1},{3,2},{4,135},{5,4},{6,5},{7,6},{8,139},{9,8},... | collective-permute-start | bytes 1572872 | tf_op jit(solution)/shard_map/ppermute | solution.py:36
  30.0 1.2 %shard_map.83 = (f32[2,448,256]{2,1,0:T(8,128)S(1)}, f32[8,128]{1,0:T(8,128)S(1)}) custom-call(s32[39]{0:T(128)S(1)} %fusion.2.refs_5_.places, bf16[2,448,4096]{2,1,0:T(8,128)(2,1)S(1)} %shard_map.76.refs_0_, bf16[4,256,256]{2,1,0:T(8,128)(2,1)S(1)} %shard_map.82.refs_1_.refs_6_, f32[2,448,256]{2,1,0:T(8,128)S(1)} %get-tuple-element.31.refs_2_), custom_call_target="tpu_custom_call" | custom-call | flops 469762048 | bytes 2359296 | tf_op jit(solution)/shard_map/pallas_call | solution.py:166
  31.2 2.9 %collective-permute-done.6.refs_2_ = bf16[4,256,256]{2,1,0:T(8,128)(2,1)S(1)} collective-permute-done((bf16[4,256,256]{2,1,0:T(8,128)(2,1)S(1)}, bf16[4,256,256]{2,1,0:T(8,128)(2,1)S(1)}, u32[]{:S(2)}, u32[]{:S(2)}) %collective-permute-start.6) | collective-permute-done | bytes 524320 | tf_op jit(solution)/shard_map/ppermute | solution.py:36
  34.1 2.2 %shard_map.81 = (f32[2,448,256]{2,1,0:T(8,128)S(1)}, f32[8,128]{1,0:T(8,128)}) custom-call(s32[39]{0:T(128)S(1)} %fusion.2.refs_5_.places, bf16[2,448,4096]{2,1,0:T(8,128)(2,1)S(1)} %shard_map.76.refs_0_, bf16[4,256,256]{2,1,0:T(8,128)(2,1)S(1)} %shard_map.80.refs_1_, bf16[4,256,256]{2,1,0:T(8,128)(2,1)S(1)} %collective-permute-done.6.refs_2_, ...), custom_call_target="tpu_custom_call" | custom-call | flops 939524096 | bytes 4718592 | tf_op jit(solution)/shard_map/pallas_call | solution.py:166
  36.3 1.2 %shard_map.84 = (f32[2,112,256]{2,1,0:T(8,128)S(1)}, bf16[2,112,256]{2,1,0:T(8,128)(2,1)S(1)}, bf16[2,112,256]{2,1,0:T(8,128)(2,1)S(1)}, bf16[2,112,256]{2,1,0:T(8,128)(2,1)S(1)}) custom-call(s32[39]{0:T(128)S(1)} %fusion.2.refs_5_.places, bf16[2,448,4096]{2,1,0:T(8,128)(2,1)S(1)} %shard_map.76.refs_0_, ...), custom_call_target="tpu_custom_call" | custom-call | flops 469762048 | bytes 2359296 | tf_op jit(solution)/shard_map/pallas_call | solution.py:166
  37.6 2.8 %collective-permute-start.9 = (bf16[2,112,256]{2,1,0:T(8,128)(2,1)S(1)}, bf16[2,112,256]{2,1,0:T(8,128)(2,1)S(1)}, u32[]{:S(2)}, u32[]{:S(2)}) collective-permute-start(bf16[2,112,256]{2,1,0:T(8,128)(2,1)S(1)} %get-tuple-element.35), channel_id=1, source_target_pairs={{0,96},{1,97},{2,98},{3,99},{4,100},{5,101},{6,102},{7,103},{8,104... | collective-permute-start | bytes 344072 | tf_op jit(solution)/shard_map/ppermute | solution.py:36
  40.4 0.4 collective-permute-start.10
  40.7 0.7 collective-permute-start.8
  41.4 1.7 %shard_map.85 = (f32[2,112,256]{2,1,0:T(8,128)S(1)}, bf16[2,112,256]{2,1,0:T(8,128)(2,1)S(1)}, bf16[2,112,256]{2,1,0:T(8,128)(2,1)S(1)}, bf16[2,112,256]{2,1,0:T(8,128)(2,1)S(1)}) custom-call(s32[39]{0:T(128)S(1)} %fusion.2.refs_5_.places, bf16[2,448,4096]{2,1,0:T(8,128)(2,1)S(1)} %shard_map.76.refs_0_, ...), custom_call_target="tpu_custom_call" | custom-call | flops 939524096 | bytes 4718592 | tf_op jit(solution)/shard_map/pallas_call | solution.py:166
  43.1 1.7 %collective-permute-start.14 = (bf16[2,112,256]{2,1,0:T(8,128)(2,1)S(1)}, bf16[2,112,256]{2,1,0:T(8,128)(2,1)S(1)}, u32[]{:S(2)}, u32[]{:S(2)}) collective-permute-start(bf16[2,112,256]{2,1,0:T(8,128)(2,1)S(1)} %get-tuple-element.39), channel_id=1, source_target_pairs={{0,32},{1,33},{2,34},{3,35},{4,36},{5,37},{6,38},{7,39},{8,40},{9,... | collective-permute-start | bytes 344072 | tf_op jit(solution)/shard_map/ppermute | solution.py:36
  44.8 1.1 %collective-permute-start.15 = (bf16[2,112,256]{2,1,0:T(8,128)(2,1)S(1)}, bf16[2,112,256]{2,1,0:T(8,128)(2,1)S(1)}, u32[]{:S(2)}, u32[]{:S(2)}) collective-permute-start(bf16[2,112,256]{2,1,0:T(8,128)(2,1)S(1)} %get-tuple-element.40), channel_id=1, source_target_pairs={{0,96},{1,97},{2,98},{3,99},{4,100},{5,101},{6,102},{7,103},{8,104... | collective-permute-start | bytes 344072 | tf_op jit(solution)/shard_map/ppermute | solution.py:36
  46.0 0.9 %collective-permute-start.16 = (bf16[2,112,256]{2,1,0:T(8,128)(2,1)S(1)}, bf16[2,112,256]{2,1,0:T(8,128)(2,1)S(1)}, u32[]{:S(2)}, u32[]{:S(2)}) collective-permute-start(bf16[2,112,256]{2,1,0:T(8,128)(2,1)S(1)} %get-tuple-element.41), channel_id=1, source_target_pairs={{0,64},{1,65},{2,66},{3,67},{4,68},{5,69},{6,70},{7,71},{8,72},{9,... | collective-permute-start | bytes 344072 | tf_op jit(solution)/shard_map/ppermute | solution.py:36
  46.9 4.1 %collective-permute-start.22 = (bf16[4,256,512]{2,1,0:T(8,128)(2,1)S(1)}, bf16[4,256,512]{2,1,0:T(8,128)(2,1)S(1)}, u32[]{:S(2)}, u32[]{:S(2)}) collective-permute-start(bf16[4,256,512]{2,1,0:T(8,128)(2,1)S(1)} %shard_map.88), channel_id=1, source_target_pairs={{0,16},{1,17},{2,18},{3,19},{4,20},{5,21},{6,22},{7,23},{8,24},{9,... | collective-permute-start | bytes 3145736 | tf_op jit(solution)/shard_map/ppermute | solution.py:36
  51.0 3.5 %collective-permute-start.11 = (bf16[112,256]{1,0:T(8,128)(2,1)S(1)}, bf16[112,256]{1,0:T(8,128)(2,1)S(1)}, u32[]{:S(2)}, u32[]{:S(2)}) collective-permute-start(bf16[112,256]{1,0:T(8,128)(2,1)S(1)} %fusion), channel_id=1, source_target_pairs={{0,128},{1,129},{2,130},{3,131},{4,132},{5,133},{6,134},{7,135},{8... | collective-permute-start | bytes 172040 | tf_op jit(solution)/shard_map/ppermute | solution.py:36
  54.7 4.6 %collective-permute-start.17 = (bf16[112,256]{1,0:T(8,128)(2,1)S(1)}, bf16[112,256]{1,0:T(8,128)(2,1)S(1)}, u32[]{:S(2)}, u32[]{:S(2)}) collective-permute-start(bf16[112,256]{1,0:T(8,128)(2,1)S(1)} %fusion.1), channel_id=1, source_target_pairs={{0,128},{1,129},{2,130},{3,131},{4,132},{5,133},{6,134},{7,135},{8... | collective-permute-start | bytes 172040 | tf_op jit(solution)/shard_map/ppermute | solution.py:36
  59.3 2.9 %collective-permute-done.17 = bf16[112,256]{1,0:T(8,128)(2,1)S(1)} collective-permute-done((bf16[112,256]{1,0:T(8,128)(2,1)S(1)}, bf16[112,256]{1,0:T(8,128)(2,1)S(1)}, u32[]{:S(2)}, u32[]{:S(2)}) %collective-permute-start.17) | collective-permute-done | bytes 57376 | tf_op jit(solution)/shard_map/ppermute | solution.py:36
  62.2 0.6 shard_map.86
  62.8 2.6 %collective-permute-start.18 = (f32[56,512]{1,0:T(8,128)S(1)}, f32[56,512]{1,0:T(8,128)S(1)}, u32[]{:S(2)}, u32[]{:S(2)}) collective-permute-start(f32[56,512]{1,0:T(8,128)S(1)} %get-tuple-element.43), channel_id=1, source_target_pairs={{0,16},{1,17},{2,18},{3,19},{4,20},{5,21},{6,22},{7,23},{8,24},{9,... | collective-permute-start | bytes 344072 | tf_op jit(solution)/shard_map/ppermute | solution.py:36
  65.4 0.9 %collective-permute-done.18.other = f32[56,512]{1,0:T(8,128)S(1)} collective-permute-done((f32[56,512]{1,0:T(8,128)S(1)}, f32[56,512]{1,0:T(8,128)S(1)}, u32[]{:S(2)}, u32[]{:S(2)}) %collective-permute-start.18) | collective-permute-done | bytes 114720 | tf_op jit(solution)/shard_map/ppermute | solution.py:36
  66.3 1.4 %shard_map.87 = (f32[1,56,1024]{2,1,0:T(8,128)}, f32[1,56,1024]{2,1,0:T(8,128)}, bf16[56,1024]{1,0:T(8,128)(2,1)S(1)}) custom-call(s32[39]{0:T(128)S(1)} %fusion.2.refs_5_.places, f32[56,512]{1,0:T(8,128)S(1)} %get-tuple-element.42.mine, f32[56,512]{1,0:T(8,128)S(1)} %collective-permute-done.18.other, f32[1,56,1024]{2,1,0:T(8,128)S(1)} %copy-done.1, ...), custom_call_target="tpu_custom_call" | custom-call | tf_op jit(solution)/shard_map/pallas_call | solution.py:339
  67.7 2.7 %collective-permute-start.21 = (bf16[56,1024]{1,0:T(8,128)(2,1)S(1)}, bf16[56,1024]{1,0:T(8,128)(2,1)S(1)}, u32[]{:S(2)}, u32[]{:S(2)}) collective-permute-start(bf16[56,1024]{1,0:T(8,128)(2,1)S(1)} %get-tuple-element.44), channel_id=1, source_target_pairs={{0,2},{1,3},{2,0},{3,1},{4,6},{5,7},{6,4},{7,5},{8,10},{9,11},{10,... | collective-permute-start | bytes 344072 | tf_op jit(solution)/shard_map/ppermute | solution.py:36
  70.5 0.5 collective-permute-start.20
  71.0 2.1 %collective-permute-start.19 = (bf16[56,1024]{1,0:T(8,128)(2,1)S(1)}, bf16[56,1024]{1,0:T(8,128)(2,1)S(1)}, u32[]{:S(2)}, u32[]{:S(2)}) collective-permute-start(bf16[56,1024]{1,0:T(8,128)(2,1)S(1)} %get-tuple-element.44), channel_id=1, source_target_pairs={{0,3},{1,0},{2,1},{3,2},{4,7},{5,4},{6,5},{7,6},{8,11},{9,8},{10,9... | collective-permute-start | bytes 344072 | tf_op jit(solution)/shard_map/ppermute | solution.py:36
  73.2 2.4 %collective-permute-done.20 = bf16[56,1024]{1,0:T(8,128)(2,1)S(1)} collective-permute-done((bf16[56,1024]{1,0:T(8,128)(2,1)S(1)}, bf16[56,1024]{1,0:T(8,128)(2,1)S(1)}, u32[]{:S(2)}, u32[]{:S(2)}) %collective-permute-start.20) | collective-permute-done | bytes 114720 | tf_op jit(solution)/shard_map/ppermute | solution.py:36
  75.7 0.1 constant_dynamic-update-slice_fusion
  75.8 0.3 convolution_convert_fusion
  76.2 0.3 convolution_convert_fusion.1
  76.5 0.3 convolution_convert_fusion.2
  76.9 0.4 collective-permute-start.23
  77.3 3.0 %collective-permute-start.24 = (bf16[224,256]{1,0:T(8,128)(2,1)S(1)}, bf16[224,256]{1,0:T(8,128)(2,1)S(1)}, u32[]{:S(2)}, u32[]{:S(2)}) collective-permute-start(bf16[224,256]{1,0:T(8,128)(2,1)S(1)} %convolution_convert_fusion.1), channel_id=1, source_target_pairs={{0,12},{1,13},{2,14},{3,15},{4,0},{5,1},{6,2},{7,3},{8,4},{9,5},{1... | collective-permute-start | bytes 344072 | tf_op jit(solution)/shard_map/ppermute | solution.py:36
  80.3 0.2 collective-permute-start.25
  80.5 0.3 convolution_convert_fusion.3
  80.8 1.7 %collective-permute-done.23 = bf16[224,256]{1,0:T(8,128)(2,1)S(1)} collective-permute-done((bf16[224,256]{1,0:T(8,128)(2,1)S(1)}, bf16[224,256]{1,0:T(8,128)(2,1)S(1)}, u32[]{:S(2)}, u32[]{:S(2)}) %collective-permute-start.23) | collective-permute-done | bytes 114720 | tf_op jit(solution)/shard_map/ppermute | solution.py:36
  82.5 3.6 %collective-permute-done.25 = bf16[224,256]{1,0:T(8,128)(2,1)S(1)} collective-permute-done((bf16[224,256]{1,0:T(8,128)(2,1)S(1)}, bf16[224,256]{1,0:T(8,128)(2,1)S(1)}, u32[]{:S(2)}, u32[]{:S(2)}) %collective-permute-start.25) | collective-permute-done | bytes 114720 | tf_op jit(solution)/shard_map/ppermute | solution.py:36
  86.1 1.3 %shard_map.89 = bf16[16,56,256]{2,1,0:T(8,128)(2,1)} custom-call(s32[39]{0:T(128)S(1)} %fusion.2.refs_5_.places, bf16[4,56,256]{2,1,0:T(8,128)(2,1)S(1)} %bitcast.47, bf16[4,56,256]{2,1,0:T(8,128)(2,1)S(1)} %bitcast.44, bf16[4,56,256]{2,1,0:T(8,128)(2,1)S(1)} %bitcast.45, bf16[4,56,256]{2,1,0:T(8,128)(2,1)S(1)} %bitcast.46), custom_call_target="tpu_custom_call" | custom-call | tf_op jit(solution)/shard_map/pallas_call | solution.py:362
  (43 shorter events, 0.5 us)
Async XLA Ops:
  0.6 15.2 %collective-permute-start = (bf16[2,448,4096]{2,1,0:T(8,128)(2,1)}, bf16[2,448,4096]{2,1,0:T(8,128)(2,1)}, u32[]{:S(2)}, u32[]{:S(2)}) collective-permute-start(bf16[2,448,4096]{2,1,0:T(8,128)(2,1)} %bitcast.41), channel_id=1, source_target_pairs={{0,16},{1,17},{2,18},{3,19},{4,20},{5,21},{6,22},{7,23},{8,24},{9,... | collective-permute-start | bytes 22020104 | tf_op jit(solution)/shard_map/ppermute | solution.py:36
  5.0 7.7 %collective-permute-start.3 = (bf16[2,256,256]{2,1,0:T(8,128)(2,1)S(1)}, bf16[2,256,256]{2,1,0:T(8,128)(2,1)S(1)}, u32[]{:S(2)}, u32[]{:S(2)}) collective-permute-start(bf16[2,256,256]{2,1,0:T(8,128)(2,1)S(1)} %pad_maximum_fusion.1.refs_0_), channel_id=1, source_target_pairs={{0,8},{1,9},{2,10},{3,11},{4,12},{5,13},{6,14},{7,15},{8,0},{9,1},... | collective-permute-start | bytes 786440 | tf_op jit(solution)/shard_map/ppermute | solution.py:36
  9.3 6.4 %collective-permute-start.2 = (bf16[2,256,256]{2,1,0:T(8,128)(2,1)S(1)}, bf16[2,256,256]{2,1,0:T(8,128)(2,1)S(1)}, u32[]{:S(2)}, u32[]{:S(2)}) collective-permute-start(bf16[2,256,256]{2,1,0:T(8,128)(2,1)S(1)} %pad_maximum_fusion.1.refs_0_), channel_id=1, source_target_pairs={{0,4},{1,5},{2,6},{3,7},{4,8},{5,9},{6,10},{7,11},{8,12},{9,13},{1... | collective-permute-start | bytes 786440 | tf_op jit(solution)/shard_map/ppermute | solution.py:36
  9.3 6.4 %collective-permute-start.1 = (bf16[2,256,256]{2,1,0:T(8,128)(2,1)S(1)}, bf16[2,256,256]{2,1,0:T(8,128)(2,1)S(1)}, u32[]{:S(2)}, u32[]{:S(2)}) collective-permute-start(bf16[2,256,256]{2,1,0:T(8,128)(2,1)S(1)} %pad_maximum_fusion.1.refs_0_), channel_id=1, source_target_pairs={{0,12},{1,13},{2,14},{3,15},{4,0},{5,1},{6,2},{7,3},{8,4},{9,5},{1... | collective-permute-start | bytes 786440 | tf_op jit(solution)/shard_map/ppermute | solution.py:36
  15.8 3.4 %copy-start = (bf16[1,16,56,4096]{3,2,1,0:T(8,128)(2,1)S(1)}, bf16[1,16,56,4096]{3,2,1,0:T(8,128)(2,1)}, u32[]{:S(2)}) copy-start(bf16[1,16,56,4096]{3,2,1,0:T(8,128)(2,1)} %param.5) | copy-start | bytes 22020100
  16.4 9.5 %collective-permute-start.4 = (bf16[4,256,256]{2,1,0:T(8,128)(2,1)S(1)}, bf16[4,256,256]{2,1,0:T(8,128)(2,1)S(1)}, u32[]{:S(2)}, u32[]{:S(2)}) collective-permute-start(bf16[4,256,256]{2,1,0:T(8,128)(2,1)S(1)} %get-tuple-element.25.refs_1_.refs_0_), channel_id=1, source_target_pairs={{0,131},{1,0},{2,1},{3,2},{4,135},{5,4},{6,5},{7,6},{8,139},{9,8},... | collective-permute-start | bytes 1572872 | tf_op jit(solution)/shard_map/ppermute | solution.py:36
  19.0 11.0 %collective-permute-start.7 = (bf16[4,256,256]{2,1,0:T(8,128)(2,1)S(1)}, bf16[4,256,256]{2,1,0:T(8,128)(2,1)S(1)}, u32[]{:S(2)}, u32[]{:S(2)}) collective-permute-start(bf16[4,256,256]{2,1,0:T(8,128)(2,1)S(1)} %get-tuple-element.27.refs_1_.refs_4_), channel_id=1, source_target_pairs={{0,1},{1,2},{2,3},{3,128},{4,5},{5,6},{6,7},{7,132},{8,9},{9,10},{... | collective-permute-start | bytes 1572872 | tf_op jit(solution)/shard_map/ppermute | solution.py:36
  19.0 15.2 %collective-permute-start.6 = (bf16[4,256,256]{2,1,0:T(8,128)(2,1)S(1)}, bf16[4,256,256]{2,1,0:T(8,128)(2,1)S(1)}, u32[]{:S(2)}, u32[]{:S(2)}) collective-permute-start(bf16[4,256,256]{2,1,0:T(8,128)(2,1)S(1)} %get-tuple-element.25.refs_1_.refs_0_), channel_id=1, source_target_pairs={{0,1},{1,2},{2,3},{3,128},{4,5},{5,6},{6,7},{7,132},{8,9},{9,10},{... | collective-permute-start | bytes 1572872 | tf_op jit(solution)/shard_map/ppermute | solution.py:36
  25.9 10.4 %collective-permute-start.5 = (bf16[4,256,256]{2,1,0:T(8,128)(2,1)S(1)}, bf16[4,256,256]{2,1,0:T(8,128)(2,1)S(1)}, u32[]{:S(2)}, u32[]{:S(2)}) collective-permute-start(bf16[4,256,256]{2,1,0:T(8,128)(2,1)S(1)} %shard_map.80.refs_1_), channel_id=1, source_target_pairs={{0,131},{1,0},{2,1},{3,2},{4,135},{5,4},{6,5},{7,6},{8,139},{9,8},... | collective-permute-start | bytes 1572872 | tf_op jit(solution)/shard_map/ppermute | solution.py:36
  28.5 12.9 %collective-permute-start.12 = (bf16[4,256,256]{2,1,0:T(8,128)(2,1)S(1)}, bf16[4,256,256]{2,1,0:T(8,128)(2,1)S(1)}, u32[]{:S(2)}, u32[]{:S(2)}) collective-permute-start(bf16[4,256,256]{2,1,0:T(8,128)(2,1)S(1)} %get-tuple-element.27.refs_1_.refs_4_), channel_id=1, source_target_pairs={{0,131},{1,0},{2,1},{3,2},{4,135},{5,4},{6,5},{7,6},{8,139},{9,8},... | collective-permute-start | bytes 1572872 | tf_op jit(solution)/shard_map/ppermute | solution.py:36
  30.0 11.4 %collective-permute-start.13 = (bf16[4,256,256]{2,1,0:T(8,128)(2,1)S(1)}, bf16[4,256,256]{2,1,0:T(8,128)(2,1)S(1)}, u32[]{:S(2)}, u32[]{:S(2)}) collective-permute-start(bf16[4,256,256]{2,1,0:T(8,128)(2,1)S(1)} %shard_map.82.refs_1_.refs_6_), channel_id=1, source_target_pairs={{0,1},{1,2},{2,3},{3,128},{4,5},{5,6},{6,7},{7,132},{8,9},{9,10},{... | collective-permute-start | bytes 1572872 | tf_op jit(solution)/shard_map/ppermute | solution.py:36
  37.6 8.4 %collective-permute-start.9 = (bf16[2,112,256]{2,1,0:T(8,128)(2,1)S(1)}, bf16[2,112,256]{2,1,0:T(8,128)(2,1)S(1)}, u32[]{:S(2)}, u32[]{:S(2)}) collective-permute-start(bf16[2,112,256]{2,1,0:T(8,128)(2,1)S(1)} %get-tuple-element.35), channel_id=1, source_target_pairs={{0,96},{1,97},{2,98},{3,99},{4,100},{5,101},{6,102},{7,103},{8,104... | collective-permute-start | bytes 344072 | tf_op jit(solution)/shard_map/ppermute | solution.py:36
  40.4 6.5 %collective-permute-start.10 = (bf16[2,112,256]{2,1,0:T(8,128)(2,1)S(1)}, bf16[2,112,256]{2,1,0:T(8,128)(2,1)S(1)}, u32[]{:S(2)}, u32[]{:S(2)}) collective-permute-start(bf16[2,112,256]{2,1,0:T(8,128)(2,1)S(1)} %get-tuple-element.36), channel_id=1, source_target_pairs={{0,64},{1,65},{2,66},{3,67},{4,68},{5,69},{6,70},{7,71},{8,72},{9,... | collective-permute-start | bytes 344072 | tf_op jit(solution)/shard_map/ppermute | solution.py:36
  40.7 10.2 %collective-permute-start.8 = (bf16[2,112,256]{2,1,0:T(8,128)(2,1)S(1)}, bf16[2,112,256]{2,1,0:T(8,128)(2,1)S(1)}, u32[]{:S(2)}, u32[]{:S(2)}) collective-permute-start(bf16[2,112,256]{2,1,0:T(8,128)(2,1)S(1)} %get-tuple-element.34.refs_4_), channel_id=1, source_target_pairs={{0,32},{1,33},{2,34},{3,35},{4,36},{5,37},{6,38},{7,39},{8,40},{9,... | collective-permute-start | bytes 344072 | tf_op jit(solution)/shard_map/ppermute | solution.py:36
  43.1 11.5 %collective-permute-start.14 = (bf16[2,112,256]{2,1,0:T(8,128)(2,1)S(1)}, bf16[2,112,256]{2,1,0:T(8,128)(2,1)S(1)}, u32[]{:S(2)}, u32[]{:S(2)}) collective-permute-start(bf16[2,112,256]{2,1,0:T(8,128)(2,1)S(1)} %get-tuple-element.39), channel_id=1, source_target_pairs={{0,32},{1,33},{2,34},{3,35},{4,36},{5,37},{6,38},{7,39},{8,40},{9,... | collective-permute-start | bytes 344072 | tf_op jit(solution)/shard_map/ppermute | solution.py:36
  44.8 9.8 %collective-permute-start.15 = (bf16[2,112,256]{2,1,0:T(8,128)(2,1)S(1)}, bf16[2,112,256]{2,1,0:T(8,128)(2,1)S(1)}, u32[]{:S(2)}, u32[]{:S(2)}) collective-permute-start(bf16[2,112,256]{2,1,0:T(8,128)(2,1)S(1)} %get-tuple-element.40), channel_id=1, source_target_pairs={{0,96},{1,97},{2,98},{3,99},{4,100},{5,101},{6,102},{7,103},{8,104... | collective-permute-start | bytes 344072 | tf_op jit(solution)/shard_map/ppermute | solution.py:36
  45.9 20.4 %copy-start.1 = (f32[1,56,1024]{2,1,0:T(8,128)S(1)}, f32[1,56,1024]{2,1,0:T(8,128)}, u32[]{:S(2)}) copy-start(f32[1,56,1024]{2,1,0:T(8,128)} %first.1) | copy-start | bytes 688132
  46.0 20.4 %copy-start.2 = (f32[1,56,1024]{2,1,0:T(8,128)S(1)}, f32[1,56,1024]{2,1,0:T(8,128)}, u32[]{:S(2)}) copy-start(f32[1,56,1024]{2,1,0:T(8,128)} %second.1) | copy-start | bytes 688132
  46.0 8.6 %collective-permute-start.16 = (bf16[2,112,256]{2,1,0:T(8,128)(2,1)S(1)}, bf16[2,112,256]{2,1,0:T(8,128)(2,1)S(1)}, u32[]{:S(2)}, u32[]{:S(2)}) collective-permute-start(bf16[2,112,256]{2,1,0:T(8,128)(2,1)S(1)} %get-tuple-element.41), channel_id=1, source_target_pairs={{0,64},{1,65},{2,66},{3,67},{4,68},{5,69},{6,70},{7,71},{8,72},{9,... | collective-permute-start | bytes 344072 | tf_op jit(solution)/shard_map/ppermute | solution.py:36
  46.9 28.8 %collective-permute-start.22 = (bf16[4,256,512]{2,1,0:T(8,128)(2,1)S(1)}, bf16[4,256,512]{2,1,0:T(8,128)(2,1)S(1)}, u32[]{:S(2)}, u32[]{:S(2)}) collective-permute-start(bf16[4,256,512]{2,1,0:T(8,128)(2,1)S(1)} %shard_map.88), channel_id=1, source_target_pairs={{0,16},{1,17},{2,18},{3,19},{4,20},{5,21},{6,22},{7,23},{8,24},{9,... | collective-permute-start | bytes 3145736 | tf_op jit(solution)/shard_map/ppermute | solution.py:36
  51.0 8.2 %collective-permute-start.11 = (bf16[112,256]{1,0:T(8,128)(2,1)S(1)}, bf16[112,256]{1,0:T(8,128)(2,1)S(1)}, u32[]{:S(2)}, u32[]{:S(2)}) collective-permute-start(bf16[112,256]{1,0:T(8,128)(2,1)S(1)} %fusion), channel_id=1, source_target_pairs={{0,128},{1,129},{2,130},{3,131},{4,132},{5,133},{6,134},{7,135},{8... | collective-permute-start | bytes 172040 | tf_op jit(solution)/shard_map/ppermute | solution.py:36
  54.7 7.5 %collective-permute-start.17 = (bf16[112,256]{1,0:T(8,128)(2,1)S(1)}, bf16[112,256]{1,0:T(8,128)(2,1)S(1)}, u32[]{:S(2)}, u32[]{:S(2)}) collective-permute-start(bf16[112,256]{1,0:T(8,128)(2,1)S(1)} %fusion.1), channel_id=1, source_target_pairs={{0,128},{1,129},{2,130},{3,131},{4,132},{5,133},{6,134},{7,135},{8... | collective-permute-start | bytes 172040 | tf_op jit(solution)/shard_map/ppermute | solution.py:36
  62.8 3.5 %collective-permute-start.18 = (f32[56,512]{1,0:T(8,128)S(1)}, f32[56,512]{1,0:T(8,128)S(1)}, u32[]{:S(2)}, u32[]{:S(2)}) collective-permute-start(f32[56,512]{1,0:T(8,128)S(1)} %get-tuple-element.43), channel_id=1, source_target_pairs={{0,16},{1,17},{2,18},{3,19},{4,20},{5,21},{6,22},{7,23},{8,24},{9,... | collective-permute-start | bytes 344072 | tf_op jit(solution)/shard_map/ppermute | solution.py:36
  67.7 5.5 %collective-permute-start.21 = (bf16[56,1024]{1,0:T(8,128)(2,1)S(1)}, bf16[56,1024]{1,0:T(8,128)(2,1)S(1)}, u32[]{:S(2)}, u32[]{:S(2)}) collective-permute-start(bf16[56,1024]{1,0:T(8,128)(2,1)S(1)} %get-tuple-element.44), channel_id=1, source_target_pairs={{0,2},{1,3},{2,0},{3,1},{4,6},{5,7},{6,4},{7,5},{8,10},{9,11},{10,... | collective-permute-start | bytes 344072 | tf_op jit(solution)/shard_map/ppermute | solution.py:36
  70.5 5.1 %collective-permute-start.20 = (bf16[56,1024]{1,0:T(8,128)(2,1)S(1)}, bf16[56,1024]{1,0:T(8,128)(2,1)S(1)}, u32[]{:S(2)}, u32[]{:S(2)}) collective-permute-start(bf16[56,1024]{1,0:T(8,128)(2,1)S(1)} %get-tuple-element.44), channel_id=1, source_target_pairs={{0,1},{1,2},{2,3},{3,0},{4,5},{5,6},{6,7},{7,4},{8,9},{9,10},{10,1... | collective-permute-start | bytes 344072 | tf_op jit(solution)/shard_map/ppermute | solution.py:36
  71.0 4.6 %collective-permute-start.19 = (bf16[56,1024]{1,0:T(8,128)(2,1)S(1)}, bf16[56,1024]{1,0:T(8,128)(2,1)S(1)}, u32[]{:S(2)}, u32[]{:S(2)}) collective-permute-start(bf16[56,1024]{1,0:T(8,128)(2,1)S(1)} %get-tuple-element.44), channel_id=1, source_target_pairs={{0,3},{1,0},{2,1},{3,2},{4,7},{5,4},{6,5},{7,6},{8,11},{9,8},{10,9... | collective-permute-start | bytes 344072 | tf_op jit(solution)/shard_map/ppermute | solution.py:36
  76.9 5.6 %collective-permute-start.23 = (bf16[224,256]{1,0:T(8,128)(2,1)S(1)}, bf16[224,256]{1,0:T(8,128)(2,1)S(1)}, u32[]{:S(2)}, u32[]{:S(2)}) collective-permute-start(bf16[224,256]{1,0:T(8,128)(2,1)S(1)} %convolution_convert_fusion.2), channel_id=1, source_target_pairs={{0,4},{1,5},{2,6},{3,7},{4,8},{5,9},{6,10},{7,11},{8,12},{9,13},{1... | collective-permute-start | bytes 344072 | tf_op jit(solution)/shard_map/ppermute | solution.py:36
  77.3 5.2 %collective-permute-start.24 = (bf16[224,256]{1,0:T(8,128)(2,1)S(1)}, bf16[224,256]{1,0:T(8,128)(2,1)S(1)}, u32[]{:S(2)}, u32[]{:S(2)}) collective-permute-start(bf16[224,256]{1,0:T(8,128)(2,1)S(1)} %convolution_convert_fusion.1), channel_id=1, source_target_pairs={{0,12},{1,13},{2,14},{3,15},{4,0},{5,1},{6,2},{7,3},{8,4},{9,5},{1... | collective-permute-start | bytes 344072 | tf_op jit(solution)/shard_map/ppermute | solution.py:36
  80.3 5.8 %collective-permute-start.25 = (bf16[224,256]{1,0:T(8,128)(2,1)S(1)}, bf16[224,256]{1,0:T(8,128)(2,1)S(1)}, u32[]{:S(2)}, u32[]{:S(2)}) collective-permute-start(bf16[224,256]{1,0:T(8,128)(2,1)S(1)} %convolution_convert_fusion), channel_id=1, source_target_pairs={{0,8},{1,9},{2,10},{3,11},{4,12},{5,13},{6,14},{7,15},{8,0},{9,1},... | collective-permute-start | bytes 344072 | tf_op jit(solution)/shard_map/ppermute | solution.py:36

commit v4 on v3

--- a/solution.py
+++ b/solution.py
@@ -313,40 +313,61 @@
     )(places, *sums)
 
 
-def adam_kernel(places, mine, other, first, second, new_first, new_second, direction):
+def halves(places, array, n):
+    half = array.shape[2] // C
+    parts = [array[0, :, m * half : (m + 1) * half] for m in (n, 1 - n)]
+    return jnp.where(places[CORE] == 0, parts[0], parts[1])
+
+
+def first_of(moment, value):
+    return beta_one * moment + (1.0 - beta_one) * value
+
+
+def second_of(moment, value):
+    return beta_two * moment + (1.0 - beta_two) * value * value
+
+
+def direction_kernel(places, mine, other, first, second, out):
+    half = mine.shape[1]
+    for n, ref in enumerate((mine, other)):
+        value = ref[...]
+        moment = first_of(halves(places, first, n), value)
+        square = second_of(halves(places, second, n), value)
+        step = moment / bias_one / (jnp.sqrt(square / bias_two) + epsilon)
+        out[:, n * half : (n + 1) * half] = step.astype(out.dtype)
+
+
+def moments_kernel(places, mine, other, first, second, after, new_first, new_second):
     half = mine.shape[1]
     is_first = places[CORE] == 0
     own, far = mine[...], other[...]
     for n in range(C):
         at = slice(n * half, (n + 1) * half)
         value = jnp.where(is_first, far, own) if n else jnp.where(is_first, own, far)
-        moment = beta_one * first[0, :, at] + (1.0 - beta_one) * value
-        square = beta_two * second[0, :, at] + (1.0 - beta_two) * value * value
-        new_first[0, :, at] = moment
-        new_second[0, :, at] = square
-    for n in range(C):
-        step = []
-        for m in (n, 1 - n):
-            at = slice(m * half, (m + 1) * half)
-            root = jnp.sqrt(new_second[0, :, at] / bias_two) + epsilon
-            step.append(new_first[0, :, at] / bias_one / root)
-        value = jnp.where(is_first, step[0], step[1])
-        direction[:, n * half : (n + 1) * half] = value.astype(direction.dtype)
+        new_first[0, :, at] = first_of(first[0, :, at], value)
+        new_second[0, :, at] = second_of(second[0, :, at], value)
 
 
 def adam(places, mine, other, first, second):
     whole = pl.BlockSpec(memory_space=pltpu.VMEM)
-    return pl.pallas_call(
-        adam_kernel,
-        out_shape=[
-            jax.ShapeDtypeStruct(first.shape, jnp.float32),
-            jax.ShapeDtypeStruct(first.shape, jnp.float32),
-            jax.ShapeDtypeStruct(first.shape[1:], jnp.bfloat16),
-        ],
-        in_specs=[pl.BlockSpec(memory_space=pltpu.SMEM)] + [whole] * 4,
-        out_specs=[whole] * 3,
-        compiler_params=pltpu.CompilerParams(vmem_limit_bytes=5 * 1024 * 1024),
-    )(places, mine, other, first, second)
+    operands = (places, mine, other, first, second)
+    specs = [pl.BlockSpec(memory_space=pltpu.SMEM)] + [whole] * 4
+    params = pltpu.CompilerParams(vmem_limit_bytes=5 * 1024 * 1024)
+    direction = pl.pallas_call(
+        direction_kernel,
+        out_shape=jax.ShapeDtypeStruct(first.shape[1:], jnp.bfloat16),
+        in_specs=specs,
+        out_specs=whole,
+        compiler_params=params,
+    )(*operands)
+    new_first, new_second = pl.pallas_call(
+        moments_kernel,
+        out_shape=[jax.ShapeDtypeStruct(first.shape, jnp.float32)] * 2,
+        in_specs=specs + [whole],
+        out_specs=[whole] * 2,
+        compiler_params=params,
+    )(*operands, direction)
+    return new_first, new_second, direction
 
 
 def place_kernel(places, *refs):
@@ -404,7 +425,7 @@
     accs, done = zip(
         *[project(places, (0,), both, [held], None, False) for held in stacks]
     )
-    ahead[0] = pass_on(ahead[0], *done)
+    ahead[0] = pass_on(ahead[0], done[0])
     behind[1] = pass_on(behind[1], *done)
     far = [
         move(ahead[0], by_core(along_ring(-1), along_x(-1))),

time: 87.7 us -> 86.7 us (0.989)
  waiting for transfers between devices: 17.4 us -> 15 us
    ppermute x26, waiting for transfers between devices: 17.4 us -> 15 us  [move(): return lax.ppermute(value, AXES, pairs)]
    pallas_call x1 -> x2, Pallas kernels: 1.41 us -> 2.09 us  [the longest x1 1.38 us: adam(): pl.pallas_call(moments_kernel, out_shape=[jax.ShapeDtypeStruct(first.shap...]
  transfers between devices with their start and end apart: 26 -> 26, of which waited for: 7 -> 8; matrix products, arithmetic and copies ran while one was open for 3% -> 3% of each run, Pallas kernels for 17% -> 18%
where the time goes in v4:
time: 86.7 us; the launch traced here: 86.5 us
  starting transfers between devices  49.3 us (57%)
  Pallas kernels  17.8 us (21%)
  waiting for transfers between devices  15 us (17%)
  local copies, waits for them, and re-layouts  1.99 us (2%)
  matrix products  1.36 us (2%)
  between operations  0.91 us (1%)
    ppermute x26, starting transfers between devices, move(): return lax.ppermute(value, AXES, pairs)  49.3 us
    ppermute x26, waiting for transfers between devices, move(): return lax.ppermute(value, AXES, pairs)  15 us
    pallas_call x6, Pallas kernels, project(): pl.pallas_call(functools.partial(project_kernel, outers, last, acc is not...  8.69 us
    pallas_call x1, Pallas kernels, add(): pl.pallas_call(add_kernel, out_shape=jax.ShapeDtypeStruct(first.shape, fi...  4.37 us
  transfers between devices with their start and end apart: 26, of which 8 were waited for; matrix products, arithmetic and copies ran while one was open for 3% of the time, Pallas kernels for 18%

profile of v4, /device:TPU:1, one launch (start us, length us, event | category | flops | bytes accessed | tf_op | source)
XLA Modules:
  0.0 86.5 jit_solution(6653988492471526657)
XLA Ops:
  0.6 3.3 %collective-permute-start = (bf16[2,448,4096]{2,1,0:T(8,128)(2,1)}, bf16[2,448,4096]{2,1,0:T(8,128)(2,1)}, u32[]{:S(2)}, u32[]{:S(2)}) collective-permute-start(bf16[2,448,4096]{2,1,0:T(8,128)(2,1)} %bitcast.41), channel_id=1, source_target_pairs={{0,16},{1,17},{2,18},{3,19},{4,20},{5,21},{6,22},{7,23},{8,24},{9,... | collective-permute-start | bytes 22020104 | tf_op jit(solution)/shard_map/ppermute | solution.py:36
  4.0 1.0 %dynamic-slice_bitcast_fusion.1 = (bf16[1,256,256]{2,1,0:T(8,128)(2,1)S(1)}, bf16[1,256,256]{2,1,0:T(8,128)(2,1)S(1)}) fusion(bf16[256,1024]{1,0:T(8,128)(2,1)} %param.6, s32[]{:T(128)S(6)} %select_n.16, s32[]{:T(128)S(6)} %add.42), kind=kLoop, calls=%fused_computation.13 | loop fusion | bytes 524296 | tf_op jit(solution)/shard_map/stack | solution.py:411
  5.0 4.4 %collective-permute-start.3 = (bf16[2,256,256]{2,1,0:T(8,128)(2,1)S(1)}, bf16[2,256,256]{2,1,0:T(8,128)(2,1)S(1)}, u32[]{:S(2)}, u32[]{:S(2)}) collective-permute-start(bf16[2,256,256]{2,1,0:T(8,128)(2,1)S(1)} %pad_maximum_fusion.1.refs_0_), channel_id=1, source_target_pairs={{0,8},{1,9},{2,10},{3,11},{4,12},{5,13},{6,14},{7,15},{8,0},{9,1},... | collective-permute-start | bytes 786440 | tf_op jit(solution)/shard_map/ppermute | solution.py:36
  9.3 2.7 %collective-permute-start.1 = (bf16[2,256,256]{2,1,0:T(8,128)(2,1)S(1)}, bf16[2,256,256]{2,1,0:T(8,128)(2,1)S(1)}, u32[]{:S(2)}, u32[]{:S(2)}) collective-permute-start(bf16[2,256,256]{2,1,0:T(8,128)(2,1)S(1)} %pad_maximum_fusion.1.refs_0_), channel_id=1, source_target_pairs={{0,12},{1,13},{2,14},{3,15},{4,0},{5,1},{6,2},{7,3},{8,4},{9,5},{1... | collective-permute-start | bytes 786440 | tf_op jit(solution)/shard_map/ppermute | solution.py:36
  12.0 0.7 fusion.2.refs_5_.places
  12.7 3.1 %collective-permute-done.2.refs_2_ = bf16[2,256,256]{2,1,0:T(8,128)(2,1)S(1)} collective-permute-done((bf16[2,256,256]{2,1,0:T(8,128)(2,1)S(1)}, bf16[2,256,256]{2,1,0:T(8,128)(2,1)S(1)}, u32[]{:S(2)}, u32[]{:S(2)}) %collective-permute-start.2) | collective-permute-done | bytes 262176 | tf_op jit(solution)/shard_map/ppermute | solution.py:36
  15.8 0.6 shard_map.77
  16.4 2.6 %collective-permute-start.4 = (bf16[4,256,256]{2,1,0:T(8,128)(2,1)S(1)}, bf16[4,256,256]{2,1,0:T(8,128)(2,1)S(1)}, u32[]{:S(2)}, u32[]{:S(2)}) collective-permute-start(bf16[4,256,256]{2,1,0:T(8,128)(2,1)S(1)} %get-tuple-element.24.refs_1_.refs_0_), channel_id=1, source_target_pairs={{0,131},{1,0},{2,1},{3,2},{4,135},{5,4},{6,5},{7,6},{8,139},{9,8},... | collective-permute-start | bytes 1572872 | tf_op jit(solution)/shard_map/ppermute | solution.py:36
  19.0 0.2 collective-permute-start.6
  19.2 4.4 %shard_map.76.refs_0_ = bf16[2,448,4096]{2,1,0:T(8,128)(2,1)S(1)} custom-call(bf16[2,448,4096]{2,1,0:T(8,128)(2,1)S(1)} %bitcast.42, bf16[2,448,4096]{2,1,0:T(8,128)(2,1)} %collective-permute-done.second.refs_4_), custom_call_target="tpu_custom_call" | custom-call | flops 3670016 | bytes 22020096 | tf_op jit(solution)/shard_map/pallas_call | solution.py:236
  23.5 1.2 %shard_map.78 = (f32[2,448,256]{2,1,0:T(8,128)S(1)}, f32[8,128]{1,0:T(8,128)S(1)}) custom-call(s32[39]{0:T(128)S(1)} %fusion.2.refs_5_.places, bf16[2,448,4096]{2,1,0:T(8,128)(2,1)S(1)} %shard_map.76.refs_0_, bf16[4,256,256]{2,1,0:T(8,128)(2,1)S(1)} %get-tuple-element.24.refs_1_.refs_0_), custom_call_target="tpu_custom_call" | custom-call | flops 469762048 | bytes 2359296 | tf_op jit(solution)/shard_map/pallas_call | solution.py:166
  24.7 0.4 collective-permute-done.4.refs_0_
  25.1 3.4 %collective-permute-start.5 = (bf16[4,256,256]{2,1,0:T(8,128)(2,1)S(1)}, bf16[4,256,256]{2,1,0:T(8,128)(2,1)S(1)}, u32[]{:S(2)}, u32[]{:S(2)}) collective-permute-start(bf16[4,256,256]{2,1,0:T(8,128)(2,1)S(1)} %shard_map.79.refs_1_), channel_id=1, source_target_pairs={{0,131},{1,0},{2,1},{3,2},{4,135},{5,4},{6,5},{7,6},{8,139},{9,8},... | collective-permute-start | bytes 1572872 | tf_op jit(solution)/shard_map/ppermute | solution.py:36
  28.5 0.3 collective-permute-start.12
  28.8 1.2 %shard_map.81 = (f32[2,448,256]{2,1,0:T(8,128)S(1)}, f32[8,128]{1,0:T(8,128)S(1)}) custom-call(s32[39]{0:T(128)S(1)} %fusion.2.refs_5_.places, bf16[2,448,4096]{2,1,0:T(8,128)(2,1)S(1)} %shard_map.76.refs_0_, bf16[4,256,256]{2,1,0:T(8,128)(2,1)S(1)} %get-tuple-element.28.refs_1_.refs_4_), custom_call_target="tpu_custom_call" | custom-call | flops 469762048 | bytes 2359296 | tf_op jit(solution)/shard_map/pallas_call | solution.py:166
  30.0 1.3 %collective-permute-start.13 = (bf16[4,256,256]{2,1,0:T(8,128)(2,1)S(1)}, bf16[4,256,256]{2,1,0:T(8,128)(2,1)S(1)}, u32[]{:S(2)}, u32[]{:S(2)}) collective-permute-start(bf16[4,256,256]{2,1,0:T(8,128)(2,1)S(1)} %shard_map.82.refs_1_.refs_6_), channel_id=1, source_target_pairs={{0,1},{1,2},{2,3},{3,128},{4,5},{5,6},{6,7},{7,132},{8,9},{9,10},{... | collective-permute-start | bytes 1572872 | tf_op jit(solution)/shard_map/ppermute | solution.py:36
  31.3 1.2 %shard_map.83 = (f32[2,448,256]{2,1,0:T(8,128)S(1)}, f32[8,128]{1,0:T(8,128)S(1)}) custom-call(s32[39]{0:T(128)S(1)} %fusion.2.refs_5_.places, bf16[2,448,4096]{2,1,0:T(8,128)(2,1)S(1)} %shard_map.76.refs_0_, bf16[4,256,256]{2,1,0:T(8,128)(2,1)S(1)} %shard_map.82.refs_1_.refs_6_, f32[2,448,256]{2,1,0:T(8,128)S(1)} %get-tuple-element.30.refs_2_), custom_call_target="tpu_custom_call" | custom-call | flops 469762048 | bytes 2359296 | tf_op jit(solution)/shard_map/pallas_call | solution.py:166
  32.5 1.7 %collective-permute-done.6.refs_2_ = bf16[4,256,256]{2,1,0:T(8,128)(2,1)S(1)} collective-permute-done((bf16[4,256,256]{2,1,0:T(8,128)(2,1)S(1)}, bf16[4,256,256]{2,1,0:T(8,128)(2,1)S(1)}, u32[]{:S(2)}, u32[]{:S(2)}) %collective-permute-start.6) | collective-permute-done | bytes 524320 | tf_op jit(solution)/shard_map/ppermute | solution.py:36
  34.1 2.2 %shard_map.80 = (f32[2,448,256]{2,1,0:T(8,128)S(1)}, f32[8,128]{1,0:T(8,128)}) custom-call(s32[39]{0:T(128)S(1)} %fusion.2.refs_5_.places, bf16[2,448,4096]{2,1,0:T(8,128)(2,1)S(1)} %shard_map.76.refs_0_, bf16[4,256,256]{2,1,0:T(8,128)(2,1)S(1)} %shard_map.79.refs_1_, bf16[4,256,256]{2,1,0:T(8,128)(2,1)S(1)} %collective-permute-done.6.refs_2_, ...), custom_call_target="tpu_custom_call" | custom-call | flops 939524096 | bytes 4718592 | tf_op jit(solution)/shard_map/pallas_call | solution.py:166
  36.3 1.2 %shard_map.84 = (f32[2,112,256]{2,1,0:T(8,128)S(1)}, bf16[2,112,256]{2,1,0:T(8,128)(2,1)S(1)}, bf16[2,112,256]{2,1,0:T(8,128)(2,1)S(1)}, bf16[2,112,256]{2,1,0:T(8,128)(2,1)S(1)}) custom-call(s32[39]{0:T(128)S(1)} %fusion.2.refs_5_.places, bf16[2,448,4096]{2,1,0:T(8,128)(2,1)S(1)} %shard_map.76.refs_0_, ...), custom_call_target="tpu_custom_call" | custom-call | flops 469762048 | bytes 2359296 | tf_op jit(solution)/shard_map/pallas_call | solution.py:166
  37.6 2.8 %collective-permute-start.9 = (bf16[2,112,256]{2,1,0:T(8,128)(2,1)S(1)}, bf16[2,112,256]{2,1,0:T(8,128)(2,1)S(1)}, u32[]{:S(2)}, u32[]{:S(2)}) collective-permute-start(bf16[2,112,256]{2,1,0:T(8,128)(2,1)S(1)} %get-tuple-element.34), channel_id=1, source_target_pairs={{0,96},{1,97},{2,98},{3,99},{4,100},{5,101},{6,102},{7,103},{8,104... | collective-permute-start | bytes 344072 | tf_op jit(solution)/shard_map/ppermute | solution.py:36
  40.4 0.4 collective-permute-start.10
  40.7 0.7 collective-permute-start.8
  41.4 1.7 %shard_map.85 = (f32[2,112,256]{2,1,0:T(8,128)S(1)}, bf16[2,112,256]{2,1,0:T(8,128)(2,1)S(1)}, bf16[2,112,256]{2,1,0:T(8,128)(2,1)S(1)}, bf16[2,112,256]{2,1,0:T(8,128)(2,1)S(1)}) custom-call(s32[39]{0:T(128)S(1)} %fusion.2.refs_5_.places, bf16[2,448,4096]{2,1,0:T(8,128)(2,1)S(1)} %shard_map.76.refs_0_, ...), custom_call_target="tpu_custom_call" | custom-call | flops 939524096 | bytes 4718592 | tf_op jit(solution)/shard_map/pallas_call | solution.py:166
  43.1 1.7 %collective-permute-start.14 = (bf16[2,112,256]{2,1,0:T(8,128)(2,1)S(1)}, bf16[2,112,256]{2,1,0:T(8,128)(2,1)S(1)}, u32[]{:S(2)}, u32[]{:S(2)}) collective-permute-start(bf16[2,112,256]{2,1,0:T(8,128)(2,1)S(1)} %get-tuple-element.38), channel_id=1, source_target_pairs={{0,32},{1,33},{2,34},{3,35},{4,36},{5,37},{6,38},{7,39},{8,40},{9,... | collective-permute-start | bytes 344072 | tf_op jit(solution)/shard_map/ppermute | solution.py:36
  44.8 1.1 %collective-permute-start.15 = (bf16[2,112,256]{2,1,0:T(8,128)(2,1)S(1)}, bf16[2,112,256]{2,1,0:T(8,128)(2,1)S(1)}, u32[]{:S(2)}, u32[]{:S(2)}) collective-permute-start(bf16[2,112,256]{2,1,0:T(8,128)(2,1)S(1)} %get-tuple-element.39), channel_id=1, source_target_pairs={{0,96},{1,97},{2,98},{3,99},{4,100},{5,101},{6,102},{7,103},{8,104... | collective-permute-start | bytes 344072 | tf_op jit(solution)/shard_map/ppermute | solution.py:36
  46.0 0.9 %collective-permute-start.16 = (bf16[2,112,256]{2,1,0:T(8,128)(2,1)S(1)}, bf16[2,112,256]{2,1,0:T(8,128)(2,1)S(1)}, u32[]{:S(2)}, u32[]{:S(2)}) collective-permute-start(bf16[2,112,256]{2,1,0:T(8,128)(2,1)S(1)} %get-tuple-element.40), channel_id=1, source_target_pairs={{0,64},{1,65},{2,66},{3,67},{4,68},{5,69},{6,70},{7,71},{8,72},{9,... | collective-permute-start | bytes 344072 | tf_op jit(solution)/shard_map/ppermute | solution.py:36
  46.9 4.1 %collective-permute-start.22 = (bf16[4,256,512]{2,1,0:T(8,128)(2,1)S(1)}, bf16[4,256,512]{2,1,0:T(8,128)(2,1)S(1)}, u32[]{:S(2)}, u32[]{:S(2)}) collective-permute-start(bf16[4,256,512]{2,1,0:T(8,128)(2,1)S(1)} %shard_map.88), channel_id=1, source_target_pairs={{0,16},{1,17},{2,18},{3,19},{4,20},{5,21},{6,22},{7,23},{8,24},{9,... | collective-permute-start | bytes 3145736 | tf_op jit(solution)/shard_map/ppermute | solution.py:36
  51.0 3.2 %collective-permute-start.11 = (bf16[112,256]{1,0:T(8,128)(2,1)S(1)}, bf16[112,256]{1,0:T(8,128)(2,1)S(1)}, u32[]{:S(2)}, u32[]{:S(2)}) collective-permute-start(bf16[112,256]{1,0:T(8,128)(2,1)S(1)} %fusion), channel_id=1, source_target_pairs={{0,128},{1,129},{2,130},{3,131},{4,132},{5,133},{6,134},{7,135},{8... | collective-permute-start | bytes 172040 | tf_op jit(solution)/shard_map/ppermute | solution.py:36
  54.3 4.6 %collective-permute-start.17 = (bf16[112,256]{1,0:T(8,128)(2,1)S(1)}, bf16[112,256]{1,0:T(8,128)(2,1)S(1)}, u32[]{:S(2)}, u32[]{:S(2)}) collective-permute-start(bf16[112,256]{1,0:T(8,128)(2,1)S(1)} %fusion.1), channel_id=1, source_target_pairs={{0,128},{1,129},{2,130},{3,131},{4,132},{5,133},{6,134},{7,135},{8... | collective-permute-start | bytes 172040 | tf_op jit(solution)/shard_map/ppermute | solution.py:36
  59.0 2.8 %collective-permute-done.17 = bf16[112,256]{1,0:T(8,128)(2,1)S(1)} collective-permute-done((bf16[112,256]{1,0:T(8,128)(2,1)S(1)}, bf16[112,256]{1,0:T(8,128)(2,1)S(1)}, u32[]{:S(2)}, u32[]{:S(2)}) %collective-permute-start.17) | collective-permute-done | bytes 57376 | tf_op jit(solution)/shard_map/ppermute | solution.py:36
  61.8 0.6 shard_map.86
  62.4 3.6 %collective-permute-start.18 = (f32[56,512]{1,0:T(8,128)S(1)}, f32[56,512]{1,0:T(8,128)S(1)}, u32[]{:S(2)}, u32[]{:S(2)}) collective-permute-start(f32[56,512]{1,0:T(8,128)S(1)} %get-tuple-element.42), channel_id=1, source_target_pairs={{0,16},{1,17},{2,18},{3,19},{4,20},{5,21},{6,22},{7,23},{8,24},{9,... | collective-permute-start | bytes 344072 | tf_op jit(solution)/shard_map/ppermute | solution.py:36
  66.0 0.9 %collective-permute-done.18.other = f32[56,512]{1,0:T(8,128)S(1)} collective-permute-done((f32[56,512]{1,0:T(8,128)S(1)}, f32[56,512]{1,0:T(8,128)S(1)}, u32[]{:S(2)}, u32[]{:S(2)}) %collective-permute-start.18) | collective-permute-done | bytes 114720 | tf_op jit(solution)/shard_map/ppermute | solution.py:36
  66.9 0.7 shard_map.87.after
  67.7 2.2 %collective-permute-start.21 = (bf16[56,1024]{1,0:T(8,128)(2,1)S(1)}, bf16[56,1024]{1,0:T(8,128)(2,1)S(1)}, u32[]{:S(2)}, u32[]{:S(2)}) collective-permute-start(bf16[56,1024]{1,0:T(8,128)(2,1)S(1)} %shard_map.87.after), channel_id=1, source_target_pairs={{0,2},{1,3},{2,0},{3,1},{4,6},{5,7},{6,4},{7,5},{8,10},{9,11},{10,... | collective-permute-start | bytes 344072 | tf_op jit(solution)/shard_map/ppermute | solution.py:36
  69.9 0.5 collective-permute-start.20
  70.4 2.1 %collective-permute-start.19 = (bf16[56,1024]{1,0:T(8,128)(2,1)S(1)}, bf16[56,1024]{1,0:T(8,128)(2,1)S(1)}, u32[]{:S(2)}, u32[]{:S(2)}) collective-permute-start(bf16[56,1024]{1,0:T(8,128)(2,1)S(1)} %shard_map.87.after), channel_id=1, source_target_pairs={{0,3},{1,0},{2,1},{3,2},{4,7},{5,4},{6,5},{7,6},{8,11},{9,8},{10,9... | collective-permute-start | bytes 344072 | tf_op jit(solution)/shard_map/ppermute | solution.py:36
  72.6 1.4 %shard_map.90 = (f32[1,56,1024]{2,1,0:T(8,128)}, f32[1,56,1024]{2,1,0:T(8,128)}) custom-call(s32[39]{0:T(128)S(1)} %fusion.2.refs_5_.places, f32[56,512]{1,0:T(8,128)S(1)} %get-tuple-element.41.mine, f32[56,512]{1,0:T(8,128)S(1)} %collective-permute-done.18.other, f32[1,56,1024]{2,1,0:T(8,128)S(1)} %copy-done.1, f32[1,56,1024]{2,1,0:T(8,128)S(1)} %copy-done.2, ...), custom_call_target="tpu_custom_call" | custom-call | tf_op jit(solution)/shard_map/pallas_call | solution.py:363
  74.0 0.7 collective-permute-done.20
  75.0 0.3 convolution_convert_fusion
  75.3 0.3 convolution_convert_fusion.1
  75.7 0.3 convolution_convert_fusion.2
  76.1 3.3 %collective-permute-start.24 = (bf16[224,256]{1,0:T(8,128)(2,1)S(1)}, bf16[224,256]{1,0:T(8,128)(2,1)S(1)}, u32[]{:S(2)}, u32[]{:S(2)}) collective-permute-start(bf16[224,256]{1,0:T(8,128)(2,1)S(1)} %convolution_convert_fusion.1), channel_id=1, source_target_pairs={{0,12},{1,13},{2,14},{3,15},{4,0},{5,1},{6,2},{7,3},{8,4},{9,5},{1... | collective-permute-start | bytes 344072 | tf_op jit(solution)/shard_map/ppermute | solution.py:36
  79.4 0.3 convolution_convert_fusion.3
  79.7 1.8 %collective-permute-done.23 = bf16[224,256]{1,0:T(8,128)(2,1)S(1)} collective-permute-done((bf16[224,256]{1,0:T(8,128)(2,1)S(1)}, bf16[224,256]{1,0:T(8,128)(2,1)S(1)}, u32[]{:S(2)}, u32[]{:S(2)}) %collective-permute-start.23) | collective-permute-done | bytes 114720 | tf_op jit(solution)/shard_map/ppermute | solution.py:36
  81.5 3.6 %collective-permute-done.25 = bf16[224,256]{1,0:T(8,128)(2,1)S(1)} collective-permute-done((bf16[224,256]{1,0:T(8,128)(2,1)S(1)}, bf16[224,256]{1,0:T(8,128)(2,1)S(1)}, u32[]{:S(2)}, u32[]{:S(2)}) %collective-permute-start.25) | collective-permute-done | bytes 114720 | tf_op jit(solution)/shard_map/ppermute | solution.py:36
  85.1 1.3 %shard_map.89 = bf16[16,56,256]{2,1,0:T(8,128)(2,1)} custom-call(s32[39]{0:T(128)S(1)} %fusion.2.refs_5_.places, bf16[4,56,256]{2,1,0:T(8,128)(2,1)S(1)} %bitcast.47, bf16[4,56,256]{2,1,0:T(8,128)(2,1)S(1)} %bitcast.44, bf16[4,56,256]{2,1,0:T(8,128)(2,1)S(1)} %bitcast.45, bf16[4,56,256]{2,1,0:T(8,128)(2,1)S(1)} %bitcast.46), custom_call_target="tpu_custom_call" | custom-call | tf_op jit(solution)/shard_map/pallas_call | solution.py:383
  (44 shorter events, 0.7 us)
Async XLA Ops:
  0.6 15.2 %collective-permute-start = (bf16[2,448,4096]{2,1,0:T(8,128)(2,1)}, bf16[2,448,4096]{2,1,0:T(8,128)(2,1)}, u32[]{:S(2)}, u32[]{:S(2)}) collective-permute-start(bf16[2,448,4096]{2,1,0:T(8,128)(2,1)} %bitcast.41), channel_id=1, source_target_pairs={{0,16},{1,17},{2,18},{3,19},{4,20},{5,21},{6,22},{7,23},{8,24},{9,... | collective-permute-start | bytes 22020104 | tf_op jit(solution)/shard_map/ppermute | solution.py:36
  5.0 7.7 %collective-permute-start.3 = (bf16[2,256,256]{2,1,0:T(8,128)(2,1)S(1)}, bf16[2,256,256]{2,1,0:T(8,128)(2,1)S(1)}, u32[]{:S(2)}, u32[]{:S(2)}) collective-permute-start(bf16[2,256,256]{2,1,0:T(8,128)(2,1)S(1)} %pad_maximum_fusion.1.refs_0_), channel_id=1, source_target_pairs={{0,8},{1,9},{2,10},{3,11},{4,12},{5,13},{6,14},{7,15},{8,0},{9,1},... | collective-permute-start | bytes 786440 | tf_op jit(solution)/shard_map/ppermute | solution.py:36
  9.3 6.4 %collective-permute-start.2 = (bf16[2,256,256]{2,1,0:T(8,128)(2,1)S(1)}, bf16[2,256,256]{2,1,0:T(8,128)(2,1)S(1)}, u32[]{:S(2)}, u32[]{:S(2)}) collective-permute-start(bf16[2,256,256]{2,1,0:T(8,128)(2,1)S(1)} %pad_maximum_fusion.1.refs_0_), channel_id=1, source_target_pairs={{0,4},{1,5},{2,6},{3,7},{4,8},{5,9},{6,10},{7,11},{8,12},{9,13},{1... | collective-permute-start | bytes 786440 | tf_op jit(solution)/shard_map/ppermute | solution.py:36
  9.3 6.4 %collective-permute-start.1 = (bf16[2,256,256]{2,1,0:T(8,128)(2,1)S(1)}, bf16[2,256,256]{2,1,0:T(8,128)(2,1)S(1)}, u32[]{:S(2)}, u32[]{:S(2)}) collective-permute-start(bf16[2,256,256]{2,1,0:T(8,128)(2,1)S(1)} %pad_maximum_fusion.1.refs_0_), channel_id=1, source_target_pairs={{0,12},{1,13},{2,14},{3,15},{4,0},{5,1},{6,2},{7,3},{8,4},{9,5},{1... | collective-permute-start | bytes 786440 | tf_op jit(solution)/shard_map/ppermute | solution.py:36
  15.8 3.4 %copy-start = (bf16[1,16,56,4096]{3,2,1,0:T(8,128)(2,1)S(1)}, bf16[1,16,56,4096]{3,2,1,0:T(8,128)(2,1)}, u32[]{:S(2)}) copy-start(bf16[1,16,56,4096]{3,2,1,0:T(8,128)(2,1)} %param.5) | copy-start | bytes 22020100
  16.4 8.7 %collective-permute-start.4 = (bf16[4,256,256]{2,1,0:T(8,128)(2,1)S(1)}, bf16[4,256,256]{2,1,0:T(8,128)(2,1)S(1)}, u32[]{:S(2)}, u32[]{:S(2)}) collective-permute-start(bf16[4,256,256]{2,1,0:T(8,128)(2,1)S(1)} %get-tuple-element.24.refs_1_.refs_0_), channel_id=1, source_target_pairs={{0,131},{1,0},{2,1},{3,2},{4,135},{5,4},{6,5},{7,6},{8,139},{9,8},... | collective-permute-start | bytes 1572872 | tf_op jit(solution)/shard_map/ppermute | solution.py:36
  19.0 11.0 %collective-permute-start.7 = (bf16[4,256,256]{2,1,0:T(8,128)(2,1)S(1)}, bf16[4,256,256]{2,1,0:T(8,128)(2,1)S(1)}, u32[]{:S(2)}, u32[]{:S(2)}) collective-permute-start(bf16[4,256,256]{2,1,0:T(8,128)(2,1)S(1)} %get-tuple-element.28.refs_1_.refs_4_), channel_id=1, source_target_pairs={{0,1},{1,2},{2,3},{3,128},{4,5},{5,6},{6,7},{7,132},{8,9},{9,10},{... | collective-permute-start | bytes 1572872 | tf_op jit(solution)/shard_map/ppermute | solution.py:36
  19.0 15.2 %collective-permute-start.6 = (bf16[4,256,256]{2,1,0:T(8,128)(2,1)S(1)}, bf16[4,256,256]{2,1,0:T(8,128)(2,1)S(1)}, u32[]{:S(2)}, u32[]{:S(2)}) collective-permute-start(bf16[4,256,256]{2,1,0:T(8,128)(2,1)S(1)} %get-tuple-element.24.refs_1_.refs_0_), channel_id=1, source_target_pairs={{0,1},{1,2},{2,3},{3,128},{4,5},{5,6},{6,7},{7,132},{8,9},{9,10},{... | collective-permute-start | bytes 1572872 | tf_op jit(solution)/shard_map/ppermute | solution.py:36
  25.1 11.3 %collective-permute-start.5 = (bf16[4,256,256]{2,1,0:T(8,128)(2,1)S(1)}, bf16[4,256,256]{2,1,0:T(8,128)(2,1)S(1)}, u32[]{:S(2)}, u32[]{:S(2)}) collective-permute-start(bf16[4,256,256]{2,1,0:T(8,128)(2,1)S(1)} %shard_map.79.refs_1_), channel_id=1, source_target_pairs={{0,131},{1,0},{2,1},{3,2},{4,135},{5,4},{6,5},{7,6},{8,139},{9,8},... | collective-permute-start | bytes 1572872 | tf_op jit(solution)/shard_map/ppermute | solution.py:36
  28.5 12.9 %collective-permute-start.12 = (bf16[4,256,256]{2,1,0:T(8,128)(2,1)S(1)}, bf16[4,256,256]{2,1,0:T(8,128)(2,1)S(1)}, u32[]{:S(2)}, u32[]{:S(2)}) collective-permute-start(bf16[4,256,256]{2,1,0:T(8,128)(2,1)S(1)} %get-tuple-element.28.refs_1_.refs_4_), channel_id=1, source_target_pairs={{0,131},{1,0},{2,1},{3,2},{4,135},{5,4},{6,5},{7,6},{8,139},{9,8},... | collective-permute-start | bytes 1572872 | tf_op jit(solution)/shard_map/ppermute | solution.py:36
  30.0 11.4 %collective-permute-start.13 = (bf16[4,256,256]{2,1,0:T(8,128)(2,1)S(1)}, bf16[4,256,256]{2,1,0:T(8,128)(2,1)S(1)}, u32[]{:S(2)}, u32[]{:S(2)}) collective-permute-start(bf16[4,256,256]{2,1,0:T(8,128)(2,1)S(1)} %shard_map.82.refs_1_.refs_6_), channel_id=1, source_target_pairs={{0,1},{1,2},{2,3},{3,128},{4,5},{5,6},{6,7},{7,132},{8,9},{9,10},{... | collective-permute-start | bytes 1572872 | tf_op jit(solution)/shard_map/ppermute | solution.py:36
  37.6 8.4 %collective-permute-start.9 = (bf16[2,112,256]{2,1,0:T(8,128)(2,1)S(1)}, bf16[2,112,256]{2,1,0:T(8,128)(2,1)S(1)}, u32[]{:S(2)}, u32[]{:S(2)}) collective-permute-start(bf16[2,112,256]{2,1,0:T(8,128)(2,1)S(1)} %get-tuple-element.34), channel_id=1, source_target_pairs={{0,96},{1,97},{2,98},{3,99},{4,100},{5,101},{6,102},{7,103},{8,104... | collective-permute-start | bytes 344072 | tf_op jit(solution)/shard_map/ppermute | solution.py:36
  40.4 6.5 %collective-permute-start.10 = (bf16[2,112,256]{2,1,0:T(8,128)(2,1)S(1)}, bf16[2,112,256]{2,1,0:T(8,128)(2,1)S(1)}, u32[]{:S(2)}, u32[]{:S(2)}) collective-permute-start(bf16[2,112,256]{2,1,0:T(8,128)(2,1)S(1)} %get-tuple-element.35), channel_id=1, source_target_pairs={{0,64},{1,65},{2,66},{3,67},{4,68},{5,69},{6,70},{7,71},{8,72},{9,... | collective-permute-start | bytes 344072 | tf_op jit(solution)/shard_map/ppermute | solution.py:36
  40.7 10.2 %collective-permute-start.8 = (bf16[2,112,256]{2,1,0:T(8,128)(2,1)S(1)}, bf16[2,112,256]{2,1,0:T(8,128)(2,1)S(1)}, u32[]{:S(2)}, u32[]{:S(2)}) collective-permute-start(bf16[2,112,256]{2,1,0:T(8,128)(2,1)S(1)} %get-tuple-element.33.refs_4_), channel_id=1, source_target_pairs={{0,32},{1,33},{2,34},{3,35},{4,36},{5,37},{6,38},{7,39},{8,40},{9,... | collective-permute-start | bytes 344072 | tf_op jit(solution)/shard_map/ppermute | solution.py:36
  43.1 11.1 %collective-permute-start.14 = (bf16[2,112,256]{2,1,0:T(8,128)(2,1)S(1)}, bf16[2,112,256]{2,1,0:T(8,128)(2,1)S(1)}, u32[]{:S(2)}, u32[]{:S(2)}) collective-permute-start(bf16[2,112,256]{2,1,0:T(8,128)(2,1)S(1)} %get-tuple-element.38), channel_id=1, source_target_pairs={{0,32},{1,33},{2,34},{3,35},{4,36},{5,37},{6,38},{7,39},{8,40},{9,... | collective-permute-start | bytes 344072 | tf_op jit(solution)/shard_map/ppermute | solution.py:36
  44.8 9.4 %collective-permute-start.15 = (bf16[2,112,256]{2,1,0:T(8,128)(2,1)S(1)}, bf16[2,112,256]{2,1,0:T(8,128)(2,1)S(1)}, u32[]{:S(2)}, u32[]{:S(2)}) collective-permute-start(bf16[2,112,256]{2,1,0:T(8,128)(2,1)S(1)} %get-tuple-element.39), channel_id=1, source_target_pairs={{0,96},{1,97},{2,98},{3,99},{4,100},{5,101},{6,102},{7,103},{8,104... | collective-permute-start | bytes 344072 | tf_op jit(solution)/shard_map/ppermute | solution.py:36
  45.9 21.0 %copy-start.1 = (f32[1,56,1024]{2,1,0:T(8,128)S(1)}, f32[1,56,1024]{2,1,0:T(8,128)}, u32[]{:S(2)}) copy-start(f32[1,56,1024]{2,1,0:T(8,128)} %first.3) | copy-start | bytes 688132
  46.0 21.0 %copy-start.2 = (f32[1,56,1024]{2,1,0:T(8,128)S(1)}, f32[1,56,1024]{2,1,0:T(8,128)}, u32[]{:S(2)}) copy-start(f32[1,56,1024]{2,1,0:T(8,128)} %second.3) | copy-start | bytes 688132
  46.0 8.3 %collective-permute-start.16 = (bf16[2,112,256]{2,1,0:T(8,128)(2,1)S(1)}, bf16[2,112,256]{2,1,0:T(8,128)(2,1)S(1)}, u32[]{:S(2)}, u32[]{:S(2)}) collective-permute-start(bf16[2,112,256]{2,1,0:T(8,128)(2,1)S(1)} %get-tuple-element.40), channel_id=1, source_target_pairs={{0,64},{1,65},{2,66},{3,67},{4,68},{5,69},{6,70},{7,71},{8,72},{9,... | collective-permute-start | bytes 344072 | tf_op jit(solution)/shard_map/ppermute | solution.py:36
  46.9 27.9 %collective-permute-start.22 = (bf16[4,256,512]{2,1,0:T(8,128)(2,1)S(1)}, bf16[4,256,512]{2,1,0:T(8,128)(2,1)S(1)}, u32[]{:S(2)}, u32[]{:S(2)}) collective-permute-start(bf16[4,256,512]{2,1,0:T(8,128)(2,1)S(1)} %shard_map.88), channel_id=1, source_target_pairs={{0,16},{1,17},{2,18},{3,19},{4,20},{5,21},{6,22},{7,23},{8,24},{9,... | collective-permute-start | bytes 3145736 | tf_op jit(solution)/shard_map/ppermute | solution.py:36
  51.0 7.9 %collective-permute-start.11 = (bf16[112,256]{1,0:T(8,128)(2,1)S(1)}, bf16[112,256]{1,0:T(8,128)(2,1)S(1)}, u32[]{:S(2)}, u32[]{:S(2)}) collective-permute-start(bf16[112,256]{1,0:T(8,128)(2,1)S(1)} %fusion), channel_id=1, source_target_pairs={{0,128},{1,129},{2,130},{3,131},{4,132},{5,133},{6,134},{7,135},{8... | collective-permute-start | bytes 172040 | tf_op jit(solution)/shard_map/ppermute | solution.py:36
  54.3 7.4 %collective-permute-start.17 = (bf16[112,256]{1,0:T(8,128)(2,1)S(1)}, bf16[112,256]{1,0:T(8,128)(2,1)S(1)}, u32[]{:S(2)}, u32[]{:S(2)}) collective-permute-start(bf16[112,256]{1,0:T(8,128)(2,1)S(1)} %fusion.1), channel_id=1, source_target_pairs={{0,128},{1,129},{2,130},{3,131},{4,132},{5,133},{6,134},{7,135},{8... | collective-permute-start | bytes 172040 | tf_op jit(solution)/shard_map/ppermute | solution.py:36
  62.4 4.6 %collective-permute-start.18 = (f32[56,512]{1,0:T(8,128)S(1)}, f32[56,512]{1,0:T(8,128)S(1)}, u32[]{:S(2)}, u32[]{:S(2)}) collective-permute-start(f32[56,512]{1,0:T(8,128)S(1)} %get-tuple-element.42), channel_id=1, source_target_pairs={{0,16},{1,17},{2,18},{3,19},{4,20},{5,21},{6,22},{7,23},{8,24},{9,... | collective-permute-start | bytes 344072 | tf_op jit(solution)/shard_map/ppermute | solution.py:36
  67.7 6.3 %collective-permute-start.21 = (bf16[56,1024]{1,0:T(8,128)(2,1)S(1)}, bf16[56,1024]{1,0:T(8,128)(2,1)S(1)}, u32[]{:S(2)}, u32[]{:S(2)}) collective-permute-start(bf16[56,1024]{1,0:T(8,128)(2,1)S(1)} %shard_map.87.after), channel_id=1, source_target_pairs={{0,2},{1,3},{2,0},{3,1},{4,6},{5,7},{6,4},{7,5},{8,10},{9,11},{10,... | collective-permute-start | bytes 344072 | tf_op jit(solution)/shard_map/ppermute | solution.py:36
  69.9 4.9 %collective-permute-start.20 = (bf16[56,1024]{1,0:T(8,128)(2,1)S(1)}, bf16[56,1024]{1,0:T(8,128)(2,1)S(1)}, u32[]{:S(2)}, u32[]{:S(2)}) collective-permute-start(bf16[56,1024]{1,0:T(8,128)(2,1)S(1)} %shard_map.87.after), channel_id=1, source_target_pairs={{0,1},{1,2},{2,3},{3,0},{4,5},{5,6},{6,7},{7,4},{8,9},{9,10},{10,1... | collective-permute-start | bytes 344072 | tf_op jit(solution)/shard_map/ppermute | solution.py:36
  70.4 4.3 %collective-permute-start.19 = (bf16[56,1024]{1,0:T(8,128)(2,1)S(1)}, bf16[56,1024]{1,0:T(8,128)(2,1)S(1)}, u32[]{:S(2)}, u32[]{:S(2)}) collective-permute-start(bf16[56,1024]{1,0:T(8,128)(2,1)S(1)} %shard_map.87.after), channel_id=1, source_target_pairs={{0,3},{1,0},{2,1},{3,2},{4,7},{5,4},{6,5},{7,6},{8,11},{9,8},{10,9... | collective-permute-start | bytes 344072 | tf_op jit(solution)/shard_map/ppermute | solution.py:36
  76.0 5.5 %collective-permute-start.23 = (bf16[224,256]{1,0:T(8,128)(2,1)S(1)}, bf16[224,256]{1,0:T(8,128)(2,1)S(1)}, u32[]{:S(2)}, u32[]{:S(2)}) collective-permute-start(bf16[224,256]{1,0:T(8,128)(2,1)S(1)} %convolution_convert_fusion.2), channel_id=1, source_target_pairs={{0,4},{1,5},{2,6},{3,7},{4,8},{5,9},{6,10},{7,11},{8,12},{9,13},{1... | collective-permute-start | bytes 344072 | tf_op jit(solution)/shard_map/ppermute | solution.py:36
  76.1 5.4 %collective-permute-start.24 = (bf16[224,256]{1,0:T(8,128)(2,1)S(1)}, bf16[224,256]{1,0:T(8,128)(2,1)S(1)}, u32[]{:S(2)}, u32[]{:S(2)}) collective-permute-start(bf16[224,256]{1,0:T(8,128)(2,1)S(1)} %convolution_convert_fusion.1), channel_id=1, source_target_pairs={{0,12},{1,13},{2,14},{3,15},{4,0},{5,1},{6,2},{7,3},{8,4},{9,5},{1... | collective-permute-start | bytes 344072 | tf_op jit(solution)/shard_map/ppermute | solution.py:36
  79.4 5.8 %collective-permute-start.25 = (bf16[224,256]{1,0:T(8,128)(2,1)S(1)}, bf16[224,256]{1,0:T(8,128)(2,1)S(1)}, u32[]{:S(2)}, u32[]{:S(2)}) collective-permute-start(bf16[224,256]{1,0:T(8,128)(2,1)S(1)} %convolution_convert_fusion), channel_id=1, source_target_pairs={{0,8},{1,9},{2,10},{3,11},{4,12},{5,13},{6,14},{7,15},{8,0},{9,1},... | collective-permute-start | bytes 344072 | tf_op jit(solution)/shard_map/ppermute | solution.py:36

commit v5 on v4

--- a/solution.py
+++ b/solution.py
@@ -370,6 +370,41 @@
     return new_first, new_second, direction
 
 
+def back_kernel(indices, rows, *refs):
+    rights, outs = refs[: -len(indices)], refs[-len(indices) :]
+    for i, out in zip(indices, outs):
+        at, value = 0, None
+        for right in rights:
+            width = right.shape[2]
+            term = lax.dot_general(
+                rows[:, at : at + width],
+                right[i],
+                (((1,), (1,)), ((), ())),
+                preferred_element_type=jnp.float32,
+            )
+            value = term if value is None else value + term
+            at += width
+        out[...] = value.astype(out.dtype)
+
+
+def back(indices, rows, rights):
+    depth = rights[0].shape[1]
+    whole = pl.BlockSpec(memory_space=pltpu.VMEM)
+    return pl.pallas_call(
+        functools.partial(back_kernel, indices),
+        out_shape=[jax.ShapeDtypeStruct((rows.shape[0], depth), rows.dtype)]
+        * len(indices),
+        in_specs=[whole] * (1 + len(rights)),
+        out_specs=[whole] * len(indices),
+        compiler_params=pltpu.CompilerParams(vmem_limit_bytes=7 * 1024 * 1024),
+        cost_estimate=pl.CostEstimate(
+            flops=2 * len(indices) * rows.size * depth,
+            bytes_accessed=4 * len(indices) * rows.shape[1] * depth,
+            transcendentals=0,
+        ),
+    )(rows, *rights)
+
+
 def place_kernel(places, *refs):
     pieces, out = refs[:-1], refs[-1]
     for i, piece in enumerate(pieces):
@@ -453,7 +488,6 @@
     basis_other = move(
         collect(list(zip(stacks, ahead, behind, far))), other_core
     )
-    basis = jnp.concatenate([*stacks, basis_other], axis=2)
     gathered = jnp.stack(
         [direction]
         + [
@@ -461,17 +495,13 @@
             for o in OFFSETS[1:]
         ]
     ).reshape(4 * owned, rank_cols)
-    pieces = []
-    for i, offset in enumerate(OFFSETS):
-        value = lax.dot_general(
-            gathered,
-            basis[i],
-            (((1,), (1,)), ((), ())),
-            preferred_element_type=jnp.float32,
-        ).astype(jnp.bfloat16)
-        if offset:
-            value = move(value, by_core(along_x(offset), along_line(offset)))
-        pieces.append(value.reshape(4, owned, depth))
+    rights = [*stacks, basis_other]
+    sent = back((1, 2, 3), gathered, rights)
+    values = list(back((0,), gathered, rights)) + [
+        move(value, by_core(along_x(offset), along_line(offset)))
+        for offset, value in zip(OFFSETS[1:], sent)
+    ]
+    pieces = [value.reshape(4, owned, depth) for value in values]
     result = place_rows(places, pieces)
     update = result.reshape(1, X * ZL * owned, depth)
     return (update, new_first, new_second)

time: 86.7 us -> 86.1 us (level)
  matrix products: 1.36 us -> 0 us
  Pallas kernels: 17.8 us -> 18.7 us
    dot_general x4 -> x0, matrix products: 1.36 us -> none  [per_device(): lax.dot_general(gathered, basis[i], (((1,), (1,)), ((), ())), preferred_e...]
    pallas_call x0 -> x2, Pallas kernels: none -> 0.96 us  [back(): pl.pallas_call(functools.partial(back_kernel, indices), out_shape=[jax.Sh...]
  transfers between devices with their start and end apart: 26 -> 26, of which waited for: 8 -> 9; matrix products, arithmetic and copies ran while one was open for 3% -> 2% of each run, Pallas kernels for 18% -> 19%
where the time goes in v5:
time: 86.1 us; the launch traced here: 85.9 us
  starting transfers between devices  49.3 us (57%)
  Pallas kernels  18.7 us (22%)
  waiting for transfers between devices  15 us (17%)
  local copies, waits for them, and re-layouts  1.88 us (2%)
    ppermute x26, starting transfers between devices, move(): return lax.ppermute(value, AXES, pairs)  49.3 us
    ppermute x26, waiting for transfers between devices, move(): return lax.ppermute(value, AXES, pairs)  15 us
    pallas_call x6, Pallas kernels, project(): pl.pallas_call(functools.partial(project_kernel, outers, last, acc is not...  8.68 us
    pallas_call x1, Pallas kernels, add(): pl.pallas_call(add_kernel, out_shape=jax.ShapeDtypeStruct(first.shape, fi...  4.37 us
  transfers between devices with their start and end apart: 26, of which 9 were waited for; matrix products, arithmetic and copies ran while one was open for 2% of the time, Pallas kernels for 19%

profile of v5, /device:TPU:1, one launch (start us, length us, event | category | flops | bytes accessed | tf_op | source)
XLA Modules:
  0.0 85.9 jit_solution(10177167322211860322)
XLA Ops:
  0.6 3.3 %collective-permute-start = (bf16[2,448,4096]{2,1,0:T(8,128)(2,1)}, bf16[2,448,4096]{2,1,0:T(8,128)(2,1)}, u32[]{:S(2)}, u32[]{:S(2)}) collective-permute-start(bf16[2,448,4096]{2,1,0:T(8,128)(2,1)} %bitcast.25), channel_id=1, source_target_pairs={{0,16},{1,17},{2,18},{3,19},{4,20},{5,21},{6,22},{7,23},{8,24},{9,... | collective-permute-start | bytes 22020104 | tf_op jit(solution)/shard_map/ppermute | solution.py:36
  4.0 1.0 %dynamic-slice_bitcast_fusion.1 = (bf16[1,256,256]{2,1,0:T(8,128)(2,1)S(1)}, bf16[1,256,256]{2,1,0:T(8,128)(2,1)S(1)}) fusion(bf16[256,1024]{1,0:T(8,128)(2,1)} %param.6, s32[]{:T(128)S(6)} %select_n.16, s32[]{:T(128)S(6)} %add.42), kind=kLoop, calls=%fused_computation.5 | loop fusion | bytes 524296 | tf_op jit(solution)/shard_map/stack | solution.py:446
  5.0 4.4 %collective-permute-start.3 = (bf16[2,256,256]{2,1,0:T(8,128)(2,1)S(1)}, bf16[2,256,256]{2,1,0:T(8,128)(2,1)S(1)}, u32[]{:S(2)}, u32[]{:S(2)}) collective-permute-start(bf16[2,256,256]{2,1,0:T(8,128)(2,1)S(1)} %pad_maximum_fusion.1.refs_0_), channel_id=1, source_target_pairs={{0,8},{1,9},{2,10},{3,11},{4,12},{5,13},{6,14},{7,15},{8,0},{9,1},... | collective-permute-start | bytes 786440 | tf_op jit(solution)/shard_map/ppermute | solution.py:36
  9.3 2.7 %collective-permute-start.1 = (bf16[2,256,256]{2,1,0:T(8,128)(2,1)S(1)}, bf16[2,256,256]{2,1,0:T(8,128)(2,1)S(1)}, u32[]{:S(2)}, u32[]{:S(2)}) collective-permute-start(bf16[2,256,256]{2,1,0:T(8,128)(2,1)S(1)} %pad_maximum_fusion.1.refs_0_), channel_id=1, source_target_pairs={{0,12},{1,13},{2,14},{3,15},{4,0},{5,1},{6,2},{7,3},{8,4},{9,5},{1... | collective-permute-start | bytes 786440 | tf_op jit(solution)/shard_map/ppermute | solution.py:36
  12.0 0.8 fusion.2.refs_5_.places
  12.9 2.9 %collective-permute-done.2.refs_2_ = bf16[2,256,256]{2,1,0:T(8,128)(2,1)S(1)} collective-permute-done((bf16[2,256,256]{2,1,0:T(8,128)(2,1)S(1)}, bf16[2,256,256]{2,1,0:T(8,128)(2,1)S(1)}, u32[]{:S(2)}, u32[]{:S(2)}) %collective-permute-start.2) | collective-permute-done | bytes 262176 | tf_op jit(solution)/shard_map/ppermute | solution.py:36
  15.8 0.6 shard_map.77
  16.4 2.6 %collective-permute-start.4 = (bf16[4,256,256]{2,1,0:T(8,128)(2,1)S(1)}, bf16[4,256,256]{2,1,0:T(8,128)(2,1)S(1)}, u32[]{:S(2)}, u32[]{:S(2)}) collective-permute-start(bf16[4,256,256]{2,1,0:T(8,128)(2,1)S(1)} %get-tuple-element.27.refs_1_.refs_0_), channel_id=1, source_target_pairs={{0,131},{1,0},{2,1},{3,2},{4,135},{5,4},{6,5},{7,6},{8,139},{9,8},... | collective-permute-start | bytes 1572872 | tf_op jit(solution)/shard_map/ppermute | solution.py:36
  19.0 0.2 collective-permute-start.6
  19.2 4.4 %shard_map.76.refs_0_ = bf16[2,448,4096]{2,1,0:T(8,128)(2,1)S(1)} custom-call(bf16[2,448,4096]{2,1,0:T(8,128)(2,1)S(1)} %bitcast.26, bf16[2,448,4096]{2,1,0:T(8,128)(2,1)} %collective-permute-done.second.refs_4_), custom_call_target="tpu_custom_call" | custom-call | flops 3670016 | bytes 22020096 | tf_op jit(solution)/shard_map/pallas_call | solution.py:236
  23.5 1.2 %shard_map.78 = (f32[2,448,256]{2,1,0:T(8,128)S(1)}, f32[8,128]{1,0:T(8,128)S(1)}) custom-call(s32[39]{0:T(128)S(1)} %fusion.2.refs_5_.places, bf16[2,448,4096]{2,1,0:T(8,128)(2,1)S(1)} %shard_map.76.refs_0_, bf16[4,256,256]{2,1,0:T(8,128)(2,1)S(1)} %get-tuple-element.27.refs_1_.refs_0_), custom_call_target="tpu_custom_call" | custom-call | flops 469762048 | bytes 2359296 | tf_op jit(solution)/shard_map/pallas_call | solution.py:166
  24.7 0.4 collective-permute-done.4.refs_0_
  25.1 3.4 %collective-permute-start.5 = (bf16[4,256,256]{2,1,0:T(8,128)(2,1)S(1)}, bf16[4,256,256]{2,1,0:T(8,128)(2,1)S(1)}, u32[]{:S(2)}, u32[]{:S(2)}) collective-permute-start(bf16[4,256,256]{2,1,0:T(8,128)(2,1)S(1)} %shard_map.79.refs_1_), channel_id=1, source_target_pairs={{0,131},{1,0},{2,1},{3,2},{4,135},{5,4},{6,5},{7,6},{8,139},{9,8},... | collective-permute-start | bytes 1572872 | tf_op jit(solution)/shard_map/ppermute | solution.py:36
  28.5 0.3 collective-permute-start.12
  28.8 1.2 %shard_map.81 = (f32[2,448,256]{2,1,0:T(8,128)S(1)}, f32[8,128]{1,0:T(8,128)S(1)}) custom-call(s32[39]{0:T(128)S(1)} %fusion.2.refs_5_.places, bf16[2,448,4096]{2,1,0:T(8,128)(2,1)S(1)} %shard_map.76.refs_0_, bf16[4,256,256]{2,1,0:T(8,128)(2,1)S(1)} %get-tuple-element.31.refs_1_.refs_4_), custom_call_target="tpu_custom_call" | custom-call | flops 469762048 | bytes 2359296 | tf_op jit(solution)/shard_map/pallas_call | solution.py:166
  30.0 1.3 %collective-permute-start.13 = (bf16[4,256,256]{2,1,0:T(8,128)(2,1)S(1)}, bf16[4,256,256]{2,1,0:T(8,128)(2,1)S(1)}, u32[]{:S(2)}, u32[]{:S(2)}) collective-permute-start(bf16[4,256,256]{2,1,0:T(8,128)(2,1)S(1)} %shard_map.82.refs_1_.refs_6_), channel_id=1, source_target_pairs={{0,1},{1,2},{2,3},{3,128},{4,5},{5,6},{6,7},{7,132},{8,9},{9,10},{... | collective-permute-start | bytes 1572872 | tf_op jit(solution)/shard_map/ppermute | solution.py:36
  31.3 1.2 %shard_map.83 = (f32[2,448,256]{2,1,0:T(8,128)S(1)}, f32[8,128]{1,0:T(8,128)S(1)}) custom-call(s32[39]{0:T(128)S(1)} %fusion.2.refs_5_.places, bf16[2,448,4096]{2,1,0:T(8,128)(2,1)S(1)} %shard_map.76.refs_0_, bf16[4,256,256]{2,1,0:T(8,128)(2,1)S(1)} %shard_map.82.refs_1_.refs_6_, f32[2,448,256]{2,1,0:T(8,128)S(1)} %get-tuple-element.33.refs_2_), custom_call_target="tpu_custom_call" | custom-call | flops 469762048 | bytes 2359296 | tf_op jit(solution)/shard_map/pallas_call | solution.py:166
  32.5 1.7 %collective-permute-done.6.refs_2_ = bf16[4,256,256]{2,1,0:T(8,128)(2,1)S(1)} collective-permute-done((bf16[4,256,256]{2,1,0:T(8,128)(2,1)S(1)}, bf16[4,256,256]{2,1,0:T(8,128)(2,1)S(1)}, u32[]{:S(2)}, u32[]{:S(2)}) %collective-permute-start.6) | collective-permute-done | bytes 524320 | tf_op jit(solution)/shard_map/ppermute | solution.py:36
  34.1 2.2 %shard_map.80 = (f32[2,448,256]{2,1,0:T(8,128)S(1)}, f32[8,128]{1,0:T(8,128)}) custom-call(s32[39]{0:T(128)S(1)} %fusion.2.refs_5_.places, bf16[2,448,4096]{2,1,0:T(8,128)(2,1)S(1)} %shard_map.76.refs_0_, bf16[4,256,256]{2,1,0:T(8,128)(2,1)S(1)} %shard_map.79.refs_1_, bf16[4,256,256]{2,1,0:T(8,128)(2,1)S(1)} %collective-permute-done.6.refs_2_, ...), custom_call_target="tpu_custom_call" | custom-call | flops 939524096 | bytes 4718592 | tf_op jit(solution)/shard_map/pallas_call | solution.py:166
  36.3 1.2 %shard_map.84 = (f32[2,112,256]{2,1,0:T(8,128)S(1)}, bf16[2,112,256]{2,1,0:T(8,128)(2,1)S(1)}, bf16[2,112,256]{2,1,0:T(8,128)(2,1)S(1)}, bf16[2,112,256]{2,1,0:T(8,128)(2,1)S(1)}) custom-call(s32[39]{0:T(128)S(1)} %fusion.2.refs_5_.places, bf16[2,448,4096]{2,1,0:T(8,128)(2,1)S(1)} %shard_map.76.refs_0_, ...), custom_call_target="tpu_custom_call" | custom-call | flops 469762048 | bytes 2359296 | tf_op jit(solution)/shard_map/pallas_call | solution.py:166
  37.6 2.8 %collective-permute-start.9 = (bf16[2,112,256]{2,1,0:T(8,128)(2,1)S(1)}, bf16[2,112,256]{2,1,0:T(8,128)(2,1)S(1)}, u32[]{:S(2)}, u32[]{:S(2)}) collective-permute-start(bf16[2,112,256]{2,1,0:T(8,128)(2,1)S(1)} %get-tuple-element.37), channel_id=1, source_target_pairs={{0,96},{1,97},{2,98},{3,99},{4,100},{5,101},{6,102},{7,103},{8,104... | collective-permute-start | bytes 344072 | tf_op jit(solution)/shard_map/ppermute | solution.py:36
  40.4 0.3 collective-permute-start.10
  40.7 0.7 collective-permute-start.8
  41.4 1.7 %shard_map.85 = (f32[2,112,256]{2,1,0:T(8,128)S(1)}, bf16[2,112,256]{2,1,0:T(8,128)(2,1)S(1)}, bf16[2,112,256]{2,1,0:T(8,128)(2,1)S(1)}, bf16[2,112,256]{2,1,0:T(8,128)(2,1)S(1)}) custom-call(s32[39]{0:T(128)S(1)} %fusion.2.refs_5_.places, bf16[2,448,4096]{2,1,0:T(8,128)(2,1)S(1)} %shard_map.76.refs_0_, ...), custom_call_target="tpu_custom_call" | custom-call | flops 939524096 | bytes 4718592 | tf_op jit(solution)/shard_map/pallas_call | solution.py:166
  43.1 1.7 %collective-permute-start.14 = (bf16[2,112,256]{2,1,0:T(8,128)(2,1)S(1)}, bf16[2,112,256]{2,1,0:T(8,128)(2,1)S(1)}, u32[]{:S(2)}, u32[]{:S(2)}) collective-permute-start(bf16[2,112,256]{2,1,0:T(8,128)(2,1)S(1)} %get-tuple-element.41), channel_id=1, source_target_pairs={{0,32},{1,33},{2,34},{3,35},{4,36},{5,37},{6,38},{7,39},{8,40},{9,... | collective-permute-start | bytes 344072 | tf_op jit(solution)/shard_map/ppermute | solution.py:36
  44.8 1.1 %collective-permute-start.15 = (bf16[2,112,256]{2,1,0:T(8,128)(2,1)S(1)}, bf16[2,112,256]{2,1,0:T(8,128)(2,1)S(1)}, u32[]{:S(2)}, u32[]{:S(2)}) collective-permute-start(bf16[2,112,256]{2,1,0:T(8,128)(2,1)S(1)} %get-tuple-element.42), channel_id=1, source_target_pairs={{0,96},{1,97},{2,98},{3,99},{4,100},{5,101},{6,102},{7,103},{8,104... | collective-permute-start | bytes 344072 | tf_op jit(solution)/shard_map/ppermute | solution.py:36
  46.0 0.9 %collective-permute-start.16 = (bf16[2,112,256]{2,1,0:T(8,128)(2,1)S(1)}, bf16[2,112,256]{2,1,0:T(8,128)(2,1)S(1)}, u32[]{:S(2)}, u32[]{:S(2)}) collective-permute-start(bf16[2,112,256]{2,1,0:T(8,128)(2,1)S(1)} %get-tuple-element.43), channel_id=1, source_target_pairs={{0,64},{1,65},{2,66},{3,67},{4,68},{5,69},{6,70},{7,71},{8,72},{9,... | collective-permute-start | bytes 344072 | tf_op jit(solution)/shard_map/ppermute | solution.py:36
  46.9 4.1 %collective-permute-start.22 = (bf16[4,256,512]{2,1,0:T(8,128)(2,1)S(1)}, bf16[4,256,512]{2,1,0:T(8,128)(2,1)S(1)}, u32[]{:S(2)}, u32[]{:S(2)}) collective-permute-start(bf16[4,256,512]{2,1,0:T(8,128)(2,1)S(1)} %shard_map.88), channel_id=1, source_target_pairs={{0,16},{1,17},{2,18},{3,19},{4,20},{5,21},{6,22},{7,23},{8,24},{9,... | collective-permute-start | bytes 3145736 | tf_op jit(solution)/shard_map/ppermute | solution.py:36
  51.0 3.2 %collective-permute-start.11 = (bf16[112,256]{1,0:T(8,128)(2,1)S(1)}, bf16[112,256]{1,0:T(8,128)(2,1)S(1)}, u32[]{:S(2)}, u32[]{:S(2)}) collective-permute-start(bf16[112,256]{1,0:T(8,128)(2,1)S(1)} %fusion), channel_id=1, source_target_pairs={{0,128},{1,129},{2,130},{3,131},{4,132},{5,133},{6,134},{7,135},{8... | collective-permute-start | bytes 172040 | tf_op jit(solution)/shard_map/ppermute | solution.py:36
  54.3 4.6 %collective-permute-start.17 = (bf16[112,256]{1,0:T(8,128)(2,1)S(1)}, bf16[112,256]{1,0:T(8,128)(2,1)S(1)}, u32[]{:S(2)}, u32[]{:S(2)}) collective-permute-start(bf16[112,256]{1,0:T(8,128)(2,1)S(1)} %fusion.1), channel_id=1, source_target_pairs={{0,128},{1,129},{2,130},{3,131},{4,132},{5,133},{6,134},{7,135},{8... | collective-permute-start | bytes 172040 | tf_op jit(solution)/shard_map/ppermute | solution.py:36
  59.0 2.8 %collective-permute-done.17 = bf16[112,256]{1,0:T(8,128)(2,1)S(1)} collective-permute-done((bf16[112,256]{1,0:T(8,128)(2,1)S(1)}, bf16[112,256]{1,0:T(8,128)(2,1)S(1)}, u32[]{:S(2)}, u32[]{:S(2)}) %collective-permute-start.17) | collective-permute-done | bytes 57376 | tf_op jit(solution)/shard_map/ppermute | solution.py:36
  61.8 0.6 shard_map.86
  62.4 3.6 %collective-permute-start.18 = (f32[56,512]{1,0:T(8,128)S(1)}, f32[56,512]{1,0:T(8,128)S(1)}, u32[]{:S(2)}, u32[]{:S(2)}) collective-permute-start(f32[56,512]{1,0:T(8,128)S(1)} %get-tuple-element.45), channel_id=1, source_target_pairs={{0,16},{1,17},{2,18},{3,19},{4,20},{5,21},{6,22},{7,23},{8,24},{9,... | collective-permute-start | bytes 344072 | tf_op jit(solution)/shard_map/ppermute | solution.py:36
  66.0 1.0 %collective-permute-done.18.other = f32[56,512]{1,0:T(8,128)S(1)} collective-permute-done((f32[56,512]{1,0:T(8,128)S(1)}, f32[56,512]{1,0:T(8,128)S(1)}, u32[]{:S(2)}, u32[]{:S(2)}) %collective-permute-start.18) | collective-permute-done | bytes 114720 | tf_op jit(solution)/shard_map/ppermute | solution.py:36
  67.0 0.7 shard_map.87.after
  67.7 2.2 %collective-permute-start.21 = (bf16[56,1024]{1,0:T(8,128)(2,1)S(1)}, bf16[56,1024]{1,0:T(8,128)(2,1)S(1)}, u32[]{:S(2)}, u32[]{:S(2)}) collective-permute-start(bf16[56,1024]{1,0:T(8,128)(2,1)S(1)} %shard_map.87.after), channel_id=1, source_target_pairs={{0,2},{1,3},{2,0},{3,1},{4,6},{5,7},{6,4},{7,5},{8,10},{9,11},{10,... | collective-permute-start | bytes 344072 | tf_op jit(solution)/shard_map/ppermute | solution.py:36
  69.9 0.5 collective-permute-start.20
  70.4 2.1 %collective-permute-start.19 = (bf16[56,1024]{1,0:T(8,128)(2,1)S(1)}, bf16[56,1024]{1,0:T(8,128)(2,1)S(1)}, u32[]{:S(2)}, u32[]{:S(2)}) collective-permute-start(bf16[56,1024]{1,0:T(8,128)(2,1)S(1)} %shard_map.87.after), channel_id=1, source_target_pairs={{0,3},{1,0},{2,1},{3,2},{4,7},{5,4},{6,5},{7,6},{8,11},{9,8},{10,9... | collective-permute-start | bytes 344072 | tf_op jit(solution)/shard_map/ppermute | solution.py:36
  72.6 0.4 collective-permute-done.21
  72.9 1.8 %collective-permute-done.20 = bf16[56,1024]{1,0:T(8,128)(2,1)S(1)} collective-permute-done((bf16[56,1024]{1,0:T(8,128)(2,1)S(1)}, bf16[56,1024]{1,0:T(8,128)(2,1)S(1)}, u32[]{:S(2)}, u32[]{:S(2)}) %collective-permute-start.20) | collective-permute-done | bytes 114720 | tf_op jit(solution)/shard_map/ppermute | solution.py:36
  74.8 0.6 shard_map.90
  75.5 0.1 collective-permute-start.23
  75.5 3.3 %collective-permute-start.24 = (bf16[224,256]{1,0:T(8,128)(2,1)S(1)}, bf16[224,256]{1,0:T(8,128)(2,1)S(1)}, u32[]{:S(2)}, u32[]{:S(2)}) collective-permute-start(bf16[224,256]{1,0:T(8,128)(2,1)S(1)} %get-tuple-element.47), channel_id=1, source_target_pairs={{0,12},{1,13},{2,14},{3,15},{4,0},{5,1},{6,2},{7,3},{8,4},{9,5},{1... | collective-permute-start | bytes 344072 | tf_op jit(solution)/shard_map/ppermute | solution.py:36
  78.8 1.4 %shard_map.92 = (f32[1,56,1024]{2,1,0:T(8,128)}, f32[1,56,1024]{2,1,0:T(8,128)}) custom-call(s32[39]{0:T(128)S(1)} %fusion.2.refs_5_.places, f32[56,512]{1,0:T(8,128)S(1)} %get-tuple-element.44.mine, f32[56,512]{1,0:T(8,128)S(1)} %collective-permute-done.18.other, f32[1,56,1024]{2,1,0:T(8,128)S(1)} %copy-done.1, f32[1,56,1024]{2,1,0:T(8,128)S(1)} %copy-done.2, ...), custom_call_target="tpu_custom_call" | custom-call | tf_op jit(solution)/shard_map/pallas_call | solution.py:363
  80.2 0.3 shard_map.89
  80.5 0.5 collective-permute-done.23
  81.0 3.6 %collective-permute-done.25 = bf16[224,256]{1,0:T(8,128)(2,1)S(1)} collective-permute-done((bf16[224,256]{1,0:T(8,128)(2,1)S(1)}, bf16[224,256]{1,0:T(8,128)(2,1)S(1)}, u32[]{:S(2)}, u32[]{:S(2)}) %collective-permute-start.25) | collective-permute-done | bytes 114720 | tf_op jit(solution)/shard_map/ppermute | solution.py:36
  84.6 1.3 %shard_map.91 = bf16[16,56,256]{2,1,0:T(8,128)(2,1)} custom-call(s32[39]{0:T(128)S(1)} %fusion.2.refs_5_.places, bf16[4,56,256]{2,1,0:T(8,128)(2,1)S(1)} %bitcast.30, bf16[4,56,256]{2,1,0:T(8,128)(2,1)S(1)} %bitcast.31, bf16[4,56,256]{2,1,0:T(8,128)(2,1)S(1)} %bitcast.32, bf16[4,56,256]{2,1,0:T(8,128)(2,1)S(1)} %bitcast.33), custom_call_target="tpu_custom_call" | custom-call | tf_op jit(solution)/shard_map/pallas_call | solution.py:418
  (39 shorter events, 0.4 us)
Async XLA Ops:
  0.6 15.2 %collective-permute-start = (bf16[2,448,4096]{2,1,0:T(8,128)(2,1)}, bf16[2,448,4096]{2,1,0:T(8,128)(2,1)}, u32[]{:S(2)}, u32[]{:S(2)}) collective-permute-start(bf16[2,448,4096]{2,1,0:T(8,128)(2,1)} %bitcast.25), channel_id=1, source_target_pairs={{0,16},{1,17},{2,18},{3,19},{4,20},{5,21},{6,22},{7,23},{8,24},{9,... | collective-permute-start | bytes 22020104 | tf_op jit(solution)/shard_map/ppermute | solution.py:36
  5.0 7.9 %collective-permute-start.3 = (bf16[2,256,256]{2,1,0:T(8,128)(2,1)S(1)}, bf16[2,256,256]{2,1,0:T(8,128)(2,1)S(1)}, u32[]{:S(2)}, u32[]{:S(2)}) collective-permute-start(bf16[2,256,256]{2,1,0:T(8,128)(2,1)S(1)} %pad_maximum_fusion.1.refs_0_), channel_id=1, source_target_pairs={{0,8},{1,9},{2,10},{3,11},{4,12},{5,13},{6,14},{7,15},{8,0},{9,1},... | collective-permute-start | bytes 786440 | tf_op jit(solution)/shard_map/ppermute | solution.py:36
  9.3 6.4 %collective-permute-start.2 = (bf16[2,256,256]{2,1,0:T(8,128)(2,1)S(1)}, bf16[2,256,256]{2,1,0:T(8,128)(2,1)S(1)}, u32[]{:S(2)}, u32[]{:S(2)}) collective-permute-start(bf16[2,256,256]{2,1,0:T(8,128)(2,1)S(1)} %pad_maximum_fusion.1.refs_0_), channel_id=1, source_target_pairs={{0,4},{1,5},{2,6},{3,7},{4,8},{5,9},{6,10},{7,11},{8,12},{9,13},{1... | collective-permute-start | bytes 786440 | tf_op jit(solution)/shard_map/ppermute | solution.py:36
  9.3 6.4 %collective-permute-start.1 = (bf16[2,256,256]{2,1,0:T(8,128)(2,1)S(1)}, bf16[2,256,256]{2,1,0:T(8,128)(2,1)S(1)}, u32[]{:S(2)}, u32[]{:S(2)}) collective-permute-start(bf16[2,256,256]{2,1,0:T(8,128)(2,1)S(1)} %pad_maximum_fusion.1.refs_0_), channel_id=1, source_target_pairs={{0,12},{1,13},{2,14},{3,15},{4,0},{5,1},{6,2},{7,3},{8,4},{9,5},{1... | collective-permute-start | bytes 786440 | tf_op jit(solution)/shard_map/ppermute | solution.py:36
  12.0 7.1 %copy-start = (bf16[1,16,56,4096]{3,2,1,0:T(8,128)(2,1)S(1)}, bf16[1,16,56,4096]{3,2,1,0:T(8,128)(2,1)}, u32[]{:S(2)}) copy-start(bf16[1,16,56,4096]{3,2,1,0:T(8,128)(2,1)} %param.5) | copy-start | bytes 22020100
  16.4 8.7 %collective-permute-start.4 = (bf16[4,256,256]{2,1,0:T(8,128)(2,1)S(1)}, bf16[4,256,256]{2,1,0:T(8,128)(2,1)S(1)}, u32[]{:S(2)}, u32[]{:S(2)}) collective-permute-start(bf16[4,256,256]{2,1,0:T(8,128)(2,1)S(1)} %get-tuple-element.27.refs_1_.refs_0_), channel_id=1, source_target_pairs={{0,131},{1,0},{2,1},{3,2},{4,135},{5,4},{6,5},{7,6},{8,139},{9,8},... | collective-permute-start | bytes 1572872 | tf_op jit(solution)/shard_map/ppermute | solution.py:36
  19.0 11.0 %collective-permute-start.7 = (bf16[4,256,256]{2,1,0:T(8,128)(2,1)S(1)}, bf16[4,256,256]{2,1,0:T(8,128)(2,1)S(1)}, u32[]{:S(2)}, u32[]{:S(2)}) collective-permute-start(bf16[4,256,256]{2,1,0:T(8,128)(2,1)S(1)} %get-tuple-element.31.refs_1_.refs_4_), channel_id=1, source_target_pairs={{0,1},{1,2},{2,3},{3,128},{4,5},{5,6},{6,7},{7,132},{8,9},{9,10},{... | collective-permute-start | bytes 1572872 | tf_op jit(solution)/shard_map/ppermute | solution.py:36
  19.0 15.2 %collective-permute-start.6 = (bf16[4,256,256]{2,1,0:T(8,128)(2,1)S(1)}, bf16[4,256,256]{2,1,0:T(8,128)(2,1)S(1)}, u32[]{:S(2)}, u32[]{:S(2)}) collective-permute-start(bf16[4,256,256]{2,1,0:T(8,128)(2,1)S(1)} %get-tuple-element.27.refs_1_.refs_0_), channel_id=1, source_target_pairs={{0,1},{1,2},{2,3},{3,128},{4,5},{5,6},{6,7},{7,132},{8,9},{9,10},{... | collective-permute-start | bytes 1572872 | tf_op jit(solution)/shard_map/ppermute | solution.py:36
  25.1 11.2 %collective-permute-start.5 = (bf16[4,256,256]{2,1,0:T(8,128)(2,1)S(1)}, bf16[4,256,256]{2,1,0:T(8,128)(2,1)S(1)}, u32[]{:S(2)}, u32[]{:S(2)}) collective-permute-start(bf16[4,256,256]{2,1,0:T(8,128)(2,1)S(1)} %shard_map.79.refs_1_), channel_id=1, source_target_pairs={{0,131},{1,0},{2,1},{3,2},{4,135},{5,4},{6,5},{7,6},{8,139},{9,8},... | collective-permute-start | bytes 1572872 | tf_op jit(solution)/shard_map/ppermute | solution.py:36
  28.5 12.9 %collective-permute-start.12 = (bf16[4,256,256]{2,1,0:T(8,128)(2,1)S(1)}, bf16[4,256,256]{2,1,0:T(8,128)(2,1)S(1)}, u32[]{:S(2)}, u32[]{:S(2)}) collective-permute-start(bf16[4,256,256]{2,1,0:T(8,128)(2,1)S(1)} %get-tuple-element.31.refs_1_.refs_4_), channel_id=1, source_target_pairs={{0,131},{1,0},{2,1},{3,2},{4,135},{5,4},{6,5},{7,6},{8,139},{9,8},... | collective-permute-start | bytes 1572872 | tf_op jit(solution)/shard_map/ppermute | solution.py:36
  30.0 11.4 %collective-permute-start.13 = (bf16[4,256,256]{2,1,0:T(8,128)(2,1)S(1)}, bf16[4,256,256]{2,1,0:T(8,128)(2,1)S(1)}, u32[]{:S(2)}, u32[]{:S(2)}) collective-permute-start(bf16[4,256,256]{2,1,0:T(8,128)(2,1)S(1)} %shard_map.82.refs_1_.refs_6_), channel_id=1, source_target_pairs={{0,1},{1,2},{2,3},{3,128},{4,5},{5,6},{6,7},{7,132},{8,9},{9,10},{... | collective-permute-start | bytes 1572872 | tf_op jit(solution)/shard_map/ppermute | solution.py:36
  37.6 8.4 %collective-permute-start.9 = (bf16[2,112,256]{2,1,0:T(8,128)(2,1)S(1)}, bf16[2,112,256]{2,1,0:T(8,128)(2,1)S(1)}, u32[]{:S(2)}, u32[]{:S(2)}) collective-permute-start(bf16[2,112,256]{2,1,0:T(8,128)(2,1)S(1)} %get-tuple-element.37), channel_id=1, source_target_pairs={{0,96},{1,97},{2,98},{3,99},{4,100},{5,101},{6,102},{7,103},{8,104... | collective-permute-start | bytes 344072 | tf_op jit(solution)/shard_map/ppermute | solution.py:36
  40.4 6.5 %collective-permute-start.10 = (bf16[2,112,256]{2,1,0:T(8,128)(2,1)S(1)}, bf16[2,112,256]{2,1,0:T(8,128)(2,1)S(1)}, u32[]{:S(2)}, u32[]{:S(2)}) collective-permute-start(bf16[2,112,256]{2,1,0:T(8,128)(2,1)S(1)} %get-tuple-element.38), channel_id=1, source_target_pairs={{0,64},{1,65},{2,66},{3,67},{4,68},{5,69},{6,70},{7,71},{8,72},{9,... | collective-permute-start | bytes 344072 | tf_op jit(solution)/shard_map/ppermute | solution.py:36
  40.7 10.2 %collective-permute-start.8 = (bf16[2,112,256]{2,1,0:T(8,128)(2,1)S(1)}, bf16[2,112,256]{2,1,0:T(8,128)(2,1)S(1)}, u32[]{:S(2)}, u32[]{:S(2)}) collective-permute-start(bf16[2,112,256]{2,1,0:T(8,128)(2,1)S(1)} %get-tuple-element.36.refs_4_), channel_id=1, source_target_pairs={{0,32},{1,33},{2,34},{3,35},{4,36},{5,37},{6,38},{7,39},{8,40},{9,... | collective-permute-start | bytes 344072 | tf_op jit(solution)/shard_map/ppermute | solution.py:36
  41.4 25.5 %copy-start.1 = (f32[1,56,1024]{2,1,0:T(8,128)S(1)}, f32[1,56,1024]{2,1,0:T(8,128)}, u32[]{:S(2)}) copy-start(f32[1,56,1024]{2,1,0:T(8,128)} %first.3) | copy-start | bytes 688132
  41.4 25.5 %copy-start.2 = (f32[1,56,1024]{2,1,0:T(8,128)S(1)}, f32[1,56,1024]{2,1,0:T(8,128)}, u32[]{:S(2)}) copy-start(f32[1,56,1024]{2,1,0:T(8,128)} %second.3) | copy-start | bytes 688132
  43.1 11.1 %collective-permute-start.14 = (bf16[2,112,256]{2,1,0:T(8,128)(2,1)S(1)}, bf16[2,112,256]{2,1,0:T(8,128)(2,1)S(1)}, u32[]{:S(2)}, u32[]{:S(2)}) collective-permute-start(bf16[2,112,256]{2,1,0:T(8,128)(2,1)S(1)} %get-tuple-element.41), channel_id=1, source_target_pairs={{0,32},{1,33},{2,34},{3,35},{4,36},{5,37},{6,38},{7,39},{8,40},{9,... | collective-permute-start | bytes 344072 | tf_op jit(solution)/shard_map/ppermute | solution.py:36
  44.8 9.4 %collective-permute-start.15 = (bf16[2,112,256]{2,1,0:T(8,128)(2,1)S(1)}, bf16[2,112,256]{2,1,0:T(8,128)(2,1)S(1)}, u32[]{:S(2)}, u32[]{:S(2)}) collective-permute-start(bf16[2,112,256]{2,1,0:T(8,128)(2,1)S(1)} %get-tuple-element.42), channel_id=1, source_target_pairs={{0,96},{1,97},{2,98},{3,99},{4,100},{5,101},{6,102},{7,103},{8,104... | collective-permute-start | bytes 344072 | tf_op jit(solution)/shard_map/ppermute | solution.py:36
  46.0 8.3 %collective-permute-start.16 = (bf16[2,112,256]{2,1,0:T(8,128)(2,1)S(1)}, bf16[2,112,256]{2,1,0:T(8,128)(2,1)S(1)}, u32[]{:S(2)}, u32[]{:S(2)}) collective-permute-start(bf16[2,112,256]{2,1,0:T(8,128)(2,1)S(1)} %get-tuple-element.43), channel_id=1, source_target_pairs={{0,64},{1,65},{2,66},{3,67},{4,68},{5,69},{6,70},{7,71},{8,72},{9,... | collective-permute-start | bytes 344072 | tf_op jit(solution)/shard_map/ppermute | solution.py:36
  46.9 27.9 %collective-permute-start.22 = (bf16[4,256,512]{2,1,0:T(8,128)(2,1)S(1)}, bf16[4,256,512]{2,1,0:T(8,128)(2,1)S(1)}, u32[]{:S(2)}, u32[]{:S(2)}) collective-permute-start(bf16[4,256,512]{2,1,0:T(8,128)(2,1)S(1)} %shard_map.88), channel_id=1, source_target_pairs={{0,16},{1,17},{2,18},{3,19},{4,20},{5,21},{6,22},{7,23},{8,24},{9,... | collective-permute-start | bytes 3145736 | tf_op jit(solution)/shard_map/ppermute | solution.py:36
  51.0 7.9 %collective-permute-start.11 = (bf16[112,256]{1,0:T(8,128)(2,1)S(1)}, bf16[112,256]{1,0:T(8,128)(2,1)S(1)}, u32[]{:S(2)}, u32[]{:S(2)}) collective-permute-start(bf16[112,256]{1,0:T(8,128)(2,1)S(1)} %fusion), channel_id=1, source_target_pairs={{0,128},{1,129},{2,130},{3,131},{4,132},{5,133},{6,134},{7,135},{8... | collective-permute-start | bytes 172040 | tf_op jit(solution)/shard_map/ppermute | solution.py:36
  54.3 7.5 %collective-permute-start.17 = (bf16[112,256]{1,0:T(8,128)(2,1)S(1)}, bf16[112,256]{1,0:T(8,128)(2,1)S(1)}, u32[]{:S(2)}, u32[]{:S(2)}) collective-permute-start(bf16[112,256]{1,0:T(8,128)(2,1)S(1)} %fusion.1), channel_id=1, source_target_pairs={{0,128},{1,129},{2,130},{3,131},{4,132},{5,133},{6,134},{7,135},{8... | collective-permute-start | bytes 172040 | tf_op jit(solution)/shard_map/ppermute | solution.py:36
  62.4 4.5 %collective-permute-start.18 = (f32[56,512]{1,0:T(8,128)S(1)}, f32[56,512]{1,0:T(8,128)S(1)}, u32[]{:S(2)}, u32[]{:S(2)}) collective-permute-start(f32[56,512]{1,0:T(8,128)S(1)} %get-tuple-element.45), channel_id=1, source_target_pairs={{0,16},{1,17},{2,18},{3,19},{4,20},{5,21},{6,22},{7,23},{8,24},{9,... | collective-permute-start | bytes 344072 | tf_op jit(solution)/shard_map/ppermute | solution.py:36
  67.7 5.2 %collective-permute-start.21 = (bf16[56,1024]{1,0:T(8,128)(2,1)S(1)}, bf16[56,1024]{1,0:T(8,128)(2,1)S(1)}, u32[]{:S(2)}, u32[]{:S(2)}) collective-permute-start(bf16[56,1024]{1,0:T(8,128)(2,1)S(1)} %shard_map.87.after), channel_id=1, source_target_pairs={{0,2},{1,3},{2,0},{3,1},{4,6},{5,7},{6,4},{7,5},{8,10},{9,11},{10,... | collective-permute-start | bytes 344072 | tf_op jit(solution)/shard_map/ppermute | solution.py:36
  69.9 4.9 %collective-permute-start.20 = (bf16[56,1024]{1,0:T(8,128)(2,1)S(1)}, bf16[56,1024]{1,0:T(8,128)(2,1)S(1)}, u32[]{:S(2)}, u32[]{:S(2)}) collective-permute-start(bf16[56,1024]{1,0:T(8,128)(2,1)S(1)} %shard_map.87.after), channel_id=1, source_target_pairs={{0,1},{1,2},{2,3},{3,0},{4,5},{5,6},{6,7},{7,4},{8,9},{9,10},{10,1... | collective-permute-start | bytes 344072 | tf_op jit(solution)/shard_map/ppermute | solution.py:36
  70.4 4.3 %collective-permute-start.19 = (bf16[56,1024]{1,0:T(8,128)(2,1)S(1)}, bf16[56,1024]{1,0:T(8,128)(2,1)S(1)}, u32[]{:S(2)}, u32[]{:S(2)}) collective-permute-start(bf16[56,1024]{1,0:T(8,128)(2,1)S(1)} %shard_map.87.after), channel_id=1, source_target_pairs={{0,3},{1,0},{2,1},{3,2},{4,7},{5,4},{6,5},{7,6},{8,11},{9,8},{10,9... | collective-permute-start | bytes 344072 | tf_op jit(solution)/shard_map/ppermute | solution.py:36
  75.5 5.5 %collective-permute-start.23 = (bf16[224,256]{1,0:T(8,128)(2,1)S(1)}, bf16[224,256]{1,0:T(8,128)(2,1)S(1)}, u32[]{:S(2)}, u32[]{:S(2)}) collective-permute-start(bf16[224,256]{1,0:T(8,128)(2,1)S(1)} %get-tuple-element.46), channel_id=1, source_target_pairs={{0,4},{1,5},{2,6},{3,7},{4,8},{5,9},{6,10},{7,11},{8,12},{9,13},{1... | collective-permute-start | bytes 344072 | tf_op jit(solution)/shard_map/ppermute | solution.py:36
  75.5 5.4 %collective-permute-start.24 = (bf16[224,256]{1,0:T(8,128)(2,1)S(1)}, bf16[224,256]{1,0:T(8,128)(2,1)S(1)}, u32[]{:S(2)}, u32[]{:S(2)}) collective-permute-start(bf16[224,256]{1,0:T(8,128)(2,1)S(1)} %get-tuple-element.47), channel_id=1, source_target_pairs={{0,12},{1,13},{2,14},{3,15},{4,0},{5,1},{6,2},{7,3},{8,4},{9,5},{1... | collective-permute-start | bytes 344072 | tf_op jit(solution)/shard_map/ppermute | solution.py:36
  78.8 5.8 %collective-permute-start.25 = (bf16[224,256]{1,0:T(8,128)(2,1)S(1)}, bf16[224,256]{1,0:T(8,128)(2,1)S(1)}, u32[]{:S(2)}, u32[]{:S(2)}) collective-permute-start(bf16[224,256]{1,0:T(8,128)(2,1)S(1)} %get-tuple-element.48), channel_id=1, source_target_pairs={{0,8},{1,9},{2,10},{3,11},{4,12},{5,13},{6,14},{7,15},{8,0},{9,1},... | collective-permute-start | bytes 344072 | tf_op jit(solution)/shard_map/ppermute | solution.py:36
